TPU v7x, 32 devices: a whole 2x2x4 slice. The times are simulated.
32 devices in a mesh: dp: 4 (over z), seq: 2 (over y), tensor: 4 (over x, core).
Axes of the slice: x: 2, y: 2, z: 4, core: 2. Of those that a mesh axis runs over, the one named last changes fastest.
Arguments:
- block_input: float32 [8192, 768], P(('dp', 'seq', 'tensor')), may hold values from -6 to 6
- attn_in_weight: bfloat16 [3, 768, 768], P(None, ('dp', 'seq'), 'tensor'), may hold values from -0.21875 to 0.21875
- attn_out_weight: bfloat16 [768, 768], P('tensor', ('dp', 'seq')), may hold values from -3.5 to 3.5
- position_bias: float32 [32, 12], P(None, 'tensor'), may hold values from -6 to 6
- norm_gains: float32 [2, 768], replicated, may hold values from 0.1 to 1.9
- router_weight: bfloat16 [768, 8], replicated, may hold values from -0.15625 to 0.15625
- expert_in: bfloat16 [8, 768, 3072], P(('dp', 'seq'), None, 'tensor'), may hold values from -0.21875 to 0.21875
- expert_out: bfloat16 [8, 3072, 768], P(('dp', 'seq'), 'tensor'), may hold values from -10 to 10
- segment_ids: int32 [4, 2048], P('dp', ('seq', 'tensor')), may hold values from 0 to 2, as said below
- expert_ids: int32 [8192, 1], P(('dp', 'seq')), may hold values from 0 to 7; in each aligned block of 1024 rows (0 to 1023, 1024 to 2047, ...) at most 256 rows name the same one
- out_grad: float32 [8192, 768], P(('dp', 'seq', 'tensor')), may hold values from -6 to 6
Outputs:
- block_out: float32 [8192, 768], P(('dp', 'seq', 'tensor'))
- input_grad: float32 [8192, 768], P(('dp', 'seq', 'tensor'))
- grad_attn_in: float32 [3, 768, 768], P(None, ('dp', 'seq'), 'tensor')
- grad_attn_out: float32 [768, 768], P('tensor', ('dp', 'seq'))
- grad_bias: float32 [32, 12], P(None, 'tensor')
- grad_gains: float32 [2, 768], replicated
- grad_router: float32 [768, 8], replicated
- grad_expert_in: float32 [8, 768, 3072], P(('dp', 'seq'), None, 'tensor')
- grad_expert_out: float32 [8, 3072, 768], P(('dp', 'seq'), 'tensor')
Inputs may be any that keep to these rules, and one draw needn't show every extreme that they name: `segment_ids`: along a sequence the ids never fall; every sequence holds documents 0, 1 and 2, each one run of positions. In some sequence document 1 begins within the first 1024 positions and ends within the last 1024. `expert_ids`: in each aligned block of 1024 rows no expert is named by more than 256 rows.
All inputs are finite; a program needn't handle non-finite values.
Results may differ from a plain program's by a relative error of at most 0.035.
Values may be sent and summed in bfloat16 or wider, within the bound.
No kernel may reach another device: no remote copies, remote signals or barrier semaphores. Data moves between devices by JAX's collectives and lax.ppermute only.
A program may use at most 448 MiB of HBM per device.

v0:
```python
import functools
import math

import jax
import jax.numpy as jnp
from jax import lax
from jax.experimental import pallas as pl
from jax.experimental.pallas import tpu as pltpu
from jax.sharding import PartitionSpec as P

EPSILON = 1e-06
EDGES = (1, 2, 3, 4, 5, 6, 7, 8, 12, 16, 23, 32, 46, 64, 91)
TILE = 256
HALF = TILE // 2
LOG2E = math.log2(math.e)
SCALE = 0.125
MASKED = -1e30
LOWEST = -1e29
EXTRA = 16
VMEM_BYTES = 48 * 1024 * 1024
GELU_A = math.sqrt(2.0 / math.pi)
GELU_B = 0.044715
BF16 = jnp.bfloat16
F32 = jnp.float32


def dot(left_side, right_side):
    return jnp.dot(left_side, right_side, preferred_element_type=F32)


def dot_rows(left_side, right_side):
    return lax.dot_general(
        left_side, right_side, (((1,), (1,)), ((), ())), preferred_element_type=F32
    )


def einsum(formula, *operands):
    return jnp.einsum(formula, *operands, preferred_element_type=F32)


def swap(values, axis, bit):
    count = lax.axis_size(axis)
    return lax.ppermute(values, axis, [(i, i ^ bit) for i in range(count)])


def bits_of(count):
    return [1 << i for i in range(count.bit_length() - 1)]


def gather_relative(values, axis):
    pieces = {0: values}
    for bit in reversed(bits_of(lax.axis_size(axis))):
        for place in list(pieces):
            pieces[place ^ bit] = swap(pieces[place], axis, bit)
    return [pieces[place] for place in range(len(pieces))]


def core_step(kept, sent):
    got = swap(sent, "tensor", 1)
    to_send = (kept[1].astype(F32) + got[1].astype(F32)).astype(BF16)
    return kept[0], got[0], to_send


def chip_step(near, got, far):
    return near.astype(F32) + got.astype(F32) + far.astype(F32)


def sum_tensor(kept, sent):
    near, got, to_send = core_step(kept, sent)
    return chip_step(near, got, swap(to_send, "tensor", 2))


def reorder(pieces, own_index):
    for bit in bits_of(len(pieces)):
        flip = (own_index & bit) != 0
        pieces = [
            jnp.where(flip, pieces[place ^ bit], pieces[place]) for place in range(len(pieces))
        ]
    return pieces


def sum_all(values, axes):
    for axis in axes:
        for bit in bits_of(lax.axis_size(axis)):
            values = values + swap(values, axis, bit)
    return values


def bucket_of(relative, half_count):
    magnitude = jnp.abs(relative)
    counted = jnp.zeros(relative.shape, jnp.int32)
    for edge_value in EDGES:
        counted = counted + (magnitude >= edge_value).astype(jnp.int32)
    return counted + jnp.where(relative > 0, half_count, 0).astype(jnp.int32)


def near_buckets(half_count):
    shape = (3, HALF, HALF)
    relative = (
        (lax.broadcasted_iota(jnp.int32, shape, 0) - 1) * HALF
        + lax.broadcasted_iota(jnp.int32, shape, 1)
        - lax.broadcasted_iota(jnp.int32, shape, 2)
    )
    return bucket_of(relative, half_count)


def bias_tiles(position_bias):
    bucket_count, heads = position_bias.shape
    half_count = bucket_count // 2
    grid = near_buckets(half_count)
    near = jnp.zeros((heads, 3, HALF, HALF), F32)
    for bucket_index in range(bucket_count):
        near = near + jnp.where(
            (grid == bucket_index)[None], position_bias[bucket_index][:, None, None, None], 0.0
        )
    before, same, after = near[:, 0], near[:, 1], near[:, 2]
    far_before = jnp.broadcast_to(
        position_bias[half_count - 1][:, None, None], (heads, HALF, HALF)
    )
    far_after = jnp.broadcast_to(
        position_bias[bucket_count - 1][:, None, None], (heads, HALF, HALF)
    )

    def square(a, b, c, d):
        return jnp.concatenate(
            [jnp.concatenate([a, b], axis=2), jnp.concatenate([c, d], axis=2)], axis=1
        )

    tiles = jnp.stack(
        [
            square(far_before, far_before, far_before, far_before),
            square(far_before, far_before, before, far_before),
            square(same, before, after, same),
            square(far_after, after, far_after, far_after),
            square(far_after, far_after, far_after, far_after),
        ]
    )
    return tiles * LOG2E


def span_of(meta_ref, query_tile, key_tiles):
    opening, closing = meta_ref[1], meta_ref[2]
    first = query_tile * TILE
    last = first + TILE - 1
    begin = jnp.where(first < opening, 0, jnp.where(first < closing, opening, closing))
    end = jnp.where(last < opening, opening, jnp.where(last < closing, closing, key_tiles * TILE))
    return begin // TILE, (end + TILE - 1) // TILE


def document_row(meta_ref, tile):
    place = tile * TILE + lax.broadcasted_iota(jnp.int32, (EXTRA, TILE), 1)
    return (place >= meta_ref[1]).astype(jnp.int32) + (place >= meta_ref[2]).astype(jnp.int32)


def key_rows(meta_ref, tile):
    row = lax.broadcasted_iota(jnp.int32, (EXTRA, TILE), 0)
    differs = jnp.where(document_row(meta_ref, tile) != row, MASKED, 0.0)
    return jnp.where(row < 3, differs, jnp.where(row < 6, 1.0, 0.0)).astype(BF16)


def query_rows(meta_ref, tile, terms):
    row = lax.broadcasted_iota(jnp.int32, (EXTRA, TILE), 0)
    agrees = jnp.where(document_row(meta_ref, tile) == row, 1.0, 0.0)
    return jnp.where(row < 3, agrees, three_rows(row - 3, terms)).astype(BF16)


def three_rows(row, terms):
    result = jnp.zeros(row.shape, F32)
    for i, term in enumerate(terms):
        result = jnp.where(row == i, term, result)
    return result


def split_three(values):
    first = values.astype(BF16).astype(F32)
    second = (values - first).astype(BF16).astype(F32)
    return first, second, values - first - second


def attend_kernel(
    meta_ref,
    q_ref,
    kv_ref,
    bias_ref,
    weight_ref,
    exact_ref,
    out_ref,
    log_ref,
    even_ref,
    odd_ref,
    key_ref,
    query_ref,
    sum_ref,
):
    key_tiles = kv_ref.shape[0]
    heads = bias_ref.shape[1]
    size = q_ref.shape[1] // heads

    def turn(j, carry):
        kept = meta_ref[3 + j]
        extra = key_rows(meta_ref, j)
        for h in range(heads):
            rows = kv_ref[kept, h * size : (h + 1) * size, :]
            key_ref[kept, h] = jnp.concatenate([rows, extra], axis=0).T
        return carry

    lax.fori_loop(0, key_tiles, turn, 0)
    ones = jnp.ones((EXTRA, TILE), BF16)

    def query_body(i, carry):
        tile = meta_ref[3 + key_tiles + i]
        place = tile % meta_ref[0]
        begin, end = span_of(meta_ref, tile, key_tiles)
        extra = query_rows(meta_ref, tile, ())
        for h in range(heads):
            rows = q_ref[i, h * size : (h + 1) * size, :]
            query_ref[h] = jnp.concatenate([rows, extra], axis=0)
        sum_ref[...] = jnp.zeros_like(sum_ref)

        def key_body(j, peaks):
            kept = meta_ref[3 + j]
            kind = jnp.clip(j - tile, -2, 2) + 2
            scores = [
                dot(key_ref[kept, h], query_ref[h]) + bias_ref[kind, h] for h in range(heads)
            ]
            new_peaks = [
                jnp.maximum(peaks[h], jnp.max(scores[h], axis=0, keepdims=True))
                for h in range(heads)
            ]
            weights = [jnp.exp2(scores[h] - new_peaks[h]).astype(BF16) for h in range(heads)]
            added = []
            for h in range(heads):
                values = kv_ref[kept, (heads + h) * size : (heads + h + 1) * size, :]
                added.append(dot(jnp.concatenate([values, ones], axis=0), weights[h]))
            for h in range(heads):
                sum_ref[h] = sum_ref[h] * jnp.exp2(peaks[h] - new_peaks[h]) + added[h]
            return tuple(new_peaks)

        start = tuple(jnp.full((1, TILE), LOWEST, F32) for _ in range(heads))
        peaks = lax.fori_loop(begin, end, key_body, start)
        for h in range(heads):
            rows = slice(h * size, (h + 1) * size)
            total = sum_ref[h, size : size + 1, :]
            result = sum_ref[h, :size, :] * (1.0 / total)
            exact_ref[i, rows, :] = result
            out_ref[place, rows, :] = result.astype(BF16)
            log_ref[i, h] = peaks[h] + jnp.log2(total)
        attended = out_ref[place]
        for k in range(weight_ref.shape[0]):
            block = dot(weight_ref[k], attended).astype(BF16)
            (odd_ref if k & 1 else even_ref)[k // 2, place] = block
        return carry

    lax.fori_loop(0, q_ref.shape[0], query_body, 0)


def estimate(queries, key_tiles, products):
    pairs = queries.shape[0] * TILE * key_tiles * TILE
    return pl.CostEstimate(
        flops=2 * products * pairs * queries.shape[1],
        bytes_accessed=8 * pairs,
        transcendentals=3 * pairs,
    )


def whole_specs(arrays):
    return [pl.BlockSpec(array.shape, functools.partial(origin, len(array.shape))) for array in arrays]


def origin(dimensions, step):
    return (0,) * dimensions


def attend(meta, queries, keys_values, bias, out_blocks):
    query_tiles, width, _ = queries.shape
    key_tiles = keys_values.shape[0]
    heads = bias.shape[1]
    parts, share, _ = out_blocks.shape
    blocks = jax.ShapeDtypeStruct((parts // 2, query_tiles, share, TILE), BF16)
    shapes = (
        jax.ShapeDtypeStruct(queries.shape, F32),
        jax.ShapeDtypeStruct(queries.shape, BF16),
        jax.ShapeDtypeStruct((query_tiles, heads, 1, TILE), F32),
        blocks,
        blocks,
    )
    operands = (queries, keys_values, bias, out_blocks)
    return pl.pallas_call(
        attend_kernel,
        grid=(1,),
        out_shape=shapes,
        in_specs=[pl.BlockSpec(memory_space=pltpu.SMEM)] + whole_specs(operands),
        out_specs=tuple(whole_specs(shapes)),
        scratch_shapes=[
            pltpu.VMEM((key_tiles, heads, TILE, width // heads + EXTRA), BF16),
            pltpu.VMEM((heads, width // heads + EXTRA, TILE), BF16),
            pltpu.VMEM((heads, width // heads + EXTRA, TILE), F32),
        ],
        compiler_params=pltpu.CompilerParams(vmem_limit_bytes=VMEM_BYTES),
        cost_estimate=estimate(queries, key_tiles, 2),
        name="attend",
    )(meta, *operands)


def bucket_rows(tiles_ref, rows_ref):
    heads, bucket_count = rows_ref.shape[:2]
    half_count = bucket_count // 2
    offset = lax.broadcasted_iota(jnp.int32, (HALF, HALF), 0) - lax.broadcasted_iota(
        jnp.int32, (HALF, HALF), 1
    )
    grids = [bucket_of(offset + shift * HALF, half_count) for shift in (-1, 0, 1)]
    first, last = slice(0, HALF), slice(HALF, TILE)

    def column_sums(values):
        return jnp.sum(values, axis=0, keepdims=True)

    def head_body(h, carry):
        before = tiles_ref[2, h, first, last] + tiles_ref[1, h, last, first]
        same = tiles_ref[2, h, first, first] + tiles_ref[2, h, last, last]
        after = tiles_ref[2, h, last, first] + tiles_ref[3, h, first, last]
        far_before = column_sums(tiles_ref[0, h, :, first] + tiles_ref[0, h, :, last])
        far_before += column_sums(tiles_ref[1, h, first, first] + tiles_ref[1, h, first, last])
        far_before += column_sums(tiles_ref[1, h, last, last])
        far_after = column_sums(tiles_ref[4, h, :, first] + tiles_ref[4, h, :, last])
        far_after += column_sums(tiles_ref[3, h, last, first] + tiles_ref[3, h, last, last])
        far_after += column_sums(tiles_ref[3, h, first, first])
        for bucket_index in range(bucket_count):
            row = column_sums(jnp.where(grids[1] == bucket_index, same, 0.0))
            if 0 < bucket_index < half_count:
                row += column_sums(jnp.where(grids[0] == bucket_index, before, 0.0))
            if bucket_index > half_count:
                row += column_sums(jnp.where(grids[2] == bucket_index, after, 0.0))
            if bucket_index == half_count - 1:
                row += far_before
            if bucket_index == bucket_count - 1:
                row += far_after
            rows_ref[h, bucket_index : bucket_index + 1, :] = row
        return carry

    lax.fori_loop(0, heads, head_body, 0)


def attend_back_kernel(
    meta_ref,
    q_ref,
    kv_ref,
    bias_ref,
    weight_ref,
    exact_ref,
    log_ref,
    *refs,
):
    parts = weight_ref.shape[0]
    branch_refs = refs[:parts]
    (
        dq_ref,
        dkv_ref,
        rows_ref,
        tiles_ref,
        key_ref,
        value_ref,
        query_ref,
        grad_ref,
        dq_sum,
        dkv_sum,
    ) = refs[parts:]
    key_tiles = kv_ref.shape[0]
    heads = bias_ref.shape[1]
    size = q_ref.shape[1] // heads

    row = lax.broadcasted_iota(jnp.int32, (EXTRA, TILE), 0)
    ones = jnp.where(row < 3, 1.0, 0.0).astype(BF16)

    def turn(j, carry):
        kept = meta_ref[3 + j]
        extra = key_rows(meta_ref, j)
        for h in range(heads):
            rows = kv_ref[kept, h * size : (h + 1) * size, :]
            key_ref[kept, h] = jnp.concatenate([rows, extra], axis=0).T
            rows = kv_ref[kept, (heads + h) * size : (heads + h + 1) * size, :]
            value_ref[kept, h] = jnp.concatenate([rows, ones], axis=0).T
        return carry

    lax.fori_loop(0, key_tiles, turn, 0)
    dkv_sum[...] = jnp.zeros_like(dkv_sum)
    tiles_ref[...] = jnp.zeros_like(tiles_ref)

    def query_body(i, carry):
        tile = meta_ref[3 + key_tiles + i]
        place = tile % meta_ref[0]
        begin, end = span_of(meta_ref, tile, key_tiles)
        dq_sum[...] = jnp.zeros_like(dq_sum)
        grad_sum = dot(weight_ref[0], branch_refs[0][place])
        for k in range(1, parts):
            grad_sum += dot(weight_ref[k], branch_refs[k][place])
        for h in range(heads):
            rows = slice(h * size, (h + 1) * size)
            grad = grad_sum[rows].astype(BF16)
            centre = jnp.sum(grad.astype(F32) * exact_ref[i, rows, :], axis=0, keepdims=True)
            extra = three_rows(row, split_three(-centre)).astype(BF16)
            grad_ref[h] = jnp.concatenate([grad, extra], axis=0)
            extra = query_rows(meta_ref, tile, split_three(-log_ref[i, h]))
            query_ref[h] = jnp.concatenate([q_ref[i, rows, :], extra], axis=0)

        def key_body(j, inner):
            kept = meta_ref[3 + j]
            kind = jnp.clip(j - tile, -2, 2) + 2
            probs = [
                jnp.exp2(dot(key_ref[kept, h], query_ref[h]) + bias_ref[kind, h])
                for h in range(heads)
            ]
            score_grads = [probs[h] * dot(value_ref[kept, h], grad_ref[h]) for h in range(heads)]
            low_probs = [prob.astype(BF16) for prob in probs]
            low_grads = [score_grad.astype(BF16) for score_grad in score_grads]
            key_adds, value_adds, query_adds = [], [], []
            for h in range(heads):
                rows = slice(h * size, (h + 1) * size)
                key_adds.append(dot_rows(q_ref[i, rows, :], low_grads[h]))
                value_adds.append(dot_rows(grad_ref[h, :size, :], low_probs[h]))
                query_adds.append(dot(kv_ref[kept, rows, :], low_grads[h]))
            for h in range(heads):
                rows = slice(h * size, (h + 1) * size)
                value_rows = slice((heads + h) * size, (heads + h + 1) * size)
                tiles_ref[kind, h] += score_grads[h]
                dkv_sum[kept, rows, :] += key_adds[h]
                dkv_sum[kept, value_rows, :] += value_adds[h]
                dq_sum[rows, :] += query_adds[h]
            return inner

        lax.fori_loop(begin, end, key_body, 0)
        dq_ref[i] = (dq_sum[...] * SCALE).astype(BF16)
        return carry

    lax.fori_loop(0, q_ref.shape[0], query_body, 0)
    middle = heads * size
    dkv_ref[:, :middle, :] = (dkv_sum[:, :middle, :] * (1.0 / LOG2E)).astype(BF16)
    dkv_ref[:, middle:, :] = dkv_sum[:, middle:, :].astype(BF16)
    bucket_rows(tiles_ref, rows_ref)


def attend_back(meta, queries, keys_values, bias, out_blocks, exact, logs, branch, buckets):
    key_tiles = keys_values.shape[0]
    heads = bias.shape[1]
    size = queries.shape[1] // heads
    shapes = (
        jax.ShapeDtypeStruct(queries.shape, BF16),
        jax.ShapeDtypeStruct(keys_values.shape, BF16),
        jax.ShapeDtypeStruct((heads, buckets, HALF), F32),
    )
    operands = (queries, keys_values, bias, out_blocks, exact, logs, *branch)
    return pl.pallas_call(
        attend_back_kernel,
        grid=(1,),
        out_shape=shapes,
        in_specs=[pl.BlockSpec(memory_space=pltpu.SMEM)] + whole_specs(operands),
        out_specs=tuple(whole_specs(shapes)),
        scratch_shapes=[
            pltpu.VMEM(bias.shape, F32),
            pltpu.VMEM((key_tiles, heads, TILE, size + EXTRA), BF16),
            pltpu.VMEM((key_tiles, heads, TILE, size + EXTRA), BF16),
            pltpu.VMEM((heads, size + EXTRA, TILE), BF16),
            pltpu.VMEM((heads, size + EXTRA, TILE), BF16),
            pltpu.VMEM(queries.shape[1:], F32),
            pltpu.VMEM(keys_values.shape, F32),
        ],
        compiler_params=pltpu.CompilerParams(vmem_limit_bytes=VMEM_BYTES),
        cost_estimate=estimate(queries, key_tiles, 5),
        name="attend_back",
    )(meta, *operands)


def project_kernel(piece_count, weight_count, tiles, share, own_ref, *refs):
    piece_refs = refs[:piece_count]
    weight_refs = refs[piece_count : piece_count + weight_count]
    gain_ref = refs[piece_count + weight_count]
    (
        meta_ref,
        q_ref,
        kv_ref,
        normed_ref,
        input_ref,
        in_ref,
        out_ref,
        out_t_ref,
        block_ref,
        turned_ref,
    ) = refs[piece_count + weight_count + 1 :]
    grid_place, tensor_place, seq_place, own_first = (own_ref[i] for i in range(4))
    width = gain_ref.shape[0]
    head_cols = q_ref.shape[1]
    columns = turned_ref.shape[0]
    for k in range(weight_count):
        place = grid_place ^ k if weight_count > 1 else 0
        block_ref[place] = weight_refs[k][...]
    full = block_ref[...].reshape(width, columns)
    in_ref[...] = full[:, : 3 * head_cols]
    turned_ref[...] = full.T
    blocks_here = width // share
    tall = block_ref.shape[1]
    per = share // tall if weight_count > 1 else 1
    for k in range(blocks_here):
        if weight_count > 1:
            block = block_ref[pl.ds((tensor_place ^ k) * per, per), :, 3 * head_cols :]
            block = block.reshape(share, head_cols)
        else:
            start = pl.multiple_of((tensor_place ^ k) * share, share)
            block = block_ref[0, pl.ds(start, share), 3 * head_cols :]
        out_ref[k] = block
        out_t_ref[k] = block.T
    key_tiles = kv_ref.shape[0]
    early = jnp.zeros((1, TILE), F32)
    late = jnp.zeros((1, TILE), F32)
    gain = gain_ref[...]
    for k in range(piece_count):
        for s in range(piece_refs[0].shape[0]):
            kept = s + k
            rows = piece_refs[k][s, :width, :].astype(F32)
            ids = piece_refs[k][s, width : width + 16, :][:1].astype(F32)
            early += (ids < 0.5).astype(F32)
            late += (ids < 1.5).astype(F32)
            root = lax.rsqrt(jnp.sum(rows * rows, axis=0, keepdims=True) * (1.0 / width) + EPSILON)
            normed = (rows * root * gain).astype(BF16)
            normed_ref[kept] = normed
            kv_ref[kept] = dot(turned_ref[head_cols : 3 * head_cols, :], normed).astype(BF16)
    for i in range(tiles):
        normed = normed_ref[own_first + i]
        q_ref[i] = (dot(turned_ref[:head_cols, :], normed) * (SCALE * LOG2E)).astype(BF16)
        start = pl.multiple_of(tensor_place * share, share)
        if piece_count > 1:
            input_ref[tensor_place ^ i] = piece_refs[i][0, pl.ds(start, share), :]
        else:
            input_ref[i] = piece_refs[0][own_first + i, pl.ds(start, share), :]
    meta_ref[0] = tiles
    meta_ref[1] = jnp.sum(early).astype(jnp.int32)
    meta_ref[2] = jnp.sum(late).astype(jnp.int32)
    for j in range(key_tiles):
        if piece_count > 1:
            meta_ref[3 + j] = ((j // tiles) ^ seq_place) * tiles + ((j % tiles) ^ tensor_place)
        else:
            meta_ref[3 + j] = j
    for i in range(tiles):
        shift = tensor_place ^ i if piece_count > 1 else i
        meta_ref[3 + key_tiles + i] = seq_place * tiles + shift


def project(own, pieces, weight_pieces, gain, tiles, key_tiles, share):
    width = gain.shape[0]
    columns = weight_pieces[0].shape[1]
    head_cols = columns // 4
    parts = width // share
    shapes = (
        jax.ShapeDtypeStruct((tiles, head_cols, TILE), BF16),
        jax.ShapeDtypeStruct((key_tiles, 2 * head_cols, TILE), BF16),
        jax.ShapeDtypeStruct((key_tiles, width, TILE), BF16),
        jax.ShapeDtypeStruct((tiles, share, TILE), BF16),
        jax.ShapeDtypeStruct((width, 3 * head_cols), BF16),
        jax.ShapeDtypeStruct((parts, share, head_cols), BF16),
        jax.ShapeDtypeStruct((parts, head_cols, share), BF16),
    )
    operands = (*pieces, *weight_pieces, gain)
    return pl.pallas_call(
        functools.partial(project_kernel, len(pieces), len(weight_pieces), tiles, share),
        grid=(1,),
        out_shape=(jax.ShapeDtypeStruct((3 + key_tiles + tiles,), jnp.int32),) + shapes,
        in_specs=[pl.BlockSpec(memory_space=pltpu.SMEM)] + whole_specs(operands),
        out_specs=(pl.BlockSpec(memory_space=pltpu.SMEM),) + tuple(whole_specs(shapes)),
        scratch_shapes=[
            pltpu.VMEM((len(weight_pieces),) + weight_pieces[0].shape, BF16),
            pltpu.VMEM((columns, width), BF16),
        ],
        compiler_params=pltpu.CompilerParams(vmem_limit_bytes=VMEM_BYTES),
        cost_estimate=pl.CostEstimate(
            flops=6 * key_tiles * TILE * width * head_cols,
            bytes_accessed=8 * key_tiles * TILE * width,
            transcendentals=0,
        ),
        name="project",
    )(own, *operands)


def project_back_kernel(fast, parts, own_ref, dq_ref, dkv_ref, normed_ref, in_ref, attended_ref, *refs):
    branch_refs = refs[:parts]
    if fast:
        far_even, far_odd, own_even, own_odd, weight_even, weight_odd, gain_ref, full_ref = refs[
            parts:
        ]
    else:
        part_ref, weight_ref, gain_ref, full_ref = refs[parts:]
    grid_place, tensor_place, seq_place, own_first = (own_ref[i] for i in range(4))
    tiles, head_cols, _ = dq_ref.shape
    key_tiles = dkv_ref.shape[0]
    width = in_ref.shape[0]
    share = width // parts
    key_weight = in_ref[:, head_cols:]
    query_weight = in_ref[:, :head_cols]
    if fast:
        for n in range(tiles):
            block = dot(key_weight, dkv_ref[tiles + n]).astype(BF16)
            (far_odd if n & 1 else far_even)[n // 2] = block
        for n in range(tiles):
            block = dot(key_weight, dkv_ref[n]) + dot(query_weight, dq_ref[n])
            (own_odd if n & 1 else own_even)[n // 2] = block.astype(BF16)
    else:
        for n in range(key_tiles):
            part_ref[n] = dot(key_weight, dkv_ref[n]).astype(BF16)
        for n in range(tiles):
            block = part_ref[own_first + n].astype(F32) + dot(query_weight, dq_ref[n])
            part_ref[own_first + n] = block.astype(BF16)
    query_sum = dot_rows(normed_ref[own_first], dq_ref[0])
    for n in range(1, tiles):
        query_sum += dot_rows(normed_ref[own_first + n], dq_ref[n])
    key_sum = dot_rows(normed_ref[0], dkv_ref[0])
    for n in range(1, key_tiles):
        key_sum += dot_rows(normed_ref[n], dkv_ref[n])
    gain_ref[...] = jnp.sum(
        query_sum * query_weight.astype(F32), axis=1, keepdims=True
    ) + jnp.sum(key_sum * key_weight.astype(F32), axis=1, keepdims=True)
    full_ref[:, :head_cols] = query_sum.astype(BF16)
    full_ref[:, head_cols : 3 * head_cols] = key_sum.astype(BF16)
    for k in range(parts):
        block = dot_rows(branch_refs[k][0], attended_ref[0])
        for n in range(1, tiles):
            block += dot_rows(branch_refs[k][n], attended_ref[n])
        start = pl.multiple_of((tensor_place ^ k) * share, share)
        full_ref[pl.ds(start, share), 3 * head_cols :] = block.astype(BF16)
    if fast:
        tall = weight_even.shape[1]
        for k in range(weight_even.shape[0]):
            place = grid_place ^ (2 * k)
            weight_even[k] = full_ref[pl.ds(pl.multiple_of(place * tall, tall), tall), :]
            weight_odd[k] = full_ref[pl.ds(pl.multiple_of((place ^ 1) * tall, tall), tall), :]
    else:
        weight_ref[...] = full_ref[...]


def project_back(fast, own, dq, dkv, normed, in_flat, attended, branch, grid_count):
    tiles, head_cols, _ = dq.shape
    key_tiles = dkv.shape[0]
    width = in_flat.shape[0]
    parts = len(branch)
    columns = 4 * head_cols
    if fast:
        block = jax.ShapeDtypeStruct((parts // 2, width, TILE), BF16)
        weight = jax.ShapeDtypeStruct((grid_count // 2, width // grid_count, columns), BF16)
        shapes = (block,) * 4 + (weight,) * 2
    else:
        shapes = (
            jax.ShapeDtypeStruct((key_tiles, width, TILE), BF16),
            jax.ShapeDtypeStruct((width, columns), BF16),
        )
    shapes = shapes + (jax.ShapeDtypeStruct((width, 1), F32),)
    operands = (dq, dkv, normed, in_flat, attended, *branch)
    return pl.pallas_call(
        functools.partial(project_back_kernel, fast, parts),
        grid=(1,),
        out_shape=shapes,
        in_specs=[pl.BlockSpec(memory_space=pltpu.SMEM)] + whole_specs(operands),
        out_specs=tuple(whole_specs(shapes)),
        scratch_shapes=[pltpu.VMEM((width, columns), BF16)],
        compiler_params=pltpu.CompilerParams(vmem_limit_bytes=VMEM_BYTES),
        cost_estimate=pl.CostEstimate(
            flops=12 * key_tiles * TILE * width * head_cols,
            bytes_accessed=8 * key_tiles * TILE * width,
            transcendentals=0,
        ),
        name="project_back",
    )(own, *operands)


def finish_kernel(input_ref, gain_ref, branch_ref, result_ref, *refs):
    sum_refs = refs[:-2]
    out_ref, grad_ref = refs[-2:]
    rows = input_ref[...]
    width = rows.shape[1]
    values = rows.T
    gain = gain_ref[...]
    grad = sum_refs[0][...].astype(F32)
    for ref in sum_refs[1:]:
        grad += ref[...].astype(F32)
    root = lax.rsqrt(jnp.sum(values * values, axis=0, keepdims=True) * (1.0 / width) + EPSILON)
    scaled = grad * gain
    centre = jnp.sum(scaled * values, axis=0, keepdims=True) * (1.0 / width)
    total = root * scaled - values * (root * root * root * centre)
    grad_ref[...] = (total + branch_ref[...].astype(F32)).T
    out_ref[...] = rows + result_ref[...].astype(F32).T


def finish(block_input, gain, branch, result, sums):
    shape = jax.ShapeDtypeStruct(block_input.shape, F32)
    operands = (block_input, gain, branch, result, *sums)
    return pl.pallas_call(
        finish_kernel,
        grid=(1,),
        out_shape=(shape, shape),
        in_specs=whole_specs(operands),
        out_specs=tuple(whole_specs((shape, shape))),
        compiler_params=pltpu.CompilerParams(vmem_limit_bytes=VMEM_BYTES),
        name="finish",
    )(*operands)


def split_low(values):
    high = values.astype(BF16)
    return high, (values - high.astype(F32)).astype(BF16)


def load_tile(ref, first, count, *place):
    return jnp.concatenate([ref[(first + m, *place)] for m in range(count)], axis=-1)


def expert_kernel(parts, own_ref, *refs):
    state_refs = refs[:parts]
    (grad_ref, other_ref, in_ref, in_t_ref, out_ref, gain_ref) = refs[parts : parts + 6]
    (
        kept_ref,
        sent_ref,
        normed_ref,
        act_ref,
        pre_ref,
        gate_ref,
        router_sum,
        state_ref,
        full_ref,
        back_ref,
        joint_ref,
    ) = refs[parts + 6 :]

    @pl.when(pl.program_id(0) == 0)
    def _():
        router_sum[...] = jnp.zeros_like(router_sum)

    width = gain_ref.shape[0]
    share = width // parts
    hidden = act_ref.shape[1]
    experts = router_sum.shape[0]
    expert, own = own_ref[0], own_ref[1]
    chains, columns = state_ref.shape[0], state_ref.shape[-1]
    merged = kept_ref.shape[1] // chains
    slots = columns // merged
    gain = gain_ref[...]
    for a in range(chains):
        for k in range(parts):
            state_ref[a, own ^ k] = load_tile(state_refs[k], a * merged, merged)
            near = 2 * (k // 2) + ((own & 1) ^ (k & 1))
            full_ref[a, near] = load_tile(
                other_ref if k & 1 else grad_ref, a * merged, merged, k // 2
            )
    for a in range(chains):
        state = state_ref[a].reshape(width, columns).astype(F32)
        root = lax.rsqrt(jnp.sum(state * state, axis=0, keepdims=True) * (1.0 / width) + EPSILON)
        normed = (state * root * gain).astype(BF16)
        normed_ref[a] = normed
        both = dot(in_t_ref[...], normed)
        pre_act, logits = both[:hidden], both[hidden : hidden + experts]
        act_grad = dot(out_ref[...], full_ref[a].reshape(width, columns))
        raised = jnp.exp(logits - jnp.max(logits, axis=0, keepdims=True))
        router_probs = raised / jnp.sum(raised, axis=0, keepdims=True)
        chosen = lax.broadcasted_iota(jnp.int32, logits.shape, 0) == expert
        gate = jnp.sum(jnp.where(chosen, router_probs, 0.0), axis=0, keepdims=True)
        gate_ref[a] = gate
        square = pre_act * pre_act
        cdf = 0.5 + 0.5 * jnp.tanh(pre_act * (GELU_A + (GELU_A * GELU_B) * square))
        activated = pre_act * cdf
        act_ref[a] = activated.astype(BF16)
        rise = (2.0 * GELU_A) + (6.0 * GELU_A * GELU_B) * square
        pre_grad = act_grad * (cdf + activated * (1.0 - cdf) * rise)
        low_grad = pre_grad.astype(BF16)
        pre_ref[a] = low_grad
        gate_grad = jnp.sum(activated * act_grad, axis=0, keepdims=True)
        logit_grad = gate_grad * (chosen.astype(F32) - router_probs)
        centre = jnp.sum(pre_grad * pre_act, axis=0, keepdims=True)
        centre += jnp.sum(logit_grad * logits, axis=0, keepdims=True)
        joint_ref[a, :hidden, :] = low_grad
        joint_ref[a, hidden:, :] = jnp.concatenate(split_low(logit_grad), axis=0)
        high, low = split_low(logit_grad * gate)
        router_sum[...] += dot_rows(high, normed) + dot_rows(low, normed)
        normed_grad = dot(in_ref[...], joint_ref[a])
        state = state_ref[a].reshape(width, columns).astype(F32)
        back = (root * gate) * (normed_grad * gain - state * (root * centre * (1.0 / width)))
        back_ref[a] = back.astype(BF16).reshape(parts, share, columns)
        for k in range(parts):
            block = back_ref[a, own ^ k]
            target = sent_ref if k & 1 else kept_ref
            for m in range(merged):
                target[k // 2, a * merged + m] = block[:, m * slots : (m + 1) * slots]


def result_kernel(parts, own_ref, *refs):
    chunks = (len(refs) - 11) // 4
    sets = [refs[4 * c : 4 * c + 4] for c in range(chunks)]
    (
        grad_ref,
        other_ref,
        in_ref,
        out_t_ref,
        kept_ref,
        sent_ref,
        in_sum,
        out_sum,
        gain_sum,
        result_ref,
        full_ref,
    ) = refs[4 * chunks :]

    @pl.when(pl.program_id(0) == 0)
    def _():
        in_sum[...] = jnp.zeros_like(in_sum)
        out_sum[...] = jnp.zeros_like(out_sum)

    own = own_ref[1]
    width = out_t_ref.shape[0]
    share = width // parts
    merged = kept_ref.shape[1]
    for c in range(chunks):
        normed_ref, act_ref, pre_ref, gate_ref = sets[c]
        gate, activated = gate_ref[0], act_ref[0]
        columns = activated.shape[-1]
        slots = columns // merged
        for k in range(parts):
            near = 2 * (k // 2) + ((own & 1) ^ (k & 1))
            source = other_ref if k & 1 else grad_ref
            full_ref[c, near] = jnp.concatenate(
                [source[m, k // 2, :, c * slots : (c + 1) * slots] for m in range(merged)], axis=-1
            )
        result = dot(out_t_ref[...], activated) * gate
        result_ref[c] = result.astype(BF16).reshape(parts, share, columns)
        for k in range(parts):
            block = result_ref[c, own ^ k]
            target = sent_ref if k & 1 else kept_ref
            for m in range(merged):
                target[k // 2, m, :, c * slots : (c + 1) * slots] = block[
                    :, m * slots : (m + 1) * slots
                ]
        normed = (normed_ref[0].astype(F32) * gate).astype(BF16)
        in_sum[...] += dot_rows(normed, pre_ref[0])
        scaled = (full_ref[c].reshape(width, columns).astype(F32) * gate).astype(BF16)
        out_sum[...] += dot_rows(activated, scaled)

    @pl.when(pl.program_id(0) == pl.num_programs(0) - 1)
    def _():
        gain_sum[...] = jnp.sum(in_sum[...] * in_ref[...].astype(F32), axis=1, keepdims=True)


def fixed_spec(shape):
    return pl.BlockSpec(shape, lambda g: (0,) * len(shape))


def run_expert(own, states, grads, chunk, merged, chains, weights):
    parts = len(states)
    count, share, slots = states[0].shape
    width = share * parts
    columns = merged * slots
    steps = count // merged
    hidden = weights[2].shape[0]
    joint = weights[0].shape[1]
    experts = (joint - hidden) // 2
    half = parts // 2
    taken = merged * chains
    piece = pl.BlockSpec((taken, share, slots), lambda g: (g, 0, 0))
    grad_piece = pl.BlockSpec((taken, half, share, slots), lambda g: (g, 0, 0, chunk))
    split = pl.BlockSpec((half, taken, share, slots), lambda g: (0, g, 0, 0))
    wide = pl.BlockSpec((chains, width, columns), lambda g: (g, 0, 0))
    deep = pl.BlockSpec((chains, hidden, columns), lambda g: (g, 0, 0))
    flat = pl.BlockSpec((chains, 1, columns), lambda g: (g, 0, 0))
    return pl.pallas_call(
        functools.partial(expert_kernel, parts),
        grid=(steps // chains,),
        out_shape=(
            jax.ShapeDtypeStruct((half, count, share, slots), BF16),
            jax.ShapeDtypeStruct((half, count, share, slots), BF16),
            jax.ShapeDtypeStruct((steps, width, columns), BF16),
            jax.ShapeDtypeStruct((steps, hidden, columns), BF16),
            jax.ShapeDtypeStruct((steps, hidden, columns), BF16),
            jax.ShapeDtypeStruct((steps, 1, columns), F32),
            jax.ShapeDtypeStruct((experts, width), F32),
        ),
        in_specs=[pl.BlockSpec(memory_space=pltpu.SMEM)]
        + [piece] * parts
        + [grad_piece] * 2
        + [fixed_spec(weight.shape) for weight in weights],
        out_specs=(split, split, wide, deep, deep, flat, fixed_spec((experts, width))),
        scratch_shapes=[
            pltpu.VMEM((chains, parts, share, columns), BF16),
            pltpu.VMEM((chains, parts, share, columns), BF16),
            pltpu.VMEM((chains, parts, share, columns), BF16),
            pltpu.VMEM((chains, joint, columns), BF16),
        ],
        compiler_params=pltpu.CompilerParams(vmem_limit_bytes=VMEM_BYTES),
        cost_estimate=pl.CostEstimate(
            flops=16 * steps * columns * width * hidden,
            bytes_accessed=16 * steps * columns * width,
            transcendentals=steps * columns * hidden,
        ),
        name="expert",
    )(own, *states, *grads, *weights)


def run_result(own, saved, grads, merged, weights):
    chunks = len(saved)
    steps, width, columns = saved[0][0].shape
    hidden = saved[0][1].shape[1]
    _, half, share, _ = grads[0].shape
    parts = 2 * half
    slots = columns // merged
    wide = pl.BlockSpec((1, width, columns), lambda g: (g, 0, 0))
    deep = pl.BlockSpec((1, hidden, columns), lambda g: (g, 0, 0))
    flat = pl.BlockSpec((1, 1, columns), lambda g: (g, 0, 0))
    grad_piece = pl.BlockSpec((merged, half, share, slots * chunks), lambda g: (g, 0, 0, 0))
    split = pl.BlockSpec((half, merged, share, slots * chunks), lambda g: (0, g, 0, 0))
    total = jax.ShapeDtypeStruct((half, steps * merged, share, slots * chunks), BF16)
    return pl.pallas_call(
        functools.partial(result_kernel, parts),
        grid=(steps,),
        out_shape=(
            total,
            total,
            jax.ShapeDtypeStruct((width, hidden), F32),
            jax.ShapeDtypeStruct((hidden, width), F32),
            jax.ShapeDtypeStruct((width, 1), F32),
        ),
        in_specs=[pl.BlockSpec(memory_space=pltpu.SMEM)]
        + [wide, deep, deep, flat] * chunks
        + [grad_piece] * 2
        + [fixed_spec(weight.shape) for weight in weights],
        out_specs=(
            split,
            split,
            fixed_spec((width, hidden)),
            fixed_spec((hidden, width)),
            fixed_spec((width, 1)),
        ),
        scratch_shapes=[
            pltpu.VMEM((chunks, parts, share, columns), BF16),
            pltpu.VMEM((chunks, parts, share, columns), BF16),
        ],
        compiler_params=pltpu.CompilerParams(vmem_limit_bytes=VMEM_BYTES),
        cost_estimate=pl.CostEstimate(
            flops=16 * chunks * steps * columns * width * hidden,
            bytes_accessed=12 * chunks * steps * columns * width,
            transcendentals=0,
        ),
        name="result",
    )(own, *[array for arrays in saved for array in arrays], *grads, *weights)


def shards(
    block_input,
    attn_in_weight,
    attn_out_weight,
    position_bias,
    norm_gains,
    router_weight,
    expert_in,
    expert_out,
    segment_ids,
    expert_ids,
    out_grad,
):
    tensor_count, seq_count = lax.axis_size("tensor"), lax.axis_size("seq")
    tensor_place, seq_place = lax.axis_index("tensor"), lax.axis_index("seq")
    grid_count = lax.axis_size("dp") * seq_count
    grid_place = lax.axis_index("dp") * seq_count + seq_place
    local_count, width = block_input.shape
    group_count = local_count * tensor_count
    share = width // tensor_count
    bucket_count, heads = position_bias.shape
    head_cols = attn_in_weight.shape[2]
    experts = router_weight.shape[1]
    capacity = max(2, 2 * group_count // experts)
    tiles = group_count // TILE
    key_tiles = tiles * seq_count
    fast = seq_count == 2 and local_count == TILE and grid_count == 8

    def tiled(pieces):
        pieces = reorder(pieces, tensor_place)
        if local_count == TILE:
            return jnp.stack(pieces)
        return jnp.concatenate(pieces, axis=-1)[None]

    half = tensor_count // 2
    core = tensor_place & 1
    own_rows = jnp.concatenate(
        [
            jnp.transpose(block_input.astype(BF16)),
            jnp.pad(segment_ids.astype(BF16), ((0, 15), (0, 0))),
        ]
    )
    weight_piece = jnp.concatenate(
        [attn_in_weight[0], attn_in_weight[1], attn_in_weight[2], jnp.transpose(attn_out_weight)],
        axis=1,
    )
    grad_rows = jnp.transpose(out_grad.astype(BF16)).reshape(half, 2, share, local_count)
    grad_mine = lax.dynamic_index_in_dim(grad_rows, core, 1, keepdims=False)
    grad_theirs = lax.dynamic_index_in_dim(grad_rows, core ^ 1, 1, keepdims=False)
    in_plain, out_plain = expert_in[0], expert_out[0]
    if fast:
        far_rows = swap(own_rows, "seq", 1)
        near_two = swap(own_rows, "tensor", 2)
        columns = [weight_piece] + [swap(weight_piece, "dp", k) for k in range(1, grid_count // 2)]
        grad_other = swap(grad_theirs, "tensor", 1)
        far_rows, near_two, columns, grad_other, position_bias, expert_ids, in_plain, out_plain = (
            lax.optimization_barrier(
                (
                    far_rows,
                    near_two,
                    columns,
                    grad_other,
                    position_bias,
                    expert_ids,
                    in_plain,
                    out_plain,
                )
            )
        )
        far_two = swap(far_rows, "tensor", 2)
        near_columns = swap(weight_piece, "seq", 1)
        far_columns = swap(jnp.stack(columns[1:]), "seq", 1)
        near_one, near_three = swap(own_rows, "tensor", 1), swap(near_two, "tensor", 1)
    else:
        grad_other = swap(grad_theirs, "tensor", 1)
        both_rows = lax.all_gather(own_rows, "seq", axis=0, tiled=False)
        row_pieces = gather_relative(both_rows, "tensor")
        own_first = seq_place * tiles
        row_pieces = jnp.concatenate(reorder(row_pieces, tensor_place), axis=-1)
        row_pieces = row_pieces.reshape(seq_count, -1, tiles, TILE)
        row_pieces = [jnp.moveaxis(row_pieces, 2, 1).reshape(key_tiles, -1, TILE)]
        weight_pieces = [lax.all_gather(weight_piece, ("dp", "seq"), axis=0, tiled=True)]

    bias = bias_tiles(position_bias)
    in_t, out_t = jnp.transpose(in_plain), jnp.transpose(out_plain)
    router_t = jnp.transpose(router_weight)
    in_joint = jnp.concatenate([in_plain, router_weight, router_weight], axis=1)
    in_t = jnp.concatenate([in_t, router_t, router_t])
    route_all = expert_ids[:, 0]
    expert_range = jnp.arange(experts, dtype=jnp.int32)
    route_hot = (route_all[:, None] == expert_range[None, :]).astype(jnp.int32)
    slot_rank = jnp.sum(jnp.cumsum(route_hot, axis=0) * route_hot, axis=-1) - 1
    target = (route_all * capacity + slot_rank).reshape(1, tiles, TILE, 1)
    places = jnp.arange(experts * capacity, dtype=jnp.int32).reshape(experts, 1, 1, capacity)
    chunks = 2 if capacity >= TILE else 1
    slots = capacity // chunks
    spread = max(1, TILE // capacity)
    merged = max(1, TILE // (slots * spread))

    def exchange(values):
        return lax.all_to_all(values, ("dp", "seq"), split_axis=0, concat_axis=0, tiled=True)

    def joined(values):
        if spread == 1:
            return values
        shape = values.shape
        values = values.reshape((-1, spread) + shape[1:])
        return jnp.moveaxis(values, 1, -2).reshape(
            (shape[0] // spread,) + shape[1:-1] + (spread * shape[-1],)
        )

    def parted(values):
        if spread == 1:
            return values
        shape = values.shape
        values = values.reshape(shape[:-1] + (spread, shape[-1] // spread))
        return jnp.moveaxis(values, -2, 1).reshape((-1,) + shape[1:-1] + (shape[-1] // spread,))


    gain_one = norm_gains[0][:, None]
    gain_two = norm_gains[1][:, None]
    if fast:
        (
            far_two,
            far_columns,
            gain_one,
            bias,
            in_t,
            in_joint,
            out_t,
            target,
            gain_two,
            grad_mine,
            grad_other,
        ) = lax.optimization_barrier(
            (
                far_two,
                far_columns,
                gain_one,
                bias,
                in_t,
                in_joint,
                out_t,
                target,
                gain_two,
                grad_mine,
                grad_other,
            )
        )
        far_one, far_three = swap(far_rows, "tensor", 1), swap(far_two, "tensor", 1)
        row_pieces = [own_rows, near_one, near_two, near_three]
        row_pieces += [far_rows, far_one, far_two, far_three]
        row_pieces = [rows[None] for rows in row_pieces]
        weight_pieces = [weight_piece, near_columns]
        for k in range(1, grid_count // 2):
            weight_pieces += [columns[k], far_columns[k - 1]]
        own_first = jnp.int32(0)
    own = jnp.stack([grid_place, tensor_place, seq_place, own_first]).astype(jnp.int32)
    onehot = (target == places).astype(BF16)
    grad_pair = swap(jnp.stack([grad_mine, grad_other]), "tensor", 2)
    grad_here = tiled([grad_mine, grad_other, grad_pair[0], grad_pair[1]])
    grad_buffer = einsum("nkdq,enqs->ekds", grad_here, onehot).astype(BF16)
    meta, queries, keys_values, normed_tiles, input_share, in_flat, out_blocks, out_t_blocks = (
        project(own, row_pieces, weight_pieces, gain_one, tiles, key_tiles, share)
    )
    queries, grad_buffer = lax.optimization_barrier((queries, grad_buffer))
    grad_arrived = joined(exchange(grad_buffer))
    exact, attended, logs, attn_even, attn_odd = attend(
        meta, queries, keys_values, bias, out_blocks
    )
    attn_share = sum_tensor(attn_even, attn_odd)
    state_share = (input_share.astype(F32) + attn_share).astype(BF16)
    state_share, grad_arrived = lax.optimization_barrier((state_share, grad_arrived))
    grad_near = swap(grad_arrived, "tensor", 1)

    weights = (in_joint, in_t, expert_out[0], gain_two)
    grads = (grad_arrived, grad_near)
    buffers = [
        einsum("ndq,enqs->eds", state_share, onehot[..., c * slots : (c + 1) * slots]).astype(BF16)
        for c in range(chunks)
    ]
    buffers = list(lax.optimization_barrier(tuple(buffers)))
    arrivals = [joined(exchange(buffer)) for buffer in buffers]
    chains = 2 if arrivals[0].shape[0] // merged % 2 == 0 else 1
    gathered = []
    for arrival in arrivals:
        gathered.append(
            [arrival, swap(arrival, "tensor", 1), swap(arrival, "tensor", 2)]
        )
    gathered[0][0], gathered[-1][0] = lax.optimization_barrier((gathered[0][0], gathered[-1][0]))
    saved, halves, crossed = [], [], []
    small = jnp.zeros((experts, width), F32)
    for c in range(chunks):
        gathered[c].append(swap(gathered[c][2], "tensor", 1))
        kept, sent, normed_two, activated, pre_grad, gate, router_sum = run_expert(
            own, gathered[c], grads, c, merged, chains, weights
        )
        saved.append((normed_two, activated, pre_grad, gate))
        if c + 1 < chunks:
            sent, gathered[c + 1][2] = lax.optimization_barrier((sent, gathered[c + 1][2]))
        if c > 0:
            sent, crossed[c - 1] = lax.optimization_barrier((sent, crossed[c - 1]))
        near, got, to_send = core_step(kept, sent)
        if c + 1 == chunks:
            own_late, to_send = lax.optimization_barrier((own, to_send))
        halves.append((near, got))
        crossed.append(swap(to_send, "tensor", 2))
        small = small + router_sum
    returned = [
        exchange(parted(chip_step(*halves[c], crossed[c]).astype(BF16)))
        for c in range(chunks - 1)
    ]
    result_even, result_odd, grad_expert_in, grad_expert_out, in_gain = run_result(
        own_late, saved, grads, merged, (expert_in[0], out_t)
    )
    tied = lax.optimization_barrier((result_odd, crossed[-1], *returned))
    result_odd, crossed[-1], returned = tied[0], tied[1], list(tied[2:])
    returned.append(exchange(parted(chip_step(*halves[-1], crossed[-1]).astype(BF16))))
    gain_part = in_gain[:, 0] + jnp.sum(small * router_t.astype(F32), axis=0)
    router_gains = jnp.concatenate([small, (gain_part / norm_gains[1])[None]])
    state_grad = lax.dynamic_index_in_dim(grad_here, tensor_place // 2, 1, keepdims=False)
    state_grad = state_grad.astype(F32)
    for c in range(chunks):
        state_grad = state_grad + einsum(
            "eds,enqs->ndq", returned[c], onehot[..., c * slots : (c + 1) * slots]
        )
    state_grad = state_grad.astype(BF16)
    result_near, result_got, result_sent = core_step(result_even, result_odd)
    result_far = swap(result_sent, "tensor", 2)

    branch = [state_grad, swap(state_grad, "tensor", 1), swap(state_grad, "tensor", 2)]
    result_far, branch[2] = lax.optimization_barrier((result_far, branch[2]))
    branch.append(swap(branch[2], "tensor", 1))
    result_total = chip_step(result_near, result_got, result_far).astype(BF16)
    result_back = exchange(parted(result_total))
    dq, dkv, bias_rows = attend_back(
        meta, queries, keys_values, bias, out_t_blocks, exact, logs, branch, bucket_count
    )
    dq, dkv, bias_rows, result_back = lax.optimization_barrier((dq, dkv, bias_rows, result_back))

    def joined_small():
        bias_padded = lax.dynamic_update_slice_in_dim(
            jnp.zeros((heads * tensor_count, bucket_count), F32),
            jnp.sum(bias_rows, axis=2),
            tensor_place * heads,
            0,
        )
        return jnp.concatenate(
            [router_gains.reshape(-1), gain_part[:, 0] / norm_gains[0], bias_padded.reshape(-1)]
        )

    def result_rows_of():
        shares = attn_share + einsum("eds,enqs->ndq", result_back, onehot)
        return jnp.moveaxis(shares.astype(BF16), 0, 1).reshape(share, tensor_count, local_count)

    if fast:
        far_even, far_odd, own_even, own_odd, weight_even, weight_odd, gain_part = project_back(
            True, own, dq, dkv, normed_tiles, in_flat, attended, branch, grid_count
        )
        far_near, far_got, far_send = core_step(far_even, far_odd)
        own_near, own_got, own_send = core_step(own_even, own_odd)
        weight_sent = swap(weight_odd, "seq", 1)
        far_send, own_send, gain_part, result_back = lax.optimization_barrier(
            (far_send, own_send, gain_part, result_back)
        )
        far_sent = swap(far_send, "tensor", 2)
        small = sum_all(joined_small(), ("seq",))
        result_share = result_rows_of()
        far_sent, weight_sent, small, result_share, own_send = lax.optimization_barrier(
            (far_sent, weight_sent, small, result_share, own_send)
        )
        own_sent = swap(own_send, "tensor", 2)
        far_sum = chip_step(far_near, far_got, far_sent).astype(BF16)
        sums = [own_near, own_got, own_sent, swap(far_sum, "seq", 1)]
        weight_half = weight_even.astype(F32) + weight_sent.astype(F32)
        weight_grad = weight_half[0]
        for k in range(1, grid_count // 2):
            weight_grad = weight_grad + swap(weight_half[k].astype(BF16), "dp", k).astype(F32)
    else:
        row_part, weight_part, gain_part = project_back(
            False, own, dq, dkv, normed_tiles, in_flat, attended, branch, grid_count
        )
        row_part = lax.psum_scatter(row_part, "seq", scatter_dimension=0, tiled=True)
        row_part = jnp.moveaxis(row_part, 0, 1).reshape(width, tensor_count, local_count)
        blocks = [
            lax.dynamic_index_in_dim(row_part, tensor_place ^ k, 1, keepdims=False)
            for k in range(tensor_count)
        ]
        sums = [sum_tensor(jnp.stack(blocks[0::2]), jnp.stack(blocks[1::2]))]
        small = sum_all(joined_small(), ("seq",))
        result_share = result_rows_of()
        weight_grad = lax.psum_scatter(
            weight_part, ("dp", "seq"), scatter_dimension=0, tiled=True
        ).astype(F32)
    grad_attn_in = jnp.stack(
        [weight_grad[:, c * head_cols : (c + 1) * head_cols] for c in range(3)]
    )
    grad_attn_out = jnp.transpose(weight_grad[:, 3 * head_cols :])

    small = sum_all(small, ("dp", "tensor"))
    first, second = experts * width, (experts + 1) * width
    grad_router = jnp.transpose(small[:first].reshape(experts, width))
    grad_gains = jnp.stack([small[second : second + width], small[first:second]])
    bias_sum = small[second + width :].reshape(heads * tensor_count, bucket_count)
    grad_bias = jnp.transpose(lax.dynamic_slice_in_dim(bias_sum, tensor_place * heads, heads, 0))

    result_rows = lax.all_to_all(
        jnp.moveaxis(result_share, 1, 0), "tensor", split_axis=0, concat_axis=0, tiled=True
    ).reshape(width, local_count)
    if local_count == TILE:
        own_branch = [
            lax.dynamic_index_in_dim(piece, tensor_place, 0, keepdims=False) for piece in branch
        ]
    else:
        own_branch = [
            lax.dynamic_slice_in_dim(piece[0], tensor_place * local_count, local_count, 1)
            for piece in branch
        ]
    own_branch = jnp.concatenate(reorder(own_branch, tensor_place))
    block_out, input_grad = finish(block_input, gain_one, own_branch, result_rows, sums)
    return (
        block_out,
        input_grad,
        grad_attn_in,
        grad_attn_out,
        grad_bias,
        grad_gains,
        grad_router,
        grad_expert_in[None],
        grad_expert_out[None],
    )


def solution(mesh):
    return jax.shard_map(
        shards,
        mesh=mesh,
        in_specs=(
            P(("dp", "seq", "tensor"), None),
            P(None, ("dp", "seq"), "tensor"),
            P("tensor", ("dp", "seq")),
            P(None, "tensor"),
            P(),
            P(),
            P(("dp", "seq"), None, "tensor"),
            P(("dp", "seq"), "tensor", None),
            P("dp", ("seq", "tensor")),
            P(("dp", "seq"), None),
            P(("dp", "seq", "tensor"), None),
        ),
        out_specs=(
            P(("dp", "seq", "tensor"), None),
            P(("dp", "seq", "tensor"), None),
            P(None, ("dp", "seq"), "tensor"),
            P("tensor", ("dp", "seq")),
            P(None, "tensor"),
            P(),
            P(),
            P(("dp", "seq"), None, "tensor"),
            P(("dp", "seq"), "tensor", None),
        ),
        check_vma=False,
    )
```

profile of v0, /device:TPU:0, one launch (start us, length us, event | category | flops | bytes accessed | tf_op | source)
XLA Modules:
  0.0 365.7 jit_solution(8365223228533729113)
XLA Ops:
  2.5 5.1 %collective-permute-start.4 = (bf16[96,768]{1,0:T(8,128)(2,1)S(1)}, bf16[96,768]{1,0:T(8,128)(2,1)S(1)}, u32[]{:S(2)}, u32[]{:S(2)}) collective-permute-start(bf16[96,768]{1,0:T(8,128)(2,1)S(1)} %pad_maximum_fusion.13.refs_8_), channel_id=1, source_target_pairs={{0,24},{8,16},{16,8},{24,0},{1,25},{9,17},{17,9},{25,1},{2,26},{10... | collective-permute-start | bytes 442376 | tf_op jit(solution)/shard_map/ppermute | solution.py:43
  14.2 2.2 broadcast_compare_fusion.21
  24.0 2.3 reduce-window.6
  30.4 3.8 %select_add_fusion = f32[3,3,128,128]{3,2,0,1:T(8,128)S(1)} fusion(f32[3]{0:T(128)S(1)} %get-tuple-element.249, f32[3]{0:T(128)S(1)} %get-tuple-element.250, f32[3]{0:T(128)S(1)} %get-tuple-element.251, f32[3]{0:T(128)S(1)} %get-tuple-element.252, f32[3]{0:T(128)S(1)} %get-tuple-element.253, f32[3]{0:T(128)S(1)} %get-tuple-element.254, ...), kind=kLoop, calls=%fused_computation.81 | loop fusion | flops 9289728 | bytes 2163072 | tf_op jit(solution)/shard_map/add | solution.py:113
  41.8 4.4 %broadcast_multiply_fusion.bias_ref = f32[5,3,256,256]{3,2,1,0:T(8,128)} fusion(f32[5,3,256,256]{3,2,1,0:T(8,128)} %fusion.74), kind=kLoop, calls=%fused_computation.19 | loop fusion | flops 983040 | bytes 7864320 | tf_op jit(solution)/shard_map/mul | solution.py:138
  50.5 6.5 %collective-permute-done.13 = bf16[2,2,192,256]{3,2,1,0:T(8,128)(2,1)} collective-permute-done((bf16[2,2,192,256]{3,2,1,0:T(8,128)(2,1)}, bf16[2,2,192,256]{3,2,1,0:T(8,128)(2,1)}, u32[]{:S(2)}, u32[]{:S(2)}) %collective-permute-start.13) | collective-permute-done | bytes 393248 | tf_op jit(solution)/shard_map/ppermute | solution.py:43
  58.2 3.3 fusion.20
  62.3 6.4 %project.1 = (s32[15]{0:T(128)S(1)}, bf16[4,192,256]{2,1,0:T(8,128)(2,1)S(1)}, bf16[8,384,256]{2,1,0:T(8,128)(2,1)}, bf16[8,768,256]{2,1,0:T(8,128)(2,1)}, bf16[...) custom-call(s32[4]{0:T(128)S(1)} %pad_add_fusion.own_ref, ...), custom_call_target="tpu_custom_call" | custom-call | flops 1811939328 | bytes 12582912 | tf_op jit(solution)/shard_map/project/pallas_call | solution.py:561
  71.0 5.5 %all-to-all-start = ((bf16[8,2,192,256]{3,2,1,0:T(8,128)(2,1)}), bf16[8,2,192,256]{3,2,1,0:T(8,128)(2,1)}, u32[]{:S(2)}, u32[]{:S(2)}) async-start(bf16[8,2,192,256]{3,2,1,0:T(8,128)(2,1)} %fusion.20), calls=%async_computation | async-start | bytes 3145728 | tf_op jit(solution)/shard_map/all_to_all | solution.py:1046
  77.9 17.9 %attend.1 = (f32[4,192,256]{2,1,0:T(8,128)S(1)}, bf16[4,192,256]{2,1,0:T(8,128)(2,1)S(1)}, f32[4,3,1,256]{3,2,1,0:T(1,128)S(1)}, bf16[2,4,192,256]{3,2,1,0:T(8,128)(2,1)S(1)}, bf16[2,4,192,256]{3,2,1,0:T(8,128)(2,1)S(1)}) custom-call(s32[15]{0:T(128)S(1)} %get-tuple-element.121.meta_ref, bf16[4,192,256]{2,1,0:T(8,128)(2,1)S(1)} %copy-done.30, ...), custom_call_target="tpu_custom_call" | custom-call | flops 1610612736 | bytes 16777216 | tf_op jit(solution)/shard_map/attend/pallas_call | solution.py:288
  96.0 2.1 collective-permute-done.14
  99.8 2.4 broadcast_compare_fusion
  102.1 7.4 %collective-permute-done.15 = bf16[4,192,256]{2,1,0:T(8,128)(2,1)S(1)} collective-permute-done((bf16[4,192,256]{2,1,0:T(8,128)(2,1)S(1)}, bf16[4,192,256]{2,1,0:T(8,128)(2,1)S(1)}, u32[]{:S(2)}, u32[]{:S(2)}) %collective-permute-start.15) | collective-permute-done | bytes 393248 | tf_op jit(solution)/shard_map/ppermute | solution.py:43
  110.5 3.7 %all-to-all-done.refs_4_.refs_8_ = bf16[8,2,192,256]{3,2,1,0:T(8,128)(2,1)} async-done(((bf16[8,2,192,256]{3,2,1,0:T(8,128)(2,1)}), bf16[8,2,192,256]{3,2,1,0:T(8,128)(2,1)}, u32[]{:S(2)}, u32[]{:S(2)}) %all-to-all-start) | async-done | bytes 1572896 | tf_op jit(solution)/shard_map/all_to_all | solution.py:1046
  114.2 2.8 fusion.62
  117.8 16.3 %all_to_all.35.refs_0_ = bf16[8,192,128]{2,1,0:T(8,128)(2,1)} all-to-all(bf16[8,192,128]{2,1,0:T(8,128)(2,1)S(1)} %fusion.59), channel_id=1, replica_groups=mesh['dp'=4,'seq'=2,'tensor'=4] {'dp','seq'}, dimensions={0} | all-to-all | bytes 786432 | tf_op jit(solution)/shard_map/all_to_all | solution.py:1046
  135.5 3.5 all-to-all-start.2
  139.1 5.3 %collective-permute-done.18.refs_2_ = bf16[8,192,128]{2,1,0:T(8,128)(2,1)} collective-permute-done((bf16[8,192,128]{2,1,0:T(8,128)(2,1)}, bf16[8,192,128]{2,1,0:T(8,128)(2,1)}, u32[]{:S(2)}, u32[]{:S(2)}) %collective-permute-start.18) | collective-permute-done | bytes 393248 | tf_op jit(solution)/shard_map/ppermute | solution.py:43
  147.1 3.4 all-to-all-done.2.refs_0_
  153.3 12.5 %expert.2 = (bf16[2,8,192,128]{3,2,1,0:T(8,128)(2,1)S(1)}, bf16[2,8,192,128]{3,2,1,0:T(8,128)(2,1)S(1)}, bf16[4,768,256]{2,1,0:T(8,128)(2,1)}, bf16[4,768,256]{2...) custom-call(s32[4]{0:T(128)S(1)} %pad_add_fusion.own_ref, ...), custom_call_target="tpu_custom_call" | custom-call | flops 9663676416 | bytes 12582912 | tf_op jit(solution)/shard_map/expert/pallas_call | solution.py:865
  169.9 12.1 %expert.3 = (bf16[2,8,192,128]{3,2,1,0:T(8,128)(2,1)S(1)}, bf16[2,8,192,128]{3,2,1,0:T(8,128)(2,1)}, bf16[4,768,256]{2,1,0:T(8,128)(2,1)}, bf16[4,768,256]{2,1,0...) custom-call(s32[4]{0:T(128)S(1)} %pad_add_fusion.own_ref, ...), custom_call_target="tpu_custom_call" | custom-call | flops 9663676416 | bytes 12582912 | tf_op jit(solution)/shard_map/expert/pallas_call | solution.py:865
  184.9 4.3 %all-to-all-start.3 = ((bf16[8,192,128]{2,1,0:T(8,128)(2,1)}), bf16[8,192,128]{2,1,0:T(8,128)(2,1)}, u32[]{:S(2)}, u32[]{:S(2)}) async-start(bf16[8,192,128]{2,1,0:T(8,128)(2,1)} %fusion.86), calls=%async_computation.3 | async-start | bytes 786432 | tf_op jit(solution)/shard_map/all_to_all | solution.py:1046
  194.0 13.7 %result.1 = (bf16[2,8,192,256]{3,2,1,0:T(8,128)(2,1)S(1)}, bf16[2,8,192,256]{3,2,1,0:T(8,128)(2,1)S(1)}, f32[768,768]{1,0:T(8,128)}, f32[768,768]{1,0:T(8,128)}, f32[768,1]{1,0:T(8,128)S(1)}) custom-call(s32[4]{0:T(128)S(1)} %pad_add_fusion.own_ref, bf16[4,768,256]{2,1,0:T(8,128)(2,1)} %get-tuple-element.149.refs_0_, ...), custom_call_target="tpu_custom_call" | custom-call | flops 19327352832 | bytes 18874368 | tf_op jit(solution)/shard_map/result/pallas_call | solution.py:911
  209.0 2.3 fusion.85
  211.3 5.9 %all-to-all-start.4 = ((bf16[8,192,128]{2,1,0:T(8,128)(2,1)}), bf16[8,192,128]{2,1,0:T(8,128)(2,1)S(1)}, u32[]{:S(2)}, u32[]{:S(2)}) async-start(bf16[8,192,128]{2,1,0:T(8,128)(2,1)} %fusion.85), calls=%async_computation.4 | async-start | bytes 786432 | tf_op jit(solution)/shard_map/all_to_all | solution.py:1046
  217.4 2.3 fusion.81
  220.7 3.1 fusion.41
  223.8 5.6 %all-to-all-done.4 = bf16[8,192,128]{2,1,0:T(8,128)(2,1)S(1)} async-done(((bf16[8,192,128]{2,1,0:T(8,128)(2,1)}), bf16[8,192,128]{2,1,0:T(8,128)(2,1)S(1)}, u32[]{:S(2)}, u32[]{:S(2)}) %all-to-all-start.4) | async-done | bytes 393248 | tf_op jit(solution)/shard_map/all_to_all | solution.py:1046
  229.4 2.4 fusion.47.refs_0_
  232.8 15.1 %collective-permute-done.29.refs_2_ = bf16[4,192,256]{2,1,0:T(8,128)(2,1)S(1)} collective-permute-done((bf16[4,192,256]{2,1,0:T(8,128)(2,1)S(1)}, bf16[4,192,256]{2,1,0:T(8,128)(2,1)S(1)}, u32[]{:S(2)}, u32[]{:S(2)}) %collective-permute-start.29) | collective-permute-done | bytes 393248 | tf_op jit(solution)/shard_map/ppermute | solution.py:43
  247.8 2.7 fusion.19
  250.5 5.9 %all-to-all-start.5 = ((bf16[8,192,256]{2,1,0:T(8,128)(2,1)}), bf16[8,192,256]{2,1,0:T(8,128)(2,1)}, u32[]{:S(2)}, u32[]{:S(2)}) async-start(bf16[8,192,256]{2,1,0:T(8,128)(2,1)} %fusion.19), calls=%async_computation.5 | async-start | bytes 1572864 | tf_op jit(solution)/shard_map/all_to_all | solution.py:1046
  264.0 26.3 %attend_back.1 = (bf16[4,192,256]{2,1,0:T(8,128)(2,1)S(1)}, bf16[8,384,256]{2,1,0:T(8,128)(2,1)S(1)}, f32[3,32,128]{2,1,0:T(8,128)S(1)}) custom-call(s32[15]{0:T(128)S(1)} %copy-done.44, bf16[4,192,256]{2,1,0:T(8,128)(2,1)S(1)} %copy-done.31, bf16[8,384,256]{2,1,0:T(8,128)(2,1)} %get-tuple-element.126.kv_ref, ...), custom_call_target="tpu_custom_call" | custom-call | flops 4026531840 | bytes 16777216 | tf_op jit(solution)/shard_map/attend_back/pallas_call | solution.py:451
  297.3 9.6 %project_back.1 = (bf16[2,768,256]{2,1,0:T(8,128)(2,1)S(1)}, bf16[2,768,256]{2,1,0:T(8,128)(2,1)}, bf16[2,768,256]{2,1,0:T(8,128)(2,1)}, bf16[2,768,256]{2,1,0:T...) custom-call(s32[4]{0:T(128)S(1)} %pad_add_fusion.own_ref, ...), custom_call_target="tpu_custom_call" | custom-call | flops 3623878656 | bytes 12582912 | tf_op jit(solution)/shard_map/project_back/pallas_call | solution.py:653
  310.8 2.0 fusion.93
  312.8 1.8 fusion.92
  314.9 2.1 collective-permute-start.36
  317.9 4.0 %fusion.65 = bf16[192,4,256]{2,0,1:T(8,128)(2,1)} fusion(s32[8,256]{1,0:T(8,128)S(1)} %copy-done.86, s32[4,256]{1,0:T(4,128)S(1)} %bitcast.308, bf16[8,192,256]{2,1,0:T(8,128)(2,1)} %all-to-all-done.5, bf16[4,192,256]{2,1,0:T(8,128)(2,1)} %copy-done.68, bf16[2,4,192,256]{3,2,1,0:T(8,128)(2,1)} %copy-done.66, bf16[2,4,192,256]{3,2,1,0:T(8,128)(2,1)S(1)} %copy-done.9), kind=kOutput, calls=%fused_computation.40 | convolution fusion | flops 808779776 | bytes 2371584 | tf_op jit(solution)/shard_map/eds,enqs->ndq/dot_general | solution.py:38
  321.9 4.1 %collective-permute-done.36 = f32[8064]{0:T(1024)S(1)} collective-permute-done((f32[8064]{0:T(1024)S(1)}, f32[8064]{0:T(1024)S(1)}, u32[]{:S(2)}, u32[]{:S(2)}) %collective-permute-start.36) | collective-permute-done | bytes 32288 | tf_op jit(solution)/shard_map/ppermute | solution.py:43
  329.5 3.5 all-to-all-start.6
  333.0 2.0 collective-permute-start.37
  335.1 2.0 fusion.84
  337.4 2.4 collective-permute-done.43
  339.9 2.3 fusion.125
  342.4 2.1 collective-permute-start.39
  344.6 5.0 %collective-permute-done.45 = f32[8064]{0:T(1024)S(1)} collective-permute-done((f32[8064]{0:T(1024)S(1)}, f32[8064]{0:T(1024)S(1)}, u32[]{:S(2)}, u32[]{:S(2)}) %collective-permute-start.45) | collective-permute-done | bytes 32288 | tf_op jit(solution)/shard_map/ppermute | solution.py:43
  352.3 7.5 %collective-permute-done.40 = bf16[96,768]{1,0:T(8,128)(2,1)} collective-permute-done((bf16[96,768]{1,0:T(8,128)(2,1)S(1)}, bf16[96,768]{1,0:T(8,128)(2,1)}, u32[]{:S(2)}, u32[]{:S(2)}) %collective-permute-start.40) | collective-permute-done | bytes 147488 | tf_op jit(solution)/shard_map/ppermute | solution.py:43
  362.5 3.1 finish.1
  (365 shorter events, 92.2 us)
Async XLA Ops:
  2.5 18.0 %collective-permute-start.4 = (bf16[96,768]{1,0:T(8,128)(2,1)S(1)}, bf16[96,768]{1,0:T(8,128)(2,1)S(1)}, u32[]{:S(2)}, u32[]{:S(2)}) collective-permute-start(bf16[96,768]{1,0:T(8,128)(2,1)S(1)} %pad_maximum_fusion.13.refs_8_), channel_id=1, source_target_pairs={{0,24},{8,16},{16,8},{24,0},{1,25},{9,17},{17,9},{25,1},{2,26},{10... | collective-permute-start | bytes 442376 | tf_op jit(solution)/shard_map/ppermute | solution.py:43
  7.6 13.5 %collective-permute-start.3 = (bf16[96,768]{1,0:T(8,128)(2,1)S(1)}, bf16[96,768]{1,0:T(8,128)(2,1)S(1)}, u32[]{:S(2)}, u32[]{:S(2)}) collective-permute-start(bf16[96,768]{1,0:T(8,128)(2,1)S(1)} %pad_maximum_fusion.13.refs_8_), channel_id=1, source_target_pairs={{0,16},{8,24},{16,0},{24,8},{1,17},{9,25},{17,1},{25,9},{2,18},{10... | collective-permute-start | bytes 442376 | tf_op jit(solution)/shard_map/ppermute | solution.py:43
  7.6 14.0 %collective-permute-start.2 = (bf16[96,768]{1,0:T(8,128)(2,1)S(1)}, bf16[96,768]{1,0:T(8,128)(2,1)S(1)}, u32[]{:S(2)}, u32[]{:S(2)}) collective-permute-start(bf16[96,768]{1,0:T(8,128)(2,1)S(1)} %pad_maximum_fusion.13.refs_8_), channel_id=1, source_target_pairs={{0,8},{8,0},{16,24},{24,16},{1,9},{9,1},{17,25},{25,17},{2,10},{10... | collective-permute-start | bytes 442376 | tf_op jit(solution)/shard_map/ppermute | solution.py:43
  11.1 10.9 %collective-permute-start.1 = (bf16[784,256]{1,0:T(8,128)(2,1)}, bf16[784,256]{1,0:T(8,128)(2,1)S(1)}, u32[]{:S(2)}, u32[]{:S(2)}) collective-permute-start(bf16[784,256]{1,0:T(8,128)(2,1)} %get-tuple-element.302), channel_id=1, source_target_pairs={{0,2},{1,3},{2,0},{3,1},{4,6},{5,7},{6,4},{7,5},{8,10},{9,11},{10,... | collective-permute-start | bytes 1204232 | tf_op jit(solution)/shard_map/ppermute | solution.py:43
  12.7 10.4 %collective-permute-start = (bf16[784,256]{1,0:T(8,128)(2,1)}, bf16[784,256]{1,0:T(8,128)(2,1)}, u32[]{:S(2)}, u32[]{:S(2)}) collective-permute-start(bf16[784,256]{1,0:T(8,128)(2,1)} %get-tuple-element.302), channel_id=1, source_target_pairs={{0,4},{4,0},{1,5},{5,1},{2,6},{6,2},{3,7},{7,3},{8,12},{12,8},{9,1... | collective-permute-start | bytes 1204232 | tf_op jit(solution)/shard_map/ppermute | solution.py:43
  21.1 40.3 %collective-permute-start.12 = (bf16[96,768]{1,0:T(8,128)(2,1)S(1)}, bf16[96,768]{1,0:T(8,128)(2,1)S(1)}, u32[]{:S(2)}, u32[]{:S(2)}) collective-permute-start(bf16[96,768]{1,0:T(8,128)(2,1)S(1)} %pad_maximum_fusion.13.refs_8_), channel_id=1, source_target_pairs={{0,4},{4,0},{1,5},{5,1},{2,6},{6,2},{3,7},{7,3},{8,12},{12,8},{9,1... | collective-permute-start | bytes 442376 | tf_op jit(solution)/shard_map/ppermute | solution.py:43
  21.6 39.8 %collective-permute-start.8 = (bf16[784,256]{1,0:T(8,128)(2,1)}, bf16[784,256]{1,0:T(8,128)(2,1)}, u32[]{:S(2)}, u32[]{:S(2)}) collective-permute-start(bf16[784,256]{1,0:T(8,128)(2,1)} %get-tuple-element.302), channel_id=1, source_target_pairs={{0,1},{1,0},{2,3},{3,2},{4,5},{5,4},{6,7},{7,6},{8,9},{9,8},{10,11... | collective-permute-start | bytes 1204232 | tf_op jit(solution)/shard_map/ppermute | solution.py:43
  27.4 18.9 %collective-permute-start.6 = (bf16[784,256]{1,0:T(8,128)(2,1)}, bf16[784,256]{1,0:T(8,128)(2,1)}, u32[]{:S(2)}, u32[]{:S(2)}) collective-permute-start(bf16[784,256]{1,0:T(8,128)(2,1)} %collective-permute-done), channel_id=1, source_target_pairs={{0,2},{1,3},{2,0},{3,1},{4,6},{5,7},{6,4},{7,5},{8,10},{9,11},{10,... | collective-permute-start | bytes 1204232 | tf_op jit(solution)/shard_map/ppermute | solution.py:43
  28.7 17.5 %collective-permute-start.7 = (bf16[3,96,768]{2,1,0:T(8,128)(2,1)}, bf16[3,96,768]{2,1,0:T(8,128)(2,1)}, u32[]{:S(2)}, u32[]{:S(2)}) collective-permute-start(bf16[3,96,768]{2,1,0:T(8,128)(2,1)} %pad_maximum_fusion.9), channel_id=1, source_target_pairs={{0,4},{4,0},{1,5},{5,1},{2,6},{6,2},{3,7},{7,3},{8,12},{12,8},{9,1... | collective-permute-start | bytes 1327112 | tf_op jit(solution)/shard_map/ppermute | solution.py:43
  47.1 9.9 %collective-permute-start.13 = (bf16[2,2,192,256]{3,2,1,0:T(8,128)(2,1)}, bf16[2,2,192,256]{3,2,1,0:T(8,128)(2,1)}, u32[]{:S(2)}, u32[]{:S(2)}) collective-permute-start(bf16[2,2,192,256]{3,2,1,0:T(8,128)(2,1)} %pad_maximum_fusion.10), channel_id=1, source_target_pairs={{0,2},{1,3},{2,0},{3,1},{4,6},{5,7},{6,4},{7,5},{8,10},{9,11},{10,... | collective-permute-start | bytes 1179656 | tf_op jit(solution)/shard_map/ppermute | solution.py:43
  48.7 12.9 %collective-permute-start.10 = (bf16[784,256]{1,0:T(8,128)(2,1)}, bf16[784,256]{1,0:T(8,128)(2,1)}, u32[]{:S(2)}, u32[]{:S(2)}) collective-permute-start(bf16[784,256]{1,0:T(8,128)(2,1)} %collective-permute-done), channel_id=1, source_target_pairs={{0,1},{1,0},{2,3},{3,2},{4,5},{5,4},{6,7},{7,6},{8,9},{9,8},{10,11... | collective-permute-start | bytes 1204232 | tf_op jit(solution)/shard_map/ppermute | solution.py:43
  48.7 12.8 %collective-permute-start.9 = (bf16[784,256]{1,0:T(8,128)(2,1)S(1)}, bf16[784,256]{1,0:T(8,128)(2,1)}, u32[]{:S(2)}, u32[]{:S(2)}) collective-permute-start(bf16[784,256]{1,0:T(8,128)(2,1)S(1)} %collective-permute-done.1), channel_id=1, source_target_pairs={{0,1},{1,0},{2,3},{3,2},{4,5},{5,4},{6,7},{7,6},{8,9},{9,8},{10,11... | collective-permute-start | bytes 1204232 | tf_op jit(solution)/shard_map/ppermute | solution.py:43
  57.0 4.5 %collective-permute-start.11 = (bf16[784,256]{1,0:T(8,128)(2,1)}, bf16[784,256]{1,0:T(8,128)(2,1)S(1)}, u32[]{:S(2)}, u32[]{:S(2)}) collective-permute-start(bf16[784,256]{1,0:T(8,128)(2,1)} %collective-permute-done.6), channel_id=1, source_target_pairs={{0,1},{1,0},{2,3},{3,2},{4,5},{5,4},{6,7},{7,6},{8,9},{9,8},{10,11... | collective-permute-start | bytes 1204232 | tf_op jit(solution)/shard_map/ppermute | solution.py:43
  71.0 43.2 %all-to-all-start = ((bf16[8,2,192,256]{3,2,1,0:T(8,128)(2,1)}), bf16[8,2,192,256]{3,2,1,0:T(8,128)(2,1)}, u32[]{:S(2)}, u32[]{:S(2)}) async-start(bf16[8,2,192,256]{3,2,1,0:T(8,128)(2,1)} %fusion.20), calls=%async_computation | async-start | bytes 3145728 | tf_op jit(solution)/shard_map/all_to_all | solution.py:1046
  95.8 2.4 collective-permute-start.14
  98.3 11.3 %collective-permute-start.15 = (bf16[4,192,256]{2,1,0:T(8,128)(2,1)S(1)}, bf16[4,192,256]{2,1,0:T(8,128)(2,1)S(1)}, u32[]{:S(2)}, u32[]{:S(2)}) collective-permute-start(bf16[4,192,256]{2,1,0:T(8,128)(2,1)S(1)} %fusion.89), channel_id=1, source_target_pairs={{0,2},{1,3},{2,0},{3,1},{4,6},{5,7},{6,4},{7,5},{8,10},{9,11},{10,... | collective-permute-start | bytes 1179656 | tf_op jit(solution)/shard_map/ppermute | solution.py:43
  114.2 36.8 %collective-permute-start.20 = (bf16[8,2,192,256]{3,2,1,0:T(8,128)(2,1)}, bf16[8,2,192,256]{3,2,1,0:T(8,128)(2,1)}, u32[]{:S(2)}, u32[]{:S(2)}) collective-permute-start(bf16[8,2,192,256]{3,2,1,0:T(8,128)(2,1)} %all-to-all-done.refs_4_.refs_8_), channel_id=1, source_target_pairs={{0,1},{1,0},{2,3},{3,2},{4,5},{5,4},{6,7},{7,6},{8,9},{9,8},{10,11... | collective-permute-start | bytes 4718600 | tf_op jit(solution)/shard_map/ppermute | solution.py:43
  134.0 10.3 %collective-permute-start.18 = (bf16[8,192,128]{2,1,0:T(8,128)(2,1)}, bf16[8,192,128]{2,1,0:T(8,128)(2,1)}, u32[]{:S(2)}, u32[]{:S(2)}) collective-permute-start(bf16[8,192,128]{2,1,0:T(8,128)(2,1)} %all_to_all.35.refs_0_), channel_id=1, source_target_pairs={{0,2},{1,3},{2,0},{3,1},{4,6},{5,7},{6,4},{7,5},{8,10},{9,11},{10,... | collective-permute-start | bytes 1179656 | tf_op jit(solution)/shard_map/ppermute | solution.py:43
  135.5 14.9 %all-to-all-start.2 = ((bf16[8,192,128]{2,1,0:T(8,128)(2,1)}), bf16[8,192,128]{2,1,0:T(8,128)(2,1)S(1)}, u32[]{:S(2)}, u32[]{:S(2)}) async-start(bf16[8,192,128]{2,1,0:T(8,128)(2,1)} %fusion.62), calls=%async_computation.2 | async-start | bytes 786432 | tf_op jit(solution)/shard_map/all_to_all | solution.py:1046
  139.0 12.0 %collective-permute-start.17 = (bf16[8,192,128]{2,1,0:T(8,128)(2,1)}, bf16[8,192,128]{2,1,0:T(8,128)(2,1)}, u32[]{:S(2)}, u32[]{:S(2)}) collective-permute-start(bf16[8,192,128]{2,1,0:T(8,128)(2,1)} %all_to_all.35.refs_0_), channel_id=1, source_target_pairs={{0,1},{1,0},{2,3},{3,2},{4,5},{5,4},{6,7},{7,6},{8,9},{9,8},{10,11... | collective-permute-start | bytes 1179656 | tf_op jit(solution)/shard_map/ppermute | solution.py:43
  144.4 6.6 %collective-permute-start.19 = (bf16[8,192,128]{2,1,0:T(8,128)(2,1)}, bf16[8,192,128]{2,1,0:T(8,128)(2,1)}, u32[]{:S(2)}, u32[]{:S(2)}) collective-permute-start(bf16[8,192,128]{2,1,0:T(8,128)(2,1)} %collective-permute-done.18.refs_2_), channel_id=1, source_target_pairs={{0,1},{1,0},{2,3},{3,2},{4,5},{5,4},{6,7},{7,6},{8,9},{9,8},{10,11... | collective-permute-start | bytes 1179656 | tf_op jit(solution)/shard_map/ppermute | solution.py:43
  150.5 15.4 %collective-permute-start.21 = (bf16[8,192,128]{2,1,0:T(8,128)(2,1)S(1)}, bf16[8,192,128]{2,1,0:T(8,128)(2,1)S(1)}, u32[]{:S(2)}, u32[]{:S(2)}) collective-permute-start(bf16[8,192,128]{2,1,0:T(8,128)(2,1)S(1)} %all-to-all-done.2.refs_0_), channel_id=1, source_target_pairs={{0,2},{1,3},{2,0},{3,1},{4,6},{5,7},{6,4},{7,5},{8,10},{9,11},{10,... | collective-permute-start | bytes 1179656 | tf_op jit(solution)/shard_map/ppermute | solution.py:43
  165.8 2.4 collective-permute-start.23
  165.9 3.9 %collective-permute-start.16 = (bf16[8,192,128]{2,1,0:T(8,128)(2,1)S(1)}, bf16[8,192,128]{2,1,0:T(8,128)(2,1)S(1)}, u32[]{:S(2)}, u32[]{:S(2)}) collective-permute-start(bf16[8,192,128]{2,1,0:T(8,128)(2,1)S(1)} %all-to-all-done.2.refs_0_), channel_id=1, source_target_pairs={{0,1},{1,0},{2,3},{3,2},{4,5},{5,4},{6,7},{7,6},{8,9},{9,8},{10,11... | collective-permute-start | bytes 1179656 | tf_op jit(solution)/shard_map/ppermute | solution.py:43
  166.4 3.5 collective-permute-start.22
  168.3 15.8 %collective-permute-start.24 = (bf16[8,192,128]{2,1,0:T(8,128)(2,1)S(1)}, bf16[8,192,128]{2,1,0:T(8,128)(2,1)S(1)}, u32[]{:S(2)}, u32[]{:S(2)}) collective-permute-start(bf16[8,192,128]{2,1,0:T(8,128)(2,1)S(1)} %fusion.90), channel_id=1, source_target_pairs={{0,2},{1,3},{2,0},{3,1},{4,6},{5,7},{6,4},{7,5},{8,10},{9,11},{10,... | collective-permute-start | bytes 1179656 | tf_op jit(solution)/shard_map/ppermute | solution.py:43
  184.0 5.2 %collective-permute-start.25 = (bf16[2,8,192,128]{3,2,1,0:T(8,128)(2,1)}, bf16[2,8,192,128]{3,2,1,0:T(8,128)(2,1)S(1)}, u32[]{:S(2)}, u32[]{:S(2)}) collective-permute-start(bf16[2,8,192,128]{3,2,1,0:T(8,128)(2,1)} %get-tuple-element.147), channel_id=1, source_target_pairs={{0,1},{1,0},{2,3},{3,2},{4,5},{5,4},{6,7},{7,6},{8,9},{9,8},{10,11... | collective-permute-start | bytes 2359304 | tf_op jit(solution)/shard_map/ppermute | solution.py:43
  184.9 23.9 %all-to-all-start.3 = ((bf16[8,192,128]{2,1,0:T(8,128)(2,1)}), bf16[8,192,128]{2,1,0:T(8,128)(2,1)}, u32[]{:S(2)}, u32[]{:S(2)}) async-start(bf16[8,192,128]{2,1,0:T(8,128)(2,1)} %fusion.86), calls=%async_computation.3 | async-start | bytes 786432 | tf_op jit(solution)/shard_map/all_to_all | solution.py:1046
  190.3 18.6 %collective-permute-start.26 = (bf16[8,192,128]{2,1,0:T(8,128)(2,1)}, bf16[8,192,128]{2,1,0:T(8,128)(2,1)}, u32[]{:S(2)}, u32[]{:S(2)}) collective-permute-start(bf16[8,192,128]{2,1,0:T(8,128)(2,1)} %fusion.91), channel_id=1, source_target_pairs={{0,2},{1,3},{2,0},{3,1},{4,6},{5,7},{6,4},{7,5},{8,10},{9,11},{10,... | collective-permute-start | bytes 1179656 | tf_op jit(solution)/shard_map/ppermute | solution.py:43
  208.8 8.5 %collective-permute-start.27 = (bf16[2,8,192,256]{3,2,1,0:T(8,128)(2,1)}, bf16[2,8,192,256]{3,2,1,0:T(8,128)(2,1)}, u32[]{:S(2)}, u32[]{:S(2)}) collective-permute-start(bf16[2,8,192,256]{3,2,1,0:T(8,128)(2,1)} %copy-done.27), channel_id=1, source_target_pairs={{0,1},{1,0},{2,3},{3,2},{4,5},{5,4},{6,7},{7,6},{8,9},{9,8},{10,11... | collective-permute-start | bytes 4718600 | tf_op jit(solution)/shard_map/ppermute | solution.py:43
  211.3 18.1 %all-to-all-start.4 = ((bf16[8,192,128]{2,1,0:T(8,128)(2,1)}), bf16[8,192,128]{2,1,0:T(8,128)(2,1)S(1)}, u32[]{:S(2)}, u32[]{:S(2)}) async-start(bf16[8,192,128]{2,1,0:T(8,128)(2,1)} %fusion.85), calls=%async_computation.4 | async-start | bytes 786432 | tf_op jit(solution)/shard_map/all_to_all | solution.py:1046
  219.7 28.1 %collective-permute-start.28 = (bf16[8,192,256]{2,1,0:T(8,128)(2,1)}, bf16[8,192,256]{2,1,0:T(8,128)(2,1)}, u32[]{:S(2)}, u32[]{:S(2)}) collective-permute-start(bf16[8,192,256]{2,1,0:T(8,128)(2,1)} %fusion.81), channel_id=1, source_target_pairs={{0,2},{1,3},{2,0},{3,1},{4,6},{5,7},{6,4},{7,5},{8,10},{9,11},{10,... | collective-permute-start | bytes 2359304 | tf_op jit(solution)/shard_map/ppermute | solution.py:43
  231.8 16.1 %collective-permute-start.29 = (bf16[4,192,256]{2,1,0:T(8,128)(2,1)S(1)}, bf16[4,192,256]{2,1,0:T(8,128)(2,1)S(1)}, u32[]{:S(2)}, u32[]{:S(2)}) collective-permute-start(bf16[4,192,256]{2,1,0:T(8,128)(2,1)S(1)} %fusion.47.refs_0_), channel_id=1, source_target_pairs={{0,2},{1,3},{2,0},{3,1},{4,6},{5,7},{6,4},{7,5},{8,10},{9,11},{10,... | collective-permute-start | bytes 1179656 | tf_op jit(solution)/shard_map/ppermute | solution.py:43
  250.5 41.7 %all-to-all-start.5 = ((bf16[8,192,256]{2,1,0:T(8,128)(2,1)}), bf16[8,192,256]{2,1,0:T(8,128)(2,1)}, u32[]{:S(2)}, u32[]{:S(2)}) async-start(bf16[8,192,256]{2,1,0:T(8,128)(2,1)} %fusion.19), calls=%async_computation.5 | async-start | bytes 1572864 | tf_op jit(solution)/shard_map/all_to_all | solution.py:1046
  307.7 3.1 collective-permute-start.33
  307.8 5.0 %collective-permute-start.32 = (bf16[2,768,256]{2,1,0:T(8,128)(2,1)}, bf16[2,768,256]{2,1,0:T(8,128)(2,1)}, u32[]{:S(2)}, u32[]{:S(2)}) collective-permute-start(bf16[2,768,256]{2,1,0:T(8,128)(2,1)} %get-tuple-element.179), channel_id=1, source_target_pairs={{0,1},{1,0},{2,3},{3,2},{4,5},{5,4},{6,7},{7,6},{8,9},{9,8},{10,11... | collective-permute-start | bytes 2359304 | tf_op jit(solution)/shard_map/ppermute | solution.py:43
  309.7 16.3 %collective-permute-start.35 = (bf16[4,96,768]{2,1,0:T(8,128)(2,1)}, bf16[4,96,768]{2,1,0:T(8,128)(2,1)}, u32[]{:S(2)}, u32[]{:S(2)}) collective-permute-start(bf16[4,96,768]{2,1,0:T(8,128)(2,1)} %get-tuple-element.185), channel_id=1, source_target_pairs={{0,4},{4,0},{1,5},{5,1},{2,6},{6,2},{3,7},{7,3},{8,12},{12,8},{9,1... | collective-permute-start | bytes 1769480 | tf_op jit(solution)/shard_map/ppermute | solution.py:43
  314.9 11.1 %collective-permute-start.36 = (f32[8064]{0:T(1024)S(1)}, f32[8064]{0:T(1024)S(1)}, u32[]{:S(2)}, u32[]{:S(2)}) collective-permute-start(f32[8064]{0:T(1024)S(1)} %pad_maximum_fusion.15), channel_id=1, source_target_pairs={{0,4},{4,0},{1,5},{5,1},{2,6},{6,2},{3,7},{7,3},{8,12},{12,8},{9,1... | collective-permute-start | bytes 96776 | tf_op jit(solution)/shard_map/ppermute | solution.py:43
  316.9 10.8 %collective-permute-start.34 = (bf16[768,256]{1,0:T(8,128)(2,1)}, bf16[768,256]{1,0:T(8,128)(2,1)S(1)}, u32[]{:S(2)}, u32[]{:S(2)}) collective-permute-start(bf16[768,256]{1,0:T(8,128)(2,1)} %fusion.92), channel_id=1, source_target_pairs={{0,2},{1,3},{2,0},{3,1},{4,6},{5,7},{6,4},{7,5},{8,10},{9,11},{10,... | collective-permute-start | bytes 1179656 | tf_op jit(solution)/shard_map/ppermute | solution.py:43
  328.5 6.5 %collective-permute-start.42 = (f32[8064]{0:T(1024)S(1)}, f32[8064]{0:T(1024)S(1)}, u32[]{:S(2)}, u32[]{:S(2)}) collective-permute-start(f32[8064]{0:T(1024)S(1)} %fusion.128), channel_id=1, source_target_pairs={{0,8},{8,0},{16,24},{24,16},{1,9},{9,1},{17,25},{25,17},{2,10},{10... | collective-permute-start | bytes 96776 | tf_op jit(solution)/shard_map/ppermute | solution.py:43
  329.5 32.9 %all-to-all-start.6 = ((bf16[4,192,256]{2,1,0:T(8,128)(2,1)}), bf16[4,192,256]{2,1,0:T(8,128)(2,1)S(1)}, u32[]{:S(2)}, u32[]{:S(2)}) async-start(bf16[4,192,256]{2,1,0:T(8,128)(2,1)} %bitcast.301), calls=%async_computation.6 | async-start | bytes 786432 | tf_op jit(solution)/shard_map/all_to_all | solution.py:1252
  333.0 29.5 %collective-permute-start.37 = (bf16[768,256]{1,0:T(8,128)(2,1)}, bf16[768,256]{1,0:T(8,128)(2,1)}, u32[]{:S(2)}, u32[]{:S(2)}) collective-permute-start(bf16[768,256]{1,0:T(8,128)(2,1)} %fusion.93), channel_id=1, source_target_pairs={{0,2},{1,3},{2,0},{3,1},{4,6},{5,7},{6,4},{7,5},{8,10},{9,11},{10,... | collective-permute-start | bytes 1179656 | tf_op jit(solution)/shard_map/ppermute | solution.py:43
  335.0 4.9 %collective-permute-start.43 = (f32[8064]{0:T(1024)S(1)}, f32[8064]{0:T(1024)S(1)}, u32[]{:S(2)}, u32[]{:S(2)}) collective-permute-start(f32[8064]{0:T(1024)S(1)} %add.2953), channel_id=1, source_target_pairs={{0,16},{8,24},{16,0},{24,8},{1,17},{9,25},{17,1},{25,9},{2,18},{10... | collective-permute-start | bytes 96776 | tf_op jit(solution)/shard_map/ppermute | solution.py:43
  337.1 25.4 %collective-permute-start.38 = (bf16[768,256]{1,0:T(8,128)(2,1)}, bf16[768,256]{1,0:T(8,128)(2,1)}, u32[]{:S(2)}, u32[]{:S(2)}) collective-permute-start(bf16[768,256]{1,0:T(8,128)(2,1)} %fusion.84), channel_id=1, source_target_pairs={{0,4},{4,0},{1,5},{5,1},{2,6},{6,2},{3,7},{7,3},{8,12},{12,8},{9,1... | collective-permute-start | bytes 1179656 | tf_op jit(solution)/shard_map/ppermute | solution.py:43
  342.2 7.3 %collective-permute-start.45 = (f32[8064]{0:T(1024)S(1)}, f32[8064]{0:T(1024)S(1)}, u32[]{:S(2)}, u32[]{:S(2)}) collective-permute-start(f32[8064]{0:T(1024)S(1)} %add.2955), channel_id=1, source_target_pairs={{0,2},{1,3},{2,0},{3,1},{4,6},{5,7},{6,4},{7,5},{8,10},{9,11},{10,... | collective-permute-start | bytes 96776 | tf_op jit(solution)/shard_map/ppermute | solution.py:43
  342.4 9.1 %collective-permute-start.39 = (bf16[96,768]{1,0:T(8,128)(2,1)S(1)}, bf16[96,768]{1,0:T(8,128)(2,1)S(1)}, u32[]{:S(2)}, u32[]{:S(2)}) collective-permute-start(bf16[96,768]{1,0:T(8,128)(2,1)S(1)} %get-tuple-element.292), channel_id=1, source_target_pairs={{0,8},{8,0},{16,24},{24,16},{1,9},{9,1},{17,25},{25,17},{2,10},{10... | collective-permute-start | bytes 442376 | tf_op jit(solution)/shard_map/ppermute | solution.py:43
  344.5 7.8 %collective-permute-start.41 = (bf16[96,768]{1,0:T(8,128)(2,1)S(1)}, bf16[96,768]{1,0:T(8,128)(2,1)S(1)}, u32[]{:S(2)}, u32[]{:S(2)}) collective-permute-start(bf16[96,768]{1,0:T(8,128)(2,1)S(1)} %get-tuple-element.293), channel_id=1, source_target_pairs={{0,24},{8,16},{16,8},{24,0},{1,25},{9,17},{17,9},{25,1},{2,26},{10... | collective-permute-start | bytes 442376 | tf_op jit(solution)/shard_map/ppermute | solution.py:43
  349.5 10.3 %collective-permute-start.40 = (bf16[96,768]{1,0:T(8,128)(2,1)S(1)}, bf16[96,768]{1,0:T(8,128)(2,1)}, u32[]{:S(2)}, u32[]{:S(2)}) collective-permute-start(bf16[96,768]{1,0:T(8,128)(2,1)S(1)} %get-tuple-element.294), channel_id=1, source_target_pairs={{0,16},{8,24},{16,0},{24,8},{1,17},{9,25},{17,1},{25,9},{2,18},{10... | collective-permute-start | bytes 442376 | tf_op jit(solution)/shard_map/ppermute | solution.py:43
  (102 other events, 790.0 us)
where the time goes:
time: 370 us; the launch traced here: 366 us
  Pallas kernels  101 us (27%)
  waiting for transfers between devices  74.9 us (20%)
  starting transfers between devices  60.4 us (16%)
  other arithmetic  49.6 us (13%)
  local copies, waits for them, and re-layouts  44.8 us (12%)
  blocking collectives  16.3 us (4%)
  matrix products  16.2 us (4%)
    ppermute x46, waiting for transfers between devices, swap(): return lax.ppermute(values, axis, [(i, i ^ bit) for i in range(count)])  62.3 us
    unnamed x202, local copies, waits for them, and re-layouts  33.5 us
    ppermute x46, starting transfers between devices, swap(): return lax.ppermute(values, axis, [(i, i ^ bit) for i in range(count)])  31.9 us
    pallas_call x1, Pallas kernels, attend_back(): pl.pallas_call(attend_back_kernel, grid=(1,), out_shape=shapes, in_specs=...  26.3 us
    all_to_all x5, starting transfers between devices, exchange(): lax.all_to_all(values, ('dp', 'seq'), split_axis=0, concat_axis=0, tiled=...  25 us
    pallas_call x2, Pallas kernels, run_expert(): pl.pallas_call(functools.partial(expert_kernel, parts), grid=(steps // ch...  24.6 us
    pallas_call x1, Pallas kernels, attend(): pl.pallas_call(attend_kernel, grid=(1,), out_shape=shapes, in_specs=[pl.B...  17.9 us
    all_to_all x1, blocking collectives, exchange(): lax.all_to_all(values, ('dp', 'seq'), split_axis=0, concat_axis=0, tiled=...  16.3 us
  transfers between devices with their start and end apart: 52, of which 19 were waited for; matrix products, arithmetic and copies ran while one was open for 22% of the time, Pallas kernels for 23%

commit v1 on v0

--- a/solution.py
+++ b/solution.py
@@ -17,7 +17,7 @@
 MASKED = -1e30
 LOWEST = -1e29
 EXTRA = 16
-VMEM_BYTES = 48 * 1024 * 1024
+VMEM_BYTES = 60 * 1024 * 1024
 GELU_A = math.sqrt(2.0 / math.pi)
 GELU_B = 0.044715
 BF16 = jnp.bfloat16
@@ -94,48 +94,37 @@
     return counted + jnp.where(relative > 0, half_count, 0).astype(jnp.int32)
 
 
-def near_buckets(half_count):
-    shape = (3, HALF, HALF)
-    relative = (
-        (lax.broadcasted_iota(jnp.int32, shape, 0) - 1) * HALF
-        + lax.broadcasted_iota(jnp.int32, shape, 1)
-        - lax.broadcasted_iota(jnp.int32, shape, 2)
-    )
-    return bucket_of(relative, half_count)
-
-
-def bias_tiles(position_bias):
-    bucket_count, heads = position_bias.shape
+KINDS = ((0, 0, 0, 0), (0, 0, 1, 0), (2, 1, 3, 2), (4, 3, 4, 4), (4, 4, 4, 4))
+
+
+def near_tiles(table_ref, near_ref):
+    heads = near_ref.shape[0]
+    bucket_count = table_ref.shape[0] // heads
     half_count = bucket_count // 2
-    grid = near_buckets(half_count)
-    near = jnp.zeros((heads, 3, HALF, HALF), F32)
-    for bucket_index in range(bucket_count):
-        near = near + jnp.where(
-            (grid == bucket_index)[None], position_bias[bucket_index][:, None, None, None], 0.0
-        )
-    before, same, after = near[:, 0], near[:, 1], near[:, 2]
-    far_before = jnp.broadcast_to(
-        position_bias[half_count - 1][:, None, None], (heads, HALF, HALF)
-    )
-    far_after = jnp.broadcast_to(
-        position_bias[bucket_count - 1][:, None, None], (heads, HALF, HALF)
-    )
-
-    def square(a, b, c, d):
-        return jnp.concatenate(
-            [jnp.concatenate([a, b], axis=2), jnp.concatenate([c, d], axis=2)], axis=1
-        )
-
-    tiles = jnp.stack(
-        [
-            square(far_before, far_before, far_before, far_before),
-            square(far_before, far_before, before, far_before),
-            square(same, before, after, same),
-            square(far_after, after, far_after, far_after),
-            square(far_after, far_after, far_after, far_after),
-        ]
-    )
-    return tiles * LOG2E
+    offset = lax.broadcasted_iota(jnp.int32, (HALF, HALF), 0) - lax.broadcasted_iota(
+        jnp.int32, (HALF, HALF), 1
+    )
+    near_of = (range(1, half_count), range(bucket_count), range(half_count + 1, bucket_count))
+    for shift, buckets in enumerate(near_of):
+        grid = bucket_of(offset + (shift - 1) * HALF, half_count)
+        for h in range(heads):
+            total = jnp.zeros((HALF, HALF), F32)
+            for bucket_index in buckets:
+                value = table_ref[bucket_index * heads + h] * LOG2E
+                total = jnp.where(grid == bucket_index, value, total)
+            near_ref[h, 1 + shift] = total
+    for h in range(heads):
+        for kind, bucket_index in ((0, half_count - 1), (4, bucket_count - 1)):
+            value = table_ref[bucket_index * heads + h] * LOG2E
+            near_ref[h, kind] = jnp.full((HALF, HALF), value, F32)
+
+
+def fill_tiles(near_ref, bias_ref):
+    for kind, blocks in enumerate(KINDS):
+        for h in range(near_ref.shape[0]):
+            for place, block in enumerate(blocks):
+                row, column = place // 2 * HALF, place % 2 * HALF
+                bias_ref[kind, h, row : row + HALF, column : column + HALF] = near_ref[h, block]
 
 
 def span_of(meta_ref, query_tile, key_tiles):
@@ -181,7 +170,7 @@
     meta_ref,
     q_ref,
     kv_ref,
-    bias_ref,
+    near_ref,
     weight_ref,
     exact_ref,
     out_ref,
@@ -191,9 +180,11 @@
     key_ref,
     query_ref,
     sum_ref,
+    bias_ref,
 ):
     key_tiles = kv_ref.shape[0]
-    heads = bias_ref.shape[1]
+    heads = near_ref.shape[0]
+    fill_tiles(near_ref, bias_ref)
     size = q_ref.shape[1] // heads
 
     def turn(j, carry):
@@ -271,10 +262,10 @@
     return (0,) * dimensions
 
 
-def attend(meta, queries, keys_values, bias, out_blocks):
+def attend(meta, queries, keys_values, near, out_blocks):
     query_tiles, width, _ = queries.shape
     key_tiles = keys_values.shape[0]
-    heads = bias.shape[1]
+    heads = near.shape[0]
     parts, share, _ = out_blocks.shape
     blocks = jax.ShapeDtypeStruct((parts // 2, query_tiles, share, TILE), BF16)
     shapes = (
@@ -284,7 +275,7 @@
         blocks,
         blocks,
     )
-    operands = (queries, keys_values, bias, out_blocks)
+    operands = (queries, keys_values, near, out_blocks)
     return pl.pallas_call(
         attend_kernel,
         grid=(1,),
@@ -295,6 +286,7 @@
             pltpu.VMEM((key_tiles, heads, TILE, width // heads + EXTRA), BF16),
             pltpu.VMEM((heads, width // heads + EXTRA, TILE), BF16),
             pltpu.VMEM((heads, width // heads + EXTRA, TILE), F32),
+            pltpu.VMEM((len(KINDS), heads, TILE, TILE), F32),
         ],
         compiler_params=pltpu.CompilerParams(vmem_limit_bytes=VMEM_BYTES),
         cost_estimate=estimate(queries, key_tiles, 2),
@@ -344,7 +336,7 @@
     meta_ref,
     q_ref,
     kv_ref,
-    bias_ref,
+    near_ref,
     weight_ref,
     exact_ref,
     log_ref,
@@ -363,9 +355,11 @@
         grad_ref,
         dq_sum,
         dkv_sum,
+        bias_ref,
     ) = refs[parts:]
     key_tiles = kv_ref.shape[0]
-    heads = bias_ref.shape[1]
+    heads = near_ref.shape[0]
+    fill_tiles(near_ref, bias_ref)
     size = q_ref.shape[1] // heads
 
     row = lax.broadcasted_iota(jnp.int32, (EXTRA, TILE), 0)
@@ -438,16 +432,16 @@
     bucket_rows(tiles_ref, rows_ref)
 
 
-def attend_back(meta, queries, keys_values, bias, out_blocks, exact, logs, branch, buckets):
+def attend_back(meta, queries, keys_values, near, out_blocks, exact, logs, branch, buckets):
     key_tiles = keys_values.shape[0]
-    heads = bias.shape[1]
+    heads = near.shape[0]
     size = queries.shape[1] // heads
     shapes = (
         jax.ShapeDtypeStruct(queries.shape, BF16),
         jax.ShapeDtypeStruct(keys_values.shape, BF16),
         jax.ShapeDtypeStruct((heads, buckets, HALF), F32),
     )
-    operands = (queries, keys_values, bias, out_blocks, exact, logs, *branch)
+    operands = (queries, keys_values, near, out_blocks, exact, logs, *branch)
     return pl.pallas_call(
         attend_back_kernel,
         grid=(1,),
@@ -455,13 +449,14 @@
         in_specs=[pl.BlockSpec(memory_space=pltpu.SMEM)] + whole_specs(operands),
         out_specs=tuple(whole_specs(shapes)),
         scratch_shapes=[
-            pltpu.VMEM(bias.shape, F32),
+            pltpu.VMEM((len(KINDS), heads, TILE, TILE), F32),
             pltpu.VMEM((key_tiles, heads, TILE, size + EXTRA), BF16),
             pltpu.VMEM((key_tiles, heads, TILE, size + EXTRA), BF16),
             pltpu.VMEM((heads, size + EXTRA, TILE), BF16),
             pltpu.VMEM((heads, size + EXTRA, TILE), BF16),
             pltpu.VMEM(queries.shape[1:], F32),
             pltpu.VMEM(keys_values.shape, F32),
+            pltpu.VMEM((len(KINDS), heads, TILE, TILE), F32),
         ],
         compiler_params=pltpu.CompilerParams(vmem_limit_bytes=VMEM_BYTES),
         cost_estimate=estimate(queries, key_tiles, 5),
@@ -469,7 +464,7 @@
     )(meta, *operands)
 
 
-def project_kernel(piece_count, weight_count, tiles, share, own_ref, *refs):
+def project_kernel(piece_count, weight_count, tiles, share, own_ref, table_ref, *refs):
     piece_refs = refs[:piece_count]
     weight_refs = refs[piece_count : piece_count + weight_count]
     gain_ref = refs[piece_count + weight_count]
@@ -482,6 +477,7 @@
         in_ref,
         out_ref,
         out_t_ref,
+        near_ref,
         block_ref,
         turned_ref,
     ) = refs[piece_count + weight_count + 1 :]
@@ -508,6 +504,7 @@
         out_ref[k] = block
         out_t_ref[k] = block.T
     key_tiles = kv_ref.shape[0]
+    near_tiles(table_ref, near_ref)
     early = jnp.zeros((1, TILE), F32)
     late = jnp.zeros((1, TILE), F32)
     gain = gain_ref[...]
@@ -543,7 +540,7 @@
         meta_ref[3 + key_tiles + i] = seq_place * tiles + shift
 
 
-def project(own, pieces, weight_pieces, gain, tiles, key_tiles, share):
+def project(own, table, pieces, weight_pieces, gain, tiles, key_tiles, share, heads):
     width = gain.shape[0]
     columns = weight_pieces[0].shape[1]
     head_cols = columns // 4
@@ -556,13 +553,14 @@
         jax.ShapeDtypeStruct((width, 3 * head_cols), BF16),
         jax.ShapeDtypeStruct((parts, share, head_cols), BF16),
         jax.ShapeDtypeStruct((parts, head_cols, share), BF16),
+        jax.ShapeDtypeStruct((heads, len(KINDS), HALF, HALF), F32),
     )
     operands = (*pieces, *weight_pieces, gain)
     return pl.pallas_call(
         functools.partial(project_kernel, len(pieces), len(weight_pieces), tiles, share),
         grid=(1,),
         out_shape=(jax.ShapeDtypeStruct((3 + key_tiles + tiles,), jnp.int32),) + shapes,
-        in_specs=[pl.BlockSpec(memory_space=pltpu.SMEM)] + whole_specs(operands),
+        in_specs=[pl.BlockSpec(memory_space=pltpu.SMEM)] * 2 + whole_specs(operands),
         out_specs=(pl.BlockSpec(memory_space=pltpu.SMEM),) + tuple(whole_specs(shapes)),
         scratch_shapes=[
             pltpu.VMEM((len(weight_pieces),) + weight_pieces[0].shape, BF16),
@@ -575,7 +573,7 @@
             transcendentals=0,
         ),
         name="project",
-    )(own, *operands)
+    )(own, table, *operands)
 
 
 def project_back_kernel(fast, parts, own_ref, dq_ref, dkv_ref, normed_ref, in_ref, attended_ref, *refs):
@@ -786,35 +784,41 @@
 
 
 def result_kernel(parts, own_ref, *refs):
-    chunks = (len(refs) - 11) // 4
-    sets = [refs[4 * c : 4 * c + 4] for c in range(chunks)]
-    (
-        grad_ref,
-        other_ref,
-        in_ref,
-        out_t_ref,
-        kept_ref,
-        sent_ref,
-        in_sum,
-        out_sum,
-        gain_sum,
-        result_ref,
-        full_ref,
-    ) = refs[4 * chunks :]
-
-    @pl.when(pl.program_id(0) == 0)
-    def _():
-        in_sum[...] = jnp.zeros_like(in_sum)
-        out_sum[...] = jnp.zeros_like(out_sum)
-
+    out_t_ref, kept_ref, sent_ref, result_ref = refs[-4:]
+    chunks = (len(refs) - 4) // 2
     own = own_ref[1]
     width = out_t_ref.shape[0]
     share = width // parts
     merged = kept_ref.shape[1]
     for c in range(chunks):
-        normed_ref, act_ref, pre_ref, gate_ref = sets[c]
-        gate, activated = gate_ref[0], act_ref[0]
-        columns = activated.shape[-1]
+        gate, activated = refs[2 * c + 1][0], refs[2 * c][0]
+        slots = activated.shape[-1] // merged
+        result = dot(out_t_ref[...], activated) * gate
+        result_ref[c] = result.astype(BF16).reshape(parts, share, -1)
+        for k in range(parts):
+            block = result_ref[c, own ^ k]
+            target = sent_ref if k & 1 else kept_ref
+            for m in range(merged):
+                target[k // 2, m, :, c * slots : (c + 1) * slots] = block[
+                    :, m * slots : (m + 1) * slots
+                ]
+
+
+def grads_kernel(parts, merged, own_ref, *refs):
+    grad_ref, other_ref, in_ref, in_sum, out_sum, gain_sum, full_ref = refs[-7:]
+    chunks = (len(refs) - 7) // 4
+
+    @pl.when(pl.program_id(0) == 0)
+    def _():
+        in_sum[...] = jnp.zeros_like(in_sum)
+        out_sum[...] = jnp.zeros_like(out_sum)
+
+    own = own_ref[1]
+    width = in_ref.shape[0]
+    for c in range(chunks):
+        normed_ref, act_ref, pre_ref, gate_ref = refs[4 * c : 4 * c + 4]
+        gate = gate_ref[0]
+        columns = gate.shape[-1]
         slots = columns // merged
         for k in range(parts):
             near = 2 * (k // 2) + ((own & 1) ^ (k & 1))
@@ -822,19 +826,10 @@
             full_ref[c, near] = jnp.concatenate(
                 [source[m, k // 2, :, c * slots : (c + 1) * slots] for m in range(merged)], axis=-1
             )
-        result = dot(out_t_ref[...], activated) * gate
-        result_ref[c] = result.astype(BF16).reshape(parts, share, columns)
-        for k in range(parts):
-            block = result_ref[c, own ^ k]
-            target = sent_ref if k & 1 else kept_ref
-            for m in range(merged):
-                target[k // 2, m, :, c * slots : (c + 1) * slots] = block[
-                    :, m * slots : (m + 1) * slots
-                ]
         normed = (normed_ref[0].astype(F32) * gate).astype(BF16)
         in_sum[...] += dot_rows(normed, pre_ref[0])
         scaled = (full_ref[c].reshape(width, columns).astype(F32) * gate).astype(BF16)
-        out_sum[...] += dot_rows(activated, scaled)
+        out_sum[...] += dot_rows(act_ref[0], scaled)
 
     @pl.when(pl.program_id(0) == pl.num_programs(0) - 1)
     def _():
@@ -895,25 +890,48 @@
     )(own, *states, *grads, *weights)
 
 
-def run_result(own, saved, grads, merged, weights):
+def run_result(own, saved, parts, merged, out_t):
+    chunks = len(saved)
+    steps, hidden, columns = saved[0][0].shape
+    width = out_t.shape[0]
+    share, half, slots = width // parts, parts // 2, columns // merged
+    deep = pl.BlockSpec((1, hidden, columns), lambda g: (g, 0, 0))
+    flat = pl.BlockSpec((1, 1, columns), lambda g: (g, 0, 0))
+    split = pl.BlockSpec((half, merged, share, slots * chunks), lambda g: (0, g, 0, 0))
+    total = jax.ShapeDtypeStruct((half, steps * merged, share, slots * chunks), BF16)
+    return pl.pallas_call(
+        functools.partial(result_kernel, parts),
+        grid=(steps,),
+        out_shape=(total, total),
+        in_specs=[pl.BlockSpec(memory_space=pltpu.SMEM)]
+        + [deep, flat] * chunks
+        + [fixed_spec(out_t.shape)],
+        out_specs=(split, split),
+        scratch_shapes=[pltpu.VMEM((chunks, parts, share, columns), BF16)],
+        compiler_params=pltpu.CompilerParams(vmem_limit_bytes=VMEM_BYTES),
+        cost_estimate=pl.CostEstimate(
+            flops=6 * chunks * steps * columns * width * hidden,
+            bytes_accessed=6 * chunks * steps * columns * width,
+            transcendentals=0,
+        ),
+        name="result",
+    )(own, *[array for arrays in saved for array in arrays], out_t)
+
+
+def run_grads(own, saved, grads, merged, weight):
     chunks = len(saved)
     steps, width, columns = saved[0][0].shape
     hidden = saved[0][1].shape[1]
     _, half, share, _ = grads[0].shape
     parts = 2 * half
-    slots = columns // merged
     wide = pl.BlockSpec((1, width, columns), lambda g: (g, 0, 0))
     deep = pl.BlockSpec((1, hidden, columns), lambda g: (g, 0, 0))
     flat = pl.BlockSpec((1, 1, columns), lambda g: (g, 0, 0))
-    grad_piece = pl.BlockSpec((merged, half, share, slots * chunks), lambda g: (g, 0, 0, 0))
-    split = pl.BlockSpec((half, merged, share, slots * chunks), lambda g: (0, g, 0, 0))
-    total = jax.ShapeDtypeStruct((half, steps * merged, share, slots * chunks), BF16)
+    grad_piece = pl.BlockSpec((merged,) + grads[0].shape[1:], lambda g: (g, 0, 0, 0))
     return pl.pallas_call(
-        functools.partial(result_kernel, parts),
+        functools.partial(grads_kernel, parts, merged),
         grid=(steps,),
         out_shape=(
-            total,
-            total,
             jax.ShapeDtypeStruct((width, hidden), F32),
             jax.ShapeDtypeStruct((hidden, width), F32),
             jax.ShapeDtypeStruct((width, 1), F32),
@@ -921,26 +939,21 @@
         in_specs=[pl.BlockSpec(memory_space=pltpu.SMEM)]
         + [wide, deep, deep, flat] * chunks
         + [grad_piece] * 2
-        + [fixed_spec(weight.shape) for weight in weights],
+        + [fixed_spec(weight.shape)],
         out_specs=(
-            split,
-            split,
             fixed_spec((width, hidden)),
             fixed_spec((hidden, width)),
             fixed_spec((width, 1)),
         ),
-        scratch_shapes=[
-            pltpu.VMEM((chunks, parts, share, columns), BF16),
-            pltpu.VMEM((chunks, parts, share, columns), BF16),
-        ],
+        scratch_shapes=[pltpu.VMEM((chunks, parts, share, columns), BF16)],
         compiler_params=pltpu.CompilerParams(vmem_limit_bytes=VMEM_BYTES),
         cost_estimate=pl.CostEstimate(
-            flops=16 * chunks * steps * columns * width * hidden,
-            bytes_accessed=12 * chunks * steps * columns * width,
+            flops=8 * chunks * steps * columns * width * hidden,
+            bytes_accessed=8 * chunks * steps * columns * width,
             transcendentals=0,
         ),
-        name="result",
-    )(own, *[array for arrays in saved for array in arrays], *grads, *weights)
+        name="grads",
+    )(own, *[array for arrays in saved for array in arrays], *grads, weight)
 
 
 def shards(
@@ -998,14 +1011,13 @@
         near_two = swap(own_rows, "tensor", 2)
         columns = [weight_piece] + [swap(weight_piece, "dp", k) for k in range(1, grid_count // 2)]
         grad_other = swap(grad_theirs, "tensor", 1)
-        far_rows, near_two, columns, grad_other, position_bias, expert_ids, in_plain, out_plain = (
+        far_rows, near_two, columns, grad_other, expert_ids, in_plain, out_plain = (
             lax.optimization_barrier(
                 (
                     far_rows,
                     near_two,
                     columns,
                     grad_other,
-                    position_bias,
                     expert_ids,
                     in_plain,
                     out_plain,
@@ -1026,7 +1038,6 @@
         row_pieces = [jnp.moveaxis(row_pieces, 2, 1).reshape(key_tiles, -1, TILE)]
         weight_pieces = [lax.all_gather(weight_piece, ("dp", "seq"), axis=0, tiled=True)]
 
-    bias = bias_tiles(position_bias)
     in_t, out_t = jnp.transpose(in_plain), jnp.transpose(out_plain)
     router_t = jnp.transpose(router_weight)
     in_joint = jnp.concatenate([in_plain, router_weight, router_weight], axis=1)
@@ -1069,7 +1080,6 @@
             far_two,
             far_columns,
             gain_one,
-            bias,
             in_t,
             in_joint,
             out_t,
@@ -1082,7 +1092,6 @@
                 far_two,
                 far_columns,
                 gain_one,
-                bias,
                 in_t,
                 in_joint,
                 out_t,
@@ -1105,13 +1114,31 @@
     grad_pair = swap(jnp.stack([grad_mine, grad_other]), "tensor", 2)
     grad_here = tiled([grad_mine, grad_other, grad_pair[0], grad_pair[1]])
     grad_buffer = einsum("nkdq,enqs->ekds", grad_here, onehot).astype(BF16)
-    meta, queries, keys_values, normed_tiles, input_share, in_flat, out_blocks, out_t_blocks = (
-        project(own, row_pieces, weight_pieces, gain_one, tiles, key_tiles, share)
+    (
+        meta,
+        queries,
+        keys_values,
+        normed_tiles,
+        input_share,
+        in_flat,
+        out_blocks,
+        out_t_blocks,
+        near,
+    ) = project(
+        own,
+        position_bias.reshape(-1),
+        row_pieces,
+        weight_pieces,
+        gain_one,
+        tiles,
+        key_tiles,
+        share,
+        heads,
     )
     queries, grad_buffer = lax.optimization_barrier((queries, grad_buffer))
     grad_arrived = joined(exchange(grad_buffer))
     exact, attended, logs, attn_even, attn_odd = attend(
-        meta, queries, keys_values, bias, out_blocks
+        meta, queries, keys_values, near, out_blocks
     )
     attn_share = sum_tensor(attn_even, attn_odd)
     state_share = (input_share.astype(F32) + attn_share).astype(BF16)
@@ -1145,22 +1172,29 @@
             sent, gathered[c + 1][2] = lax.optimization_barrier((sent, gathered[c + 1][2]))
         if c > 0:
             sent, crossed[c - 1] = lax.optimization_barrier((sent, crossed[c - 1]))
-        near, got, to_send = core_step(kept, sent)
+        stayed, got, to_send = core_step(kept, sent)
         if c + 1 == chunks:
             own_late, to_send = lax.optimization_barrier((own, to_send))
-        halves.append((near, got))
+        halves.append((stayed, got))
         crossed.append(swap(to_send, "tensor", 2))
         small = small + router_sum
     returned = [
         exchange(parted(chip_step(*halves[c], crossed[c]).astype(BF16)))
         for c in range(chunks - 1)
     ]
-    result_even, result_odd, grad_expert_in, grad_expert_out, in_gain = run_result(
-        own_late, saved, grads, merged, (expert_in[0], out_t)
+    result_even, result_odd = run_result(
+        own_late, [(arrays[1], arrays[3]) for arrays in saved], tensor_count, merged, out_t
     )
     tied = lax.optimization_barrier((result_odd, crossed[-1], *returned))
     result_odd, crossed[-1], returned = tied[0], tied[1], list(tied[2:])
     returned.append(exchange(parted(chip_step(*halves[-1], crossed[-1]).astype(BF16))))
+    result_near, result_got, result_sent = core_step(result_even, result_odd)
+    result_far = swap(result_sent, "tensor", 2)
+    own_late, result_sent = lax.optimization_barrier((own, result_sent))
+    grad_expert_in, grad_expert_out, in_gain = run_grads(
+        own_late, saved, grads, merged, expert_in[0]
+    )
+    in_gain, returned[-1] = lax.optimization_barrier((in_gain, returned[-1]))
     gain_part = in_gain[:, 0] + jnp.sum(small * router_t.astype(F32), axis=0)
     router_gains = jnp.concatenate([small, (gain_part / norm_gains[1])[None]])
     state_grad = lax.dynamic_index_in_dim(grad_here, tensor_place // 2, 1, keepdims=False)
@@ -1170,8 +1204,6 @@
             "eds,enqs->ndq", returned[c], onehot[..., c * slots : (c + 1) * slots]
         )
     state_grad = state_grad.astype(BF16)
-    result_near, result_got, result_sent = core_step(result_even, result_odd)
-    result_far = swap(result_sent, "tensor", 2)
 
     branch = [state_grad, swap(state_grad, "tensor", 1), swap(state_grad, "tensor", 2)]
     result_far, branch[2] = lax.optimization_barrier((result_far, branch[2]))
@@ -1179,7 +1211,7 @@
     result_total = chip_step(result_near, result_got, result_far).astype(BF16)
     result_back = exchange(parted(result_total))
     dq, dkv, bias_rows = attend_back(
-        meta, queries, keys_values, bias, out_t_blocks, exact, logs, branch, bucket_count
+        meta, queries, keys_values, near, out_t_blocks, exact, logs, branch, bucket_count
     )
     dq, dkv, bias_rows, result_back = lax.optimization_barrier((dq, dkv, bias_rows, result_back))
 
@@ -1209,12 +1241,13 @@
             (far_send, own_send, gain_part, result_back)
         )
         far_sent = swap(far_send, "tensor", 2)
-        small = sum_all(joined_small(), ("seq",))
+        small = sum_all(joined_small(), ("dp",))
         result_share = result_rows_of()
-        far_sent, weight_sent, small, result_share, own_send = lax.optimization_barrier(
-            (far_sent, weight_sent, small, result_share, own_send)
+        own_send, far_sent = lax.optimization_barrier((own_send, far_sent))
+        own_sent = swap(own_send, "tensor", 2)
+        far_sent, weight_sent, small, result_share, branch = lax.optimization_barrier(
+            (far_sent, weight_sent, small, result_share, branch)
         )
-        own_sent = swap(own_send, "tensor", 2)
         far_sum = chip_step(far_near, far_got, far_sent).astype(BF16)
         sums = [own_near, own_got, own_sent, swap(far_sum, "seq", 1)]
         weight_half = weight_even.astype(F32) + weight_sent.astype(F32)
@@ -1232,7 +1265,7 @@
             for k in range(tensor_count)
         ]
         sums = [sum_tensor(jnp.stack(blocks[0::2]), jnp.stack(blocks[1::2]))]
-        small = sum_all(joined_small(), ("seq",))
+        small = sum_all(joined_small(), ("dp",))
         result_share = result_rows_of()
         weight_grad = lax.psum_scatter(
             weight_part, ("dp", "seq"), scatter_dimension=0, tiled=True
@@ -1242,7 +1275,7 @@
     )
     grad_attn_out = jnp.transpose(weight_grad[:, 3 * head_cols :])
 
-    small = sum_all(small, ("dp", "tensor"))
+    small = sum_all(small, ("seq", "tensor"))
     first, second = experts * width, (experts + 1) * width
     grad_router = jnp.transpose(small[:first].reshape(experts, width))
     grad_gains = jnp.stack([small[second : second + width], small[first:second]])

time: 370 us -> 355 us (0.959)
  local copies, waits for them, and re-layouts: 44.8 us -> 23.3 us
  starting transfers between devices: 60.4 us -> 77.7 us
  other arithmetic: 49.6 us -> 33.2 us
  Pallas kernels: 101 us -> 107 us
    unnamed x202 -> x117, local copies, waits for them, and re-layouts: 33.5 us -> 11.5 us
    pallas_call x0 -> x1, Pallas kernels: none -> 11.8 us  [run_grads(): pl.pallas_call(functools.partial(grads_kernel, parts, merged), grid=(step...]
    all_to_all x5, starting transfers between devices: 25 us -> 35.2 us  [exchange(): lax.all_to_all(values, ('dp', 'seq'), split_axis=0, concat_axis=0, tiled=...]
    ppermute x46, starting transfers between devices: 31.9 us -> 39 us  [swap(): return lax.ppermute(values, axis, [(i, i ^ bit) for i in range(count)])]
    pallas_call x1, Pallas kernels: 13.7 us -> 6.78 us  [run_result(): pl.pallas_call(functools.partial(result_kernel, parts), grid=(steps,), ou...]
    mul x2 -> x0, other arithmetic: 4.43 us -> none  [the longest x1 4.42 us: bias_tiles(): return tiles * LOG2E]
    ppermute x46, waiting for transfers between devices: 62.3 us -> 66.6 us  [swap(): return lax.ppermute(values, axis, [(i, i ^ bit) for i in range(count)])]
    unnamed x5 -> x1, other arithmetic: 3.85 us -> 0.08 us
  transfers between devices with their start and end apart: 52 -> 52, of which waited for: 19 -> 19; matrix products, arithmetic and copies ran while one was open for 22% -> 17% of each run, Pallas kernels for 23% -> 24%
where the time goes in v1:
time: 355 us; the launch traced here: 354 us
  Pallas kernels  107 us (30%)
  starting transfers between devices  77.7 us (22%)
  waiting for transfers between devices  77.4 us (22%)
  other arithmetic  33.2 us (9%)
  local copies, waits for them, and re-layouts  23.3 us (7%)
  matrix products  16.9 us (5%)
  blocking collectives  16.5 us (5%)
    ppermute x46, waiting for transfers between devices, swap(): return lax.ppermute(values, axis, [(i, i ^ bit) for i in range(count)])  66.6 us
    ppermute x46, starting transfers between devices, swap(): return lax.ppermute(values, axis, [(i, i ^ bit) for i in range(count)])  39 us
    all_to_all x5, starting transfers between devices, exchange(): lax.all_to_all(values, ('dp', 'seq'), split_axis=0, concat_axis=0, tiled=...  35.2 us
    pallas_call x2, Pallas kernels, run_expert(): pl.pallas_call(functools.partial(expert_kernel, parts), grid=(steps // ch...  26.9 us
    pallas_call x1, Pallas kernels, attend_back(): pl.pallas_call(attend_back_kernel, grid=(1,), out_shape=shapes, in_specs=...  22.6 us
    dot_general x6, matrix products, einsum(): return jnp.einsum(formula, *operands, preferred_element_type=F32)  16.9 us
    all_to_all x1, blocking collectives, exchange(): lax.all_to_all(values, ('dp', 'seq'), split_axis=0, concat_axis=0, tiled=...  16.5 us
    pallas_call x1, Pallas kernels, attend(): pl.pallas_call(attend_kernel, grid=(1,), out_shape=shapes, in_specs=[pl.B...  15.6 us
  transfers between devices with their start and end apart: 52, of which 19 were waited for; matrix products, arithmetic and copies ran while one was open for 17% of the time, Pallas kernels for 24%

profile of v1, /device:TPU:0, one launch (start us, length us, event | category | flops | bytes accessed | tf_op | source)
XLA Modules:
  0.0 353.9 jit_solution(5784217977272617452)
XLA Ops:
  3.7 2.9 collective-permute-start.1
  9.1 3.6 %collective-permute-start.4 = (bf16[96,768]{1,0:T(8,128)(2,1)}, bf16[96,768]{1,0:T(8,128)(2,1)S(1)}, u32[]{:S(2)}, u32[]{:S(2)}) collective-permute-start(bf16[96,768]{1,0:T(8,128)(2,1)} %pad_maximum_fusion.7.refs_8_), channel_id=1, source_target_pairs={{0,24},{8,16},{16,8},{24,0},{1,25},{9,17},{17,9},{25,1},{2,26},{10... | collective-permute-start | bytes 442376 | tf_op jit(solution)/shard_map/ppermute | solution.py:43
  15.3 2.5 collective-permute-done.4.refs_14_
  18.5 6.3 %collective-permute-done.3.refs_12_ = bf16[96,768]{1,0:T(8,128)(2,1)S(1)} collective-permute-done((bf16[96,768]{1,0:T(8,128)(2,1)}, bf16[96,768]{1,0:T(8,128)(2,1)S(1)}, u32[]{:S(2)}, u32[]{:S(2)}) %collective-permute-start.3) | collective-permute-done | bytes 147488 | tf_op jit(solution)/shard_map/ppermute | solution.py:43
  25.4 2.3 reduce-window.6
  34.2 9.0 %collective-permute-done.6 = bf16[784,256]{1,0:T(8,128)(2,1)} collective-permute-done((bf16[784,256]{1,0:T(8,128)(2,1)}, bf16[784,256]{1,0:T(8,128)(2,1)}, u32[]{:S(2)}, u32[]{:S(2)}) %collective-permute-start.6) | collective-permute-done | bytes 401440 | tf_op jit(solution)/shard_map/ppermute | solution.py:43
  48.5 5.3 %collective-permute-done.13 = bf16[2,2,192,256]{3,2,1,0:T(8,128)(2,1)S(1)} collective-permute-done((bf16[2,2,192,256]{3,2,1,0:T(8,128)(2,1)S(1)}, bf16[2,2,192,256]{3,2,1,0:T(8,128)(2,1)S(1)}, u32[]{:S(2)}, u32[]{:S(2)}) %collective-permute-start.13) | collective-permute-done | bytes 393248 | tf_op jit(solution)/shard_map/ppermute | solution.py:43
  53.9 3.2 fusion.20
  57.9 8.9 %project.1 = (s32[15]{0:T(128)}, bf16[4,192,256]{2,1,0:T(8,128)(2,1)}, bf16[8,384,256]{2,1,0:T(8,128)(2,1)}, bf16[8,768,256]{2,1,0:T(8,128)(2,1)}, bf16[4,192,25...) custom-call(s32[4]{0:T(128)} %pad_add_fusion.own_ref, ...), custom_call_target="tpu_custom_call" | custom-call | flops 1811939328 | bytes 12582912 | tf_op jit(solution)/shard_map/project/pallas_call | solution.py:559
  66.9 4.9 %all-to-all-start = ((bf16[8,2,192,256]{3,2,1,0:T(8,128)(2,1)}), bf16[8,2,192,256]{3,2,1,0:T(8,128)(2,1)S(1)}, u32[]{:S(2)}, u32[]{:S(2)}) async-start(bf16[8,2,192,256]{3,2,1,0:T(8,128)(2,1)} %fusion.20), calls=%async_computation | async-start | bytes 3145728 | tf_op jit(solution)/shard_map/all_to_all | solution.py:1057
  71.7 15.6 %attend.1 = (f32[4,192,256]{2,1,0:T(8,128)}, bf16[4,192,256]{2,1,0:T(8,128)(2,1)}, f32[4,3,1,256]{3,2,1,0:T(1,128)}, bf16[2,4,192,256]{3,2,1,0:T(8,128)(2,1)}, bf16[2,4,192,256]{3,2,1,0:T(8,128)(2,1)}) custom-call(s32[15]{0:T(128)} %get-tuple-element.125.meta_ref, bf16[4,192,256]{2,1,0:T(8,128)(2,1)} %get-tuple-element.130.q_ref, ...), custom_call_target="tpu_custom_call" | custom-call | flops 1610612736 | bytes 16777216 | tf_op jit(solution)/shard_map/attend/pallas_call | solution.py:279
  87.6 2.2 collective-permute-done.14
  91.9 2.3 broadcast_compare_fusion
  94.2 8.4 %collective-permute-done.15 = bf16[4,192,256]{2,1,0:T(8,128)(2,1)S(1)} collective-permute-done((bf16[4,192,256]{2,1,0:T(8,128)(2,1)S(1)}, bf16[4,192,256]{2,1,0:T(8,128)(2,1)S(1)}, u32[]{:S(2)}, u32[]{:S(2)}) %collective-permute-start.15) | collective-permute-done | bytes 393248 | tf_op jit(solution)/shard_map/ppermute | solution.py:43
  104.4 5.0 %all-to-all-done.refs_4_.refs_8_ = bf16[8,2,192,256]{3,2,1,0:T(8,128)(2,1)S(1)} async-done(((bf16[8,2,192,256]{3,2,1,0:T(8,128)(2,1)}), bf16[8,2,192,256]{3,2,1,0:T(8,128)(2,1)S(1)}, u32[]{:S(2)}, u32[]{:S(2)}) %all-to-all-start) | async-done | bytes 1572896 | tf_op jit(solution)/shard_map/all_to_all | solution.py:1057
  109.4 3.4 fusion.62
  113.5 16.5 %all_to_all.35.refs_0_ = bf16[8,192,128]{2,1,0:T(8,128)(2,1)} all-to-all(bf16[8,192,128]{2,1,0:T(8,128)(2,1)S(1)} %fusion.59), channel_id=1, replica_groups=mesh['dp'=4,'seq'=2,'tensor'=4] {'dp','seq'}, dimensions={0} | all-to-all | bytes 786432 | tf_op jit(solution)/shard_map/all_to_all | solution.py:1057
  130.5 4.1 %all-to-all-start.2 = ((bf16[8,192,128]{2,1,0:T(8,128)(2,1)}), bf16[8,192,128]{2,1,0:T(8,128)(2,1)}, u32[]{:S(2)}, u32[]{:S(2)}) async-start(bf16[8,192,128]{2,1,0:T(8,128)(2,1)} %fusion.62), calls=%async_computation.2 | async-start | bytes 786432 | tf_op jit(solution)/shard_map/all_to_all | solution.py:1057
  134.7 5.8 %collective-permute-done.18.refs_2_ = bf16[8,192,128]{2,1,0:T(8,128)(2,1)} collective-permute-done((bf16[8,192,128]{2,1,0:T(8,128)(2,1)}, bf16[8,192,128]{2,1,0:T(8,128)(2,1)}, u32[]{:S(2)}, u32[]{:S(2)}) %collective-permute-start.18) | collective-permute-done | bytes 393248 | tf_op jit(solution)/shard_map/ppermute | solution.py:43
  143.5 2.1 all-to-all-done.2.refs_0_
  147.1 13.5 %expert.2 = (bf16[2,8,192,128]{3,2,1,0:T(8,128)(2,1)}, bf16[2,8,192,128]{3,2,1,0:T(8,128)(2,1)}, bf16[4,768,256]{2,1,0:T(8,128)(2,1)}, bf16[4,768,256]{2,1,0:T(8...) custom-call(s32[4]{0:T(128)} %pad_add_fusion.own_ref, ...), custom_call_target="tpu_custom_call" | custom-call | flops 9663676416 | bytes 12582912 | tf_op jit(solution)/shard_map/expert/pallas_call | solution.py:860
  161.3 2.4 collective-permute-done.23
  167.0 13.4 %expert.3 = (bf16[2,8,192,128]{3,2,1,0:T(8,128)(2,1)}, bf16[2,8,192,128]{3,2,1,0:T(8,128)(2,1)}, bf16[4,768,256]{2,1,0:T(8,128)(2,1)}, bf16[4,768,256]{2,1,0:T(8...) custom-call(s32[4]{0:T(128)} %pad_add_fusion.own_ref, ...), custom_call_target="tpu_custom_call" | custom-call | flops 9663676416 | bytes 12582912 | tf_op jit(solution)/shard_map/expert/pallas_call | solution.py:860
  180.5 2.0 fusion.73
  182.5 3.7 %all-to-all-start.3 = ((bf16[8,192,128]{2,1,0:T(8,128)(2,1)}), bf16[8,192,128]{2,1,0:T(8,128)(2,1)S(1)}, u32[]{:S(2)}, u32[]{:S(2)}) async-start(bf16[8,192,128]{2,1,0:T(8,128)(2,1)} %fusion.73), calls=%async_computation.3 | async-start | bytes 786432 | tf_op jit(solution)/shard_map/all_to_all | solution.py:1057
  187.9 6.8 %result.1 = (bf16[2,8,192,256]{3,2,1,0:T(8,128)(2,1)}, bf16[2,8,192,256]{3,2,1,0:T(8,128)(2,1)}) custom-call(s32[4]{0:T(128)} %pad_add_fusion.own_ref, bf16[4,768,256]{2,1,0:T(8,128)(2,1)} %get-tuple-element.158.refs_0_.refs_1_, f32[4,1,256]{2,1,0:T(1,128)} %get-tuple-element.159.refs_1_.refs_3_, bf16[4,768,256]{2,1,0:T(8,128)(2,1)} %get-tuple-element.160.refs_2_.refs_5_, ...), custom_call_target="tpu_custom_call" | custom-call | flops 7247757312 | bytes 9437184 | tf_op jit(solution)/shard_map/result/pallas_call | solution.py:902
  194.6 3.8 %all-to-all-done.3 = bf16[8,192,128]{2,1,0:T(8,128)(2,1)S(1)} async-done(((bf16[8,192,128]{2,1,0:T(8,128)(2,1)}), bf16[8,192,128]{2,1,0:T(8,128)(2,1)S(1)}, u32[]{:S(2)}, u32[]{:S(2)}) %all-to-all-start.3) | async-done | bytes 393248 | tf_op jit(solution)/shard_map/all_to_all | solution.py:1057
  200.5 2.2 fusion.72
  202.7 16.8 %all-to-all-start.4 = ((bf16[8,192,128]{2,1,0:T(8,128)(2,1)}), bf16[8,192,128]{2,1,0:T(8,128)(2,1)S(1)}, u32[]{:S(2)}, u32[]{:S(2)}) async-start(bf16[8,192,128]{2,1,0:T(8,128)(2,1)} %fusion.72), calls=%async_computation.4 | async-start | bytes 786432 | tf_op jit(solution)/shard_map/all_to_all | solution.py:1057
  219.5 3.2 fusion.41
  222.6 2.2 fusion.69
  226.4 11.8 %grads.1 = (f32[768,768]{1,0:T(8,128)}, f32[768,768]{1,0:T(8,128)}, f32[768,1]{1,0:T(8,128)}) custom-call(s32[4]{0:T(128)} %pad_add_fusion.own_ref, bf16[4,768,256]{2,1,0:T(8,128)(2,1)} %get-tuple-element.170.refs_0_, bf16[4,768,256]{2,1,0:T(8,128)(2,1)} %get-tuple-element.158.refs_0_.refs_1_, bf16[4,768,256]{2,1,0:T(8,128)(2,1)} %get-tuple-element.171.refs_2_, ...), custom_call_target="tpu_custom_call" | custom-call | flops 9663676416 | bytes 12582912 | tf_op jit(solution)/shard_map/grads/pallas_call | solution.py:931
  238.2 2.5 fusion.47.refs_0_
  241.3 11.2 %collective-permute-done.30.refs_2_ = bf16[4,192,256]{2,1,0:T(8,128)(2,1)S(1)} collective-permute-done((bf16[4,192,256]{2,1,0:T(8,128)(2,1)S(1)}, bf16[4,192,256]{2,1,0:T(8,128)(2,1)S(1)}, u32[]{:S(2)}, u32[]{:S(2)}) %collective-permute-start.30) | collective-permute-done | bytes 393248 | tf_op jit(solution)/shard_map/ppermute | solution.py:43
  252.5 2.5 fusion.19
  255.0 5.8 %all-to-all-start.5 = ((bf16[8,192,256]{2,1,0:T(8,128)(2,1)}), bf16[8,192,256]{2,1,0:T(8,128)(2,1)S(1)}, u32[]{:S(2)}, u32[]{:S(2)}) async-start(bf16[8,192,256]{2,1,0:T(8,128)(2,1)} %fusion.19), calls=%async_computation.5 | async-start | bytes 1572864 | tf_op jit(solution)/shard_map/all_to_all | solution.py:1057
  263.9 22.6 %attend_back.1 = (bf16[4,192,256]{2,1,0:T(8,128)(2,1)}, bf16[8,384,256]{2,1,0:T(8,128)(2,1)}, f32[3,32,128]{2,1,0:T(8,128)}) custom-call(s32[15]{0:T(128)} %get-tuple-element.125.meta_ref, bf16[4,192,256]{2,1,0:T(8,128)(2,1)} %get-tuple-element.130.q_ref, bf16[8,384,256]{2,1,0:T(8,128)(2,1)} %get-tuple-element.131.kv_ref, ...), custom_call_target="tpu_custom_call" | custom-call | flops 4026531840 | bytes 16777216 | tf_op jit(solution)/shard_map/attend_back/pallas_call | solution.py:445
  286.6 10.7 %project_back.1 = (bf16[2,768,256]{2,1,0:T(8,128)(2,1)}, bf16[2,768,256]{2,1,0:T(8,128)(2,1)}, bf16[2,768,256]{2,1,0:T(8,128)(2,1)}, bf16[2,768,256]{2,1,0:T(8,1...) custom-call(s32[4]{0:T(128)} %pad_add_fusion.own_ref, ...), custom_call_target="tpu_custom_call" | custom-call | flops 3623878656 | bytes 12582912 | tf_op jit(solution)/shard_map/project_back/pallas_call | solution.py:651
  298.5 2.0 collective-permute-start.35
  307.6 3.9 %fusion.65 = bf16[192,4,256]{2,0,1:T(8,128)(2,1)} fusion(s32[8,256]{1,0:T(8,128)S(1)} %multiply_add_fusion, s32[4,256]{1,0:T(4,128)S(1)} %bitcast.280, bf16[8,192,256]{2,1,0:T(8,128)(2,1)S(1)} %all-to-all-done.5, bf16[4,192,256]{2,1,0:T(8,128)(2,1)} %copy-done.29, bf16[2,4,192,256]{3,2,1,0:T(8,128)(2,1)} %copy-done.21, ...), kind=kOutput, calls=%fused_computation.39 | convolution fusion | flops 808779776 | bytes 2371584 | tf_op jit(solution)/shard_map/eds,enqs->ndq/dot_general | solution.py:38
  311.5 2.4 collective-permute-start.37
  317.6 3.5 all-to-all-start.6
  321.7 2.0 fusion.71
  328.6 2.6 collective-permute-start.42
  333.4 4.2 %collective-permute-done.45 = f32[8064]{0:T(1024)S(1)} collective-permute-done((f32[8064]{0:T(1024)S(1)}, f32[8064]{0:T(1024)S(1)}, u32[]{:S(2)}, u32[]{:S(2)}) %collective-permute-start.45) | collective-permute-done | bytes 32288 | tf_op jit(solution)/shard_map/ppermute | solution.py:43
  337.6 2.4 collective-permute-start.41
  341.9 5.3 %collective-permute-done.41 = bf16[96,768]{1,0:T(8,128)(2,1)S(1)} collective-permute-done((bf16[96,768]{1,0:T(8,128)(2,1)S(1)}, bf16[96,768]{1,0:T(8,128)(2,1)S(1)}, u32[]{:S(2)}, u32[]{:S(2)}) %collective-permute-start.41) | collective-permute-done | bytes 147488 | tf_op jit(solution)/shard_map/ppermute | solution.py:43
  349.8 3.9 %finish.1 = (f32[256,768]{1,0:T(8,128)}, f32[256,768]{1,0:T(8,128)}) custom-call(f32[256,768]{1,0:T(8,128)} %input_ref.1, f32[768,1]{1,0:T(8,128)} %copy.133.refs_16_.gain_ref, bf16[768,256]{1,0:T(8,128)(2,1)} %pad_maximum_fusion.5.branch_ref, bf16[768,256]{1,0:T(8,128)(2,1)} %bitcast.264, bf16[768,256]{1,0:T(8,128)(2,1)} %slice_bitcast_fusion.1.refs_0_, ...), custom_call_target="tpu_custom_call" | custom-call | tf_op jit(solution)/shard_map/finish/pallas_call | solution.py:689
  (268 shorter events, 68.8 us)
Async XLA Ops:
  3.7 21.6 %collective-permute-start.1 = (bf16[784,256]{1,0:T(8,128)(2,1)}, bf16[784,256]{1,0:T(8,128)(2,1)}, u32[]{:S(2)}, u32[]{:S(2)}) collective-permute-start(bf16[784,256]{1,0:T(8,128)(2,1)} %get-tuple-element.281), channel_id=1, source_target_pairs={{0,2},{1,3},{2,0},{3,1},{4,6},{5,7},{6,4},{7,5},{8,10},{9,11},{10,... | collective-permute-start | bytes 1204232 | tf_op jit(solution)/shard_map/ppermute | solution.py:43
  6.7 18.7 %collective-permute-start = (bf16[784,256]{1,0:T(8,128)(2,1)}, bf16[784,256]{1,0:T(8,128)(2,1)}, u32[]{:S(2)}, u32[]{:S(2)}) collective-permute-start(bf16[784,256]{1,0:T(8,128)(2,1)} %get-tuple-element.281), channel_id=1, source_target_pairs={{0,4},{4,0},{1,5},{5,1},{2,6},{6,2},{3,7},{7,3},{8,12},{12,8},{9,1... | collective-permute-start | bytes 1204232 | tf_op jit(solution)/shard_map/ppermute | solution.py:43
  9.1 8.8 %collective-permute-start.4 = (bf16[96,768]{1,0:T(8,128)(2,1)}, bf16[96,768]{1,0:T(8,128)(2,1)S(1)}, u32[]{:S(2)}, u32[]{:S(2)}) collective-permute-start(bf16[96,768]{1,0:T(8,128)(2,1)} %pad_maximum_fusion.7.refs_8_), channel_id=1, source_target_pairs={{0,24},{8,16},{16,8},{24,0},{1,25},{9,17},{17,9},{25,1},{2,26},{10... | collective-permute-start | bytes 442376 | tf_op jit(solution)/shard_map/ppermute | solution.py:43
  12.7 12.1 %collective-permute-start.3 = (bf16[96,768]{1,0:T(8,128)(2,1)}, bf16[96,768]{1,0:T(8,128)(2,1)S(1)}, u32[]{:S(2)}, u32[]{:S(2)}) collective-permute-start(bf16[96,768]{1,0:T(8,128)(2,1)} %pad_maximum_fusion.7.refs_8_), channel_id=1, source_target_pairs={{0,16},{8,24},{16,0},{24,8},{1,17},{9,25},{17,1},{25,9},{2,18},{10... | collective-permute-start | bytes 442376 | tf_op jit(solution)/shard_map/ppermute | solution.py:43
  12.7 12.6 %collective-permute-start.2 = (bf16[96,768]{1,0:T(8,128)(2,1)}, bf16[96,768]{1,0:T(8,128)(2,1)}, u32[]{:S(2)}, u32[]{:S(2)}) collective-permute-start(bf16[96,768]{1,0:T(8,128)(2,1)} %pad_maximum_fusion.7.refs_8_), channel_id=1, source_target_pairs={{0,8},{8,0},{16,24},{24,16},{1,9},{9,1},{17,25},{25,17},{2,10},{10... | collective-permute-start | bytes 442376 | tf_op jit(solution)/shard_map/ppermute | solution.py:43
  17.9 7.5 %collective-permute-start.5 = (bf16[2,192,256]{2,1,0:T(8,128)(2,1)S(1)}, bf16[2,192,256]{2,1,0:T(8,128)(2,1)S(1)}, u32[]{:S(2)}, u32[]{:S(2)}) collective-permute-start(bf16[2,192,256]{2,1,0:T(8,128)(2,1)S(1)} %get-tuple-element.283), channel_id=1, source_target_pairs={{0,1},{1,0},{2,3},{3,2},{4,5},{5,4},{6,7},{7,6},{8,9},{9,8},{10,11... | collective-permute-start | bytes 589832 | tf_op jit(solution)/shard_map/ppermute | solution.py:43
  24.8 32.3 %collective-permute-start.12 = (bf16[96,768]{1,0:T(8,128)(2,1)}, bf16[96,768]{1,0:T(8,128)(2,1)}, u32[]{:S(2)}, u32[]{:S(2)}) collective-permute-start(bf16[96,768]{1,0:T(8,128)(2,1)} %pad_maximum_fusion.7.refs_8_), channel_id=1, source_target_pairs={{0,4},{4,0},{1,5},{5,1},{2,6},{6,2},{3,7},{7,3},{8,12},{12,8},{9,1... | collective-permute-start | bytes 442376 | tf_op jit(solution)/shard_map/ppermute | solution.py:43
  25.3 31.8 %collective-permute-start.8 = (bf16[784,256]{1,0:T(8,128)(2,1)}, bf16[784,256]{1,0:T(8,128)(2,1)}, u32[]{:S(2)}, u32[]{:S(2)}) collective-permute-start(bf16[784,256]{1,0:T(8,128)(2,1)} %get-tuple-element.281), channel_id=1, source_target_pairs={{0,1},{1,0},{2,3},{3,2},{4,5},{5,4},{6,7},{7,6},{8,9},{9,8},{10,11... | collective-permute-start | bytes 1204232 | tf_op jit(solution)/shard_map/ppermute | solution.py:43
  29.9 13.3 %collective-permute-start.7 = (bf16[3,96,768]{2,1,0:T(8,128)(2,1)}, bf16[3,96,768]{2,1,0:T(8,128)(2,1)}, u32[]{:S(2)}, u32[]{:S(2)}) collective-permute-start(bf16[3,96,768]{2,1,0:T(8,128)(2,1)} %pad_maximum_fusion.3), channel_id=1, source_target_pairs={{0,4},{4,0},{1,5},{5,1},{2,6},{6,2},{3,7},{7,3},{8,12},{12,8},{9,1... | collective-permute-start | bytes 1327112 | tf_op jit(solution)/shard_map/ppermute | solution.py:43
  31.4 11.8 %collective-permute-start.6 = (bf16[784,256]{1,0:T(8,128)(2,1)}, bf16[784,256]{1,0:T(8,128)(2,1)}, u32[]{:S(2)}, u32[]{:S(2)}) collective-permute-start(bf16[784,256]{1,0:T(8,128)(2,1)} %collective-permute-done), channel_id=1, source_target_pairs={{0,2},{1,3},{2,0},{3,1},{4,6},{5,7},{6,4},{7,5},{8,10},{9,11},{10,... | collective-permute-start | bytes 1204232 | tf_op jit(solution)/shard_map/ppermute | solution.py:43
  43.3 10.5 %collective-permute-start.13 = (bf16[2,2,192,256]{3,2,1,0:T(8,128)(2,1)S(1)}, bf16[2,2,192,256]{3,2,1,0:T(8,128)(2,1)S(1)}, u32[]{:S(2)}, u32[]{:S(2)}) collective-permute-start(bf16[2,2,192,256]{3,2,1,0:T(8,128)(2,1)S(1)} %pad_maximum_fusion.4), channel_id=1, source_target_pairs={{0,2},{1,3},{2,0},{3,1},{4,6},{5,7},{6,4},{7,5},{8,10},{9,11},{10,... | collective-permute-start | bytes 1179656 | tf_op jit(solution)/shard_map/ppermute | solution.py:43
  45.2 11.9 %collective-permute-start.10 = (bf16[784,256]{1,0:T(8,128)(2,1)}, bf16[784,256]{1,0:T(8,128)(2,1)}, u32[]{:S(2)}, u32[]{:S(2)}) collective-permute-start(bf16[784,256]{1,0:T(8,128)(2,1)} %collective-permute-done), channel_id=1, source_target_pairs={{0,1},{1,0},{2,3},{3,2},{4,5},{5,4},{6,7},{7,6},{8,9},{9,8},{10,11... | collective-permute-start | bytes 1204232 | tf_op jit(solution)/shard_map/ppermute | solution.py:43
  45.2 11.9 %collective-permute-start.9 = (bf16[784,256]{1,0:T(8,128)(2,1)}, bf16[784,256]{1,0:T(8,128)(2,1)}, u32[]{:S(2)}, u32[]{:S(2)}) collective-permute-start(bf16[784,256]{1,0:T(8,128)(2,1)} %collective-permute-done.1), channel_id=1, source_target_pairs={{0,1},{1,0},{2,3},{3,2},{4,5},{5,4},{6,7},{7,6},{8,9},{9,8},{10,11... | collective-permute-start | bytes 1204232 | tf_op jit(solution)/shard_map/ppermute | solution.py:43
  53.8 3.4 collective-permute-start.11
  66.9 42.5 %all-to-all-start = ((bf16[8,2,192,256]{3,2,1,0:T(8,128)(2,1)}), bf16[8,2,192,256]{3,2,1,0:T(8,128)(2,1)S(1)}, u32[]{:S(2)}, u32[]{:S(2)}) async-start(bf16[8,2,192,256]{3,2,1,0:T(8,128)(2,1)} %fusion.20), calls=%async_computation | async-start | bytes 3145728 | tf_op jit(solution)/shard_map/all_to_all | solution.py:1057
  91.3 11.4 %collective-permute-start.15 = (bf16[4,192,256]{2,1,0:T(8,128)(2,1)S(1)}, bf16[4,192,256]{2,1,0:T(8,128)(2,1)S(1)}, u32[]{:S(2)}, u32[]{:S(2)}) collective-permute-start(bf16[4,192,256]{2,1,0:T(8,128)(2,1)S(1)} %fusion.76), channel_id=1, source_target_pairs={{0,2},{1,3},{2,0},{3,1},{4,6},{5,7},{6,4},{7,5},{8,10},{9,11},{10,... | collective-permute-start | bytes 1179656 | tf_op jit(solution)/shard_map/ppermute | solution.py:43
  109.4 37.8 %collective-permute-start.20 = (bf16[8,2,192,256]{3,2,1,0:T(8,128)(2,1)S(1)}, bf16[8,2,192,256]{3,2,1,0:T(8,128)(2,1)}, u32[]{:S(2)}, u32[]{:S(2)}) collective-permute-start(bf16[8,2,192,256]{3,2,1,0:T(8,128)(2,1)S(1)} %all-to-all-done.refs_4_.refs_8_), channel_id=1, source_target_pairs={{0,1},{1,0},{2,3},{3,2},{4,5},{5,4},{6,7},{7,6},{8,9},{9,8},{10,11... | collective-permute-start | bytes 4718600 | tf_op jit(solution)/shard_map/ppermute | solution.py:43
  129.9 10.5 %collective-permute-start.18 = (bf16[8,192,128]{2,1,0:T(8,128)(2,1)}, bf16[8,192,128]{2,1,0:T(8,128)(2,1)}, u32[]{:S(2)}, u32[]{:S(2)}) collective-permute-start(bf16[8,192,128]{2,1,0:T(8,128)(2,1)} %all_to_all.35.refs_0_), channel_id=1, source_target_pairs={{0,2},{1,3},{2,0},{3,1},{4,6},{5,7},{6,4},{7,5},{8,10},{9,11},{10,... | collective-permute-start | bytes 1179656 | tf_op jit(solution)/shard_map/ppermute | solution.py:43
  130.5 15.1 %all-to-all-start.2 = ((bf16[8,192,128]{2,1,0:T(8,128)(2,1)}), bf16[8,192,128]{2,1,0:T(8,128)(2,1)}, u32[]{:S(2)}, u32[]{:S(2)}) async-start(bf16[8,192,128]{2,1,0:T(8,128)(2,1)} %fusion.62), calls=%async_computation.2 | async-start | bytes 786432 | tf_op jit(solution)/shard_map/all_to_all | solution.py:1057
  134.6 12.5 %collective-permute-start.17 = (bf16[8,192,128]{2,1,0:T(8,128)(2,1)}, bf16[8,192,128]{2,1,0:T(8,128)(2,1)}, u32[]{:S(2)}, u32[]{:S(2)}) collective-permute-start(bf16[8,192,128]{2,1,0:T(8,128)(2,1)} %all_to_all.35.refs_0_), channel_id=1, source_target_pairs={{0,1},{1,0},{2,3},{3,2},{4,5},{5,4},{6,7},{7,6},{8,9},{9,8},{10,11... | collective-permute-start | bytes 1179656 | tf_op jit(solution)/shard_map/ppermute | solution.py:43
  140.5 6.6 %collective-permute-start.19 = (bf16[8,192,128]{2,1,0:T(8,128)(2,1)}, bf16[8,192,128]{2,1,0:T(8,128)(2,1)}, u32[]{:S(2)}, u32[]{:S(2)}) collective-permute-start(bf16[8,192,128]{2,1,0:T(8,128)(2,1)} %collective-permute-done.18.refs_2_), channel_id=1, source_target_pairs={{0,1},{1,0},{2,3},{3,2},{4,5},{5,4},{6,7},{7,6},{8,9},{9,8},{10,11... | collective-permute-start | bytes 1179656 | tf_op jit(solution)/shard_map/ppermute | solution.py:43
  145.6 15.0 %collective-permute-start.21 = (bf16[8,192,128]{2,1,0:T(8,128)(2,1)}, bf16[8,192,128]{2,1,0:T(8,128)(2,1)S(1)}, u32[]{:S(2)}, u32[]{:S(2)}) collective-permute-start(bf16[8,192,128]{2,1,0:T(8,128)(2,1)} %all-to-all-done.2.refs_0_), channel_id=1, source_target_pairs={{0,2},{1,3},{2,0},{3,1},{4,6},{5,7},{6,4},{7,5},{8,10},{9,11},{10,... | collective-permute-start | bytes 1179656 | tf_op jit(solution)/shard_map/ppermute | solution.py:43
  160.6 3.0 collective-permute-start.23
  160.7 4.8 %collective-permute-start.16 = (bf16[8,192,128]{2,1,0:T(8,128)(2,1)}, bf16[8,192,128]{2,1,0:T(8,128)(2,1)S(1)}, u32[]{:S(2)}, u32[]{:S(2)}) collective-permute-start(bf16[8,192,128]{2,1,0:T(8,128)(2,1)} %all-to-all-done.2.refs_0_), channel_id=1, source_target_pairs={{0,1},{1,0},{2,3},{3,2},{4,5},{5,4},{6,7},{7,6},{8,9},{9,8},{10,11... | collective-permute-start | bytes 1179656 | tf_op jit(solution)/shard_map/ppermute | solution.py:43
  161.2 4.3 %collective-permute-start.22 = (bf16[8,192,128]{2,1,0:T(8,128)(2,1)S(1)}, bf16[8,192,128]{2,1,0:T(8,128)(2,1)S(1)}, u32[]{:S(2)}, u32[]{:S(2)}) collective-permute-start(bf16[8,192,128]{2,1,0:T(8,128)(2,1)S(1)} %collective-permute-done.21.refs_2_), channel_id=1, source_target_pairs={{0,1},{1,0},{2,3},{3,2},{4,5},{5,4},{6,7},{7,6},{8,9},{9,8},{10,11... | collective-permute-start | bytes 1179656 | tf_op jit(solution)/shard_map/ppermute | solution.py:43
  164.9 15.6 %collective-permute-start.24 = (bf16[8,192,128]{2,1,0:T(8,128)(2,1)S(1)}, bf16[8,192,128]{2,1,0:T(8,128)(2,1)S(1)}, u32[]{:S(2)}, u32[]{:S(2)}) collective-permute-start(bf16[8,192,128]{2,1,0:T(8,128)(2,1)S(1)} %fusion.77), channel_id=1, source_target_pairs={{0,2},{1,3},{2,0},{3,1},{4,6},{5,7},{6,4},{7,5},{8,10},{9,11},{10,... | collective-permute-start | bytes 1179656 | tf_op jit(solution)/shard_map/ppermute | solution.py:43
  180.4 5.7 %collective-permute-start.25 = (bf16[2,8,192,128]{3,2,1,0:T(8,128)(2,1)}, bf16[2,8,192,128]{3,2,1,0:T(8,128)(2,1)S(1)}, u32[]{:S(2)}, u32[]{:S(2)}) collective-permute-start(bf16[2,8,192,128]{3,2,1,0:T(8,128)(2,1)} %get-tuple-element.156), channel_id=1, source_target_pairs={{0,1},{1,0},{2,3},{3,2},{4,5},{5,4},{6,7},{7,6},{8,9},{9,8},{10,11... | collective-permute-start | bytes 2359304 | tf_op jit(solution)/shard_map/ppermute | solution.py:43
  182.5 15.9 %all-to-all-start.3 = ((bf16[8,192,128]{2,1,0:T(8,128)(2,1)}), bf16[8,192,128]{2,1,0:T(8,128)(2,1)S(1)}, u32[]{:S(2)}, u32[]{:S(2)}) async-start(bf16[8,192,128]{2,1,0:T(8,128)(2,1)} %fusion.73), calls=%async_computation.3 | async-start | bytes 786432 | tf_op jit(solution)/shard_map/all_to_all | solution.py:1057
  186.3 12.1 %collective-permute-start.26 = (bf16[8,192,128]{2,1,0:T(8,128)(2,1)S(1)}, bf16[8,192,128]{2,1,0:T(8,128)(2,1)S(1)}, u32[]{:S(2)}, u32[]{:S(2)}) collective-permute-start(bf16[8,192,128]{2,1,0:T(8,128)(2,1)S(1)} %fusion.78), channel_id=1, source_target_pairs={{0,2},{1,3},{2,0},{3,1},{4,6},{5,7},{6,4},{7,5},{8,10},{9,11},{10,... | collective-permute-start | bytes 1179656 | tf_op jit(solution)/shard_map/ppermute | solution.py:43
  198.4 24.2 %collective-permute-start.27 = (bf16[2,8,192,256]{3,2,1,0:T(8,128)(2,1)}, bf16[2,8,192,256]{3,2,1,0:T(8,128)(2,1)}, u32[]{:S(2)}, u32[]{:S(2)}) collective-permute-start(bf16[2,8,192,256]{3,2,1,0:T(8,128)(2,1)} %get-tuple-element.168), channel_id=1, source_target_pairs={{0,1},{1,0},{2,3},{3,2},{4,5},{5,4},{6,7},{7,6},{8,9},{9,8},{10,11... | collective-permute-start | bytes 4718600 | tf_op jit(solution)/shard_map/ppermute | solution.py:43
  202.7 35.5 %all-to-all-start.4 = ((bf16[8,192,128]{2,1,0:T(8,128)(2,1)}), bf16[8,192,128]{2,1,0:T(8,128)(2,1)S(1)}, u32[]{:S(2)}, u32[]{:S(2)}) async-start(bf16[8,192,128]{2,1,0:T(8,128)(2,1)} %fusion.72), calls=%async_computation.4 | async-start | bytes 786432 | tf_op jit(solution)/shard_map/all_to_all | solution.py:1057
  224.9 27.6 %collective-permute-start.29 = (bf16[8,192,256]{2,1,0:T(8,128)(2,1)}, bf16[8,192,256]{2,1,0:T(8,128)(2,1)S(1)}, u32[]{:S(2)}, u32[]{:S(2)}) collective-permute-start(bf16[8,192,256]{2,1,0:T(8,128)(2,1)} %fusion.69), channel_id=1, source_target_pairs={{0,2},{1,3},{2,0},{3,1},{4,6},{5,7},{6,4},{7,5},{8,10},{9,11},{10,... | collective-permute-start | bytes 2359304 | tf_op jit(solution)/shard_map/ppermute | solution.py:43
  240.7 11.8 %collective-permute-start.30 = (bf16[4,192,256]{2,1,0:T(8,128)(2,1)S(1)}, bf16[4,192,256]{2,1,0:T(8,128)(2,1)S(1)}, u32[]{:S(2)}, u32[]{:S(2)}) collective-permute-start(bf16[4,192,256]{2,1,0:T(8,128)(2,1)S(1)} %fusion.47.refs_0_), channel_id=1, source_target_pairs={{0,2},{1,3},{2,0},{3,1},{4,6},{5,7},{6,4},{7,5},{8,10},{9,11},{10,... | collective-permute-start | bytes 1179656 | tf_op jit(solution)/shard_map/ppermute | solution.py:43
  255.0 31.6 %all-to-all-start.5 = ((bf16[8,192,256]{2,1,0:T(8,128)(2,1)}), bf16[8,192,256]{2,1,0:T(8,128)(2,1)S(1)}, u32[]{:S(2)}, u32[]{:S(2)}) async-start(bf16[8,192,256]{2,1,0:T(8,128)(2,1)} %fusion.19), calls=%async_computation.5 | async-start | bytes 1572864 | tf_op jit(solution)/shard_map/all_to_all | solution.py:1057
  297.3 5.0 %collective-permute-start.33 = (bf16[2,768,256]{2,1,0:T(8,128)(2,1)}, bf16[2,768,256]{2,1,0:T(8,128)(2,1)S(1)}, u32[]{:S(2)}, u32[]{:S(2)}) collective-permute-start(bf16[2,768,256]{2,1,0:T(8,128)(2,1)} %get-tuple-element.190), channel_id=1, source_target_pairs={{0,1},{1,0},{2,3},{3,2},{4,5},{5,4},{6,7},{7,6},{8,9},{9,8},{10,11... | collective-permute-start | bytes 2359304 | tf_op jit(solution)/shard_map/ppermute | solution.py:43
  297.7 5.5 %collective-permute-start.32 = (bf16[2,768,256]{2,1,0:T(8,128)(2,1)}, bf16[2,768,256]{2,1,0:T(8,128)(2,1)}, u32[]{:S(2)}, u32[]{:S(2)}) collective-permute-start(bf16[2,768,256]{2,1,0:T(8,128)(2,1)} %get-tuple-element.188), channel_id=1, source_target_pairs={{0,1},{1,0},{2,3},{3,2},{4,5},{5,4},{6,7},{7,6},{8,9},{9,8},{10,11... | collective-permute-start | bytes 2359304 | tf_op jit(solution)/shard_map/ppermute | solution.py:43
  298.5 18.4 %collective-permute-start.35 = (bf16[4,96,768]{2,1,0:T(8,128)(2,1)}, bf16[4,96,768]{2,1,0:T(8,128)(2,1)S(1)}, u32[]{:S(2)}, u32[]{:S(2)}) collective-permute-start(bf16[4,96,768]{2,1,0:T(8,128)(2,1)} %get-tuple-element.196), channel_id=1, source_target_pairs={{0,4},{4,0},{1,5},{5,1},{2,6},{6,2},{3,7},{7,3},{8,12},{12,8},{9,1... | collective-permute-start | bytes 1769480 | tf_op jit(solution)/shard_map/ppermute | solution.py:43
  305.2 6.2 %collective-permute-start.36 = (f32[8064]{0:T(1024)S(1)}, f32[8064]{0:T(1024)S(1)}, u32[]{:S(2)}, u32[]{:S(2)}) collective-permute-start(f32[8064]{0:T(1024)S(1)} %pad_maximum_fusion.9), channel_id=1, source_target_pairs={{0,8},{8,0},{16,24},{24,16},{1,9},{9,1},{17,25},{25,17},{2,10},{10... | collective-permute-start | bytes 96776 | tf_op jit(solution)/shard_map/ppermute | solution.py:43
  306.1 10.8 %collective-permute-start.34 = (bf16[768,256]{1,0:T(8,128)(2,1)}, bf16[768,256]{1,0:T(8,128)(2,1)S(1)}, u32[]{:S(2)}, u32[]{:S(2)}) collective-permute-start(bf16[768,256]{1,0:T(8,128)(2,1)} %fusion.79), channel_id=1, source_target_pairs={{0,2},{1,3},{2,0},{3,1},{4,6},{5,7},{6,4},{7,5},{8,10},{9,11},{10,... | collective-permute-start | bytes 1179656 | tf_op jit(solution)/shard_map/ppermute | solution.py:43
  311.5 4.9 %collective-permute-start.37 = (f32[8064]{0:T(1024)S(1)}, f32[8064]{0:T(1024)S(1)}, u32[]{:S(2)}, u32[]{:S(2)}) collective-permute-start(f32[8064]{0:T(1024)S(1)} %fusion.98), channel_id=1, source_target_pairs={{0,16},{8,24},{16,0},{24,8},{1,17},{9,25},{17,1},{25,9},{2,18},{10... | collective-permute-start | bytes 96776 | tf_op jit(solution)/shard_map/ppermute | solution.py:43
  317.6 31.2 %all-to-all-start.6 = ((bf16[4,192,256]{2,1,0:T(8,128)(2,1)}), bf16[4,192,256]{2,1,0:T(8,128)(2,1)S(1)}, u32[]{:S(2)}, u32[]{:S(2)}) async-start(bf16[4,192,256]{2,1,0:T(8,128)(2,1)} %bitcast.271), calls=%async_computation.6 | async-start | bytes 786432 | tf_op jit(solution)/shard_map/all_to_all | solution.py:1285
  321.1 10.1 %collective-permute-start.43 = (f32[8064]{0:T(1024)S(1)}, f32[8064]{0:T(1024)S(1)}, u32[]{:S(2)}, u32[]{:S(2)}) collective-permute-start(f32[8064]{0:T(1024)S(1)} %add.210), channel_id=1, source_target_pairs={{0,4},{4,0},{1,5},{5,1},{2,6},{6,2},{3,7},{7,3},{8,12},{12,8},{9,1... | collective-permute-start | bytes 96776 | tf_op jit(solution)/shard_map/ppermute | solution.py:43
  323.7 25.1 %collective-permute-start.39 = (bf16[768,256]{1,0:T(8,128)(2,1)}, bf16[768,256]{1,0:T(8,128)(2,1)S(1)}, u32[]{:S(2)}, u32[]{:S(2)}) collective-permute-start(bf16[768,256]{1,0:T(8,128)(2,1)} %fusion.71), channel_id=1, source_target_pairs={{0,4},{4,0},{1,5},{5,1},{2,6},{6,2},{3,7},{7,3},{8,12},{12,8},{9,1... | collective-permute-start | bytes 1179656 | tf_op jit(solution)/shard_map/ppermute | solution.py:43
  325.2 23.7 %collective-permute-start.38 = (bf16[768,256]{1,0:T(8,128)(2,1)}, bf16[768,256]{1,0:T(8,128)(2,1)}, u32[]{:S(2)}, u32[]{:S(2)}) collective-permute-start(bf16[768,256]{1,0:T(8,128)(2,1)} %fusion.80), channel_id=1, source_target_pairs={{0,2},{1,3},{2,0},{3,1},{4,6},{5,7},{6,4},{7,5},{8,10},{9,11},{10,... | collective-permute-start | bytes 1179656 | tf_op jit(solution)/shard_map/ppermute | solution.py:43
  327.3 14.6 %collective-permute-start.40 = (bf16[96,768]{1,0:T(8,128)(2,1)S(1)}, bf16[96,768]{1,0:T(8,128)(2,1)S(1)}, u32[]{:S(2)}, u32[]{:S(2)}) collective-permute-start(bf16[96,768]{1,0:T(8,128)(2,1)S(1)} %get-tuple-element.274), channel_id=1, source_target_pairs={{0,8},{8,0},{16,24},{24,16},{1,9},{9,1},{17,25},{25,17},{2,10},{10... | collective-permute-start | bytes 442376 | tf_op jit(solution)/shard_map/ppermute | solution.py:43
  328.6 13.3 %collective-permute-start.42 = (bf16[96,768]{1,0:T(8,128)(2,1)S(1)}, bf16[96,768]{1,0:T(8,128)(2,1)S(1)}, u32[]{:S(2)}, u32[]{:S(2)}) collective-permute-start(bf16[96,768]{1,0:T(8,128)(2,1)S(1)} %get-tuple-element.275), channel_id=1, source_target_pairs={{0,24},{8,16},{16,8},{24,0},{1,25},{9,17},{17,9},{25,1},{2,26},{10... | collective-permute-start | bytes 442376 | tf_op jit(solution)/shard_map/ppermute | solution.py:43
  332.5 5.1 %collective-permute-start.45 = (f32[8064]{0:T(1024)S(1)}, f32[8064]{0:T(1024)S(1)}, u32[]{:S(2)}, u32[]{:S(2)}) collective-permute-start(f32[8064]{0:T(1024)S(1)} %add.221), channel_id=1, source_target_pairs={{0,2},{1,3},{2,0},{3,1},{4,6},{5,7},{6,4},{7,5},{8,10},{9,11},{10,... | collective-permute-start | bytes 96776 | tf_op jit(solution)/shard_map/ppermute | solution.py:43
  337.6 9.6 %collective-permute-start.41 = (bf16[96,768]{1,0:T(8,128)(2,1)S(1)}, bf16[96,768]{1,0:T(8,128)(2,1)S(1)}, u32[]{:S(2)}, u32[]{:S(2)}) collective-permute-start(bf16[96,768]{1,0:T(8,128)(2,1)S(1)} %get-tuple-element.276), channel_id=1, source_target_pairs={{0,16},{8,24},{16,0},{24,8},{1,17},{9,25},{17,1},{25,9},{2,18},{10... | collective-permute-start | bytes 442376 | tf_op jit(solution)/shard_map/ppermute | solution.py:43
  (59 other events, 434.3 us)

commit v2 on v1

--- a/solution.py
+++ b/solution.py
@@ -672,9 +672,9 @@
     width = rows.shape[1]
     values = rows.T
     gain = gain_ref[...]
-    grad = sum_refs[0][...].astype(F32)
+    grad = sum_refs[0][0].astype(F32)
     for ref in sum_refs[1:]:
-        grad += ref[...].astype(F32)
+        grad += ref[0].astype(F32)
     root = lax.rsqrt(jnp.sum(values * values, axis=0, keepdims=True) * (1.0 / width) + EPSILON)
     scaled = grad * gain
     centre = jnp.sum(scaled * values, axis=0, keepdims=True) * (1.0 / width)
@@ -686,11 +686,12 @@
 def finish(block_input, gain, branch, result, sums):
     shape = jax.ShapeDtypeStruct(block_input.shape, F32)
     operands = (block_input, gain, branch, result, *sums)
+    first = pl.BlockSpec((1,) + sums[0].shape[1:], functools.partial(origin, 3))
     return pl.pallas_call(
         finish_kernel,
         grid=(1,),
         out_shape=(shape, shape),
-        in_specs=whole_specs(operands),
+        in_specs=whole_specs(operands[:4]) + [first] * len(sums),
         out_specs=tuple(whole_specs((shape, shape))),
         compiler_params=pltpu.CompilerParams(vmem_limit_bytes=VMEM_BYTES),
         name="finish",
@@ -1112,8 +1113,6 @@
     own = jnp.stack([grid_place, tensor_place, seq_place, own_first]).astype(jnp.int32)
     onehot = (target == places).astype(BF16)
     grad_pair = swap(jnp.stack([grad_mine, grad_other]), "tensor", 2)
-    grad_here = tiled([grad_mine, grad_other, grad_pair[0], grad_pair[1]])
-    grad_buffer = einsum("nkdq,enqs->ekds", grad_here, onehot).astype(BF16)
     (
         meta,
         queries,
@@ -1135,6 +1134,9 @@
         share,
         heads,
     )
+    queries, grad_pair = lax.optimization_barrier((queries, grad_pair))
+    grad_here = tiled([grad_mine, grad_other, grad_pair[0], grad_pair[1]])
+    grad_buffer = einsum("nkdq,enqs->ekds", grad_here, onehot).astype(BF16)
     queries, grad_buffer = lax.optimization_barrier((queries, grad_buffer))
     grad_arrived = joined(exchange(grad_buffer))
     exact, attended, logs, attn_even, attn_odd = attend(
@@ -1206,9 +1208,9 @@
     state_grad = state_grad.astype(BF16)
 
     branch = [state_grad, swap(state_grad, "tensor", 1), swap(state_grad, "tensor", 2)]
-    result_far, branch[2] = lax.optimization_barrier((result_far, branch[2]))
+    result_total = chip_step(result_near, result_got, result_far).astype(BF16)
+    result_total, branch[2] = lax.optimization_barrier((result_total, branch[2]))
     branch.append(swap(branch[2], "tensor", 1))
-    result_total = chip_step(result_near, result_got, result_far).astype(BF16)
     result_back = exchange(parted(result_total))
     dq, dkv, bias_rows = attend_back(
         meta, queries, keys_values, near, out_t_blocks, exact, logs, branch, bucket_count
@@ -1235,7 +1237,8 @@
             True, own, dq, dkv, normed_tiles, in_flat, attended, branch, grid_count
         )
         far_near, far_got, far_send = core_step(far_even, far_odd)
-        own_near, own_got, own_send = core_step(own_even, own_odd)
+        own_got = swap(own_odd, "tensor", 1)
+        own_send = (own_even[1].astype(F32) + own_got[1].astype(F32)).astype(BF16)
         weight_sent = swap(weight_odd, "seq", 1)
         far_send, own_send, gain_part, result_back = lax.optimization_barrier(
             (far_send, own_send, gain_part, result_back)
@@ -1243,13 +1246,13 @@
         far_sent = swap(far_send, "tensor", 2)
         small = sum_all(joined_small(), ("dp",))
         result_share = result_rows_of()
-        own_send, far_sent = lax.optimization_barrier((own_send, far_sent))
+        own_send, result_share = lax.optimization_barrier((own_send, result_share))
         own_sent = swap(own_send, "tensor", 2)
         far_sent, weight_sent, small, result_share, branch = lax.optimization_barrier(
             (far_sent, weight_sent, small, result_share, branch)
         )
         far_sum = chip_step(far_near, far_got, far_sent).astype(BF16)
-        sums = [own_near, own_got, own_sent, swap(far_sum, "seq", 1)]
+        sums = [own_even, own_got, own_sent[None], swap(far_sum, "seq", 1)[None]]
         weight_half = weight_even.astype(F32) + weight_sent.astype(F32)
         weight_grad = weight_half[0]
         for k in range(1, grid_count // 2):
@@ -1264,7 +1267,7 @@
             lax.dynamic_index_in_dim(row_part, tensor_place ^ k, 1, keepdims=False)
             for k in range(tensor_count)
         ]
-        sums = [sum_tensor(jnp.stack(blocks[0::2]), jnp.stack(blocks[1::2]))]
+        sums = [sum_tensor(jnp.stack(blocks[0::2]), jnp.stack(blocks[1::2]))[None]]
         small = sum_all(joined_small(), ("dp",))
         result_share = result_rows_of()
         weight_grad = lax.psum_scatter(

time: 355 us -> 351 us (0.989)
  waiting for transfers between devices: 77.4 us -> 67.6 us
    ppermute x46, waiting for transfers between devices: 66.6 us -> 56.2 us  [swap(): return lax.ppermute(values, axis, [(i, i ^ bit) for i in range(count)])]
    unnamed x117 -> x109, local copies, waits for them, and re-layouts: 11.5 us -> 13.9 us
    convert_element_type x6 -> x5, other arithmetic: 7.73 us -> 6.73 us  [core_step(): to_send = (kept[1].astype(F32) + got[1].astype(F32)).astype(BF16)]
  transfers between devices with their start and end apart: 52 -> 52, of which waited for: 19 -> 20; matrix products, arithmetic and copies ran while one was open for 17% -> 17% of each run, Pallas kernels for 24% -> 26%
where the time goes in v2:
time: 351 us; the launch traced here: 347 us
  Pallas kernels  106 us (30%)
  starting transfers between devices  79.8 us (23%)
  waiting for transfers between devices  67.6 us (19%)
  other arithmetic  34.9 us (10%)
  local copies, waits for them, and re-layouts  23.9 us (7%)
  matrix products  16.9 us (5%)
  blocking collectives  16.4 us (5%)
    ppermute x46, waiting for transfers between devices, swap(): return lax.ppermute(values, axis, [(i, i ^ bit) for i in range(count)])  56.2 us
    ppermute x46, starting transfers between devices, swap(): return lax.ppermute(values, axis, [(i, i ^ bit) for i in range(count)])  38.7 us
    all_to_all x5, starting transfers between devices, exchange(): lax.all_to_all(values, ('dp', 'seq'), split_axis=0, concat_axis=0, tiled=...  37.6 us
    pallas_call x2, Pallas kernels, run_expert(): pl.pallas_call(functools.partial(expert_kernel, parts), grid=(steps // ch...  26.9 us
    pallas_call x1, Pallas kernels, attend_back(): pl.pallas_call(attend_back_kernel, grid=(1,), out_shape=shapes, in_specs=...  22 us
    dot_general x6, matrix products, einsum(): return jnp.einsum(formula, *operands, preferred_element_type=F32)  16.9 us
    all_to_all x1, blocking collectives, exchange(): lax.all_to_all(values, ('dp', 'seq'), split_axis=0, concat_axis=0, tiled=...  16.4 us
    pallas_call x1, Pallas kernels, attend(): pl.pallas_call(attend_kernel, grid=(1,), out_shape=shapes, in_specs=[pl.B...  15.2 us
  transfers between devices with their start and end apart: 52, of which 20 were waited for; matrix products, arithmetic and copies ran while one was open for 17% of the time, Pallas kernels for 26%

profile of v2, /device:TPU:0, one launch (start us, length us, event | category | flops | bytes accessed | tf_op | source)
XLA Modules:
  0.0 347.1 jit_solution(2290152463927172121)
XLA Ops:
  3.2 5.0 %collective-permute-start.4 = (bf16[96,768]{1,0:T(8,128)(2,1)}, bf16[96,768]{1,0:T(8,128)(2,1)S(1)}, u32[]{:S(2)}, u32[]{:S(2)}) collective-permute-start(bf16[96,768]{1,0:T(8,128)(2,1)} %pad_maximum_fusion.7.refs_8_), channel_id=1, source_target_pairs={{0,24},{8,16},{16,8},{24,0},{1,25},{9,17},{17,9},{25,1},{2,26},{10... | collective-permute-start | bytes 442376 | tf_op jit(solution)/shard_map/ppermute | solution.py:43
  16.0 2.5 copy.116
  18.5 2.6 collective-permute-done.3.refs_12_
  24.7 2.3 reduce-window.6
  32.3 3.4 collective-permute-done.6
  35.7 5.8 %collective-permute-done.7 = bf16[3,96,768]{2,1,0:T(8,128)(2,1)} collective-permute-done((bf16[3,96,768]{2,1,0:T(8,128)(2,1)}, bf16[3,96,768]{2,1,0:T(8,128)(2,1)}, u32[]{:S(2)}, u32[]{:S(2)}) %collective-permute-start.7) | collective-permute-done | bytes 442400 | tf_op jit(solution)/shard_map/ppermute | solution.py:43
  46.7 1.8 slice_bitcast_fusion.4
  49.3 8.9 %project.1 = (s32[15]{0:T(128)}, bf16[4,192,256]{2,1,0:T(8,128)(2,1)}, bf16[8,384,256]{2,1,0:T(8,128)(2,1)}, bf16[8,768,256]{2,1,0:T(8,128)(2,1)}, bf16[4,192,25...) custom-call(s32[4]{0:T(128)} %pad_add_fusion.own_ref, ...), custom_call_target="tpu_custom_call" | custom-call | flops 1811939328 | bytes 12582912 | tf_op jit(solution)/shard_map/project/pallas_call | solution.py:559
  58.8 3.2 fusion.20
  62.1 7.3 %all-to-all-start = ((bf16[8,2,192,256]{3,2,1,0:T(8,128)(2,1)}), bf16[8,2,192,256]{3,2,1,0:T(8,128)(2,1)S(1)}, u32[]{:S(2)}, u32[]{:S(2)}) async-start(bf16[8,2,192,256]{3,2,1,0:T(8,128)(2,1)} %fusion.20), calls=%async_computation | async-start | bytes 3145728 | tf_op jit(solution)/shard_map/all_to_all | solution.py:1058
  69.4 15.2 %attend.1 = (f32[4,192,256]{2,1,0:T(8,128)}, bf16[4,192,256]{2,1,0:T(8,128)(2,1)}, f32[4,3,1,256]{3,2,1,0:T(1,128)}, bf16[2,4,192,256]{3,2,1,0:T(8,128)(2,1)}, bf16[2,4,192,256]{3,2,1,0:T(8,128)(2,1)}) custom-call(s32[15]{0:T(128)} %get-tuple-element.127.meta_ref, bf16[4,192,256]{2,1,0:T(8,128)(2,1)} %get-tuple-element.134.q_ref, ...), custom_call_target="tpu_custom_call" | custom-call | flops 1610612736 | bytes 16777216 | tf_op jit(solution)/shard_map/attend/pallas_call | solution.py:279
  84.6 2.5 collective-permute-done.14
  88.8 2.3 broadcast_compare_fusion
  91.2 8.5 %collective-permute-done.15 = bf16[4,192,256]{2,1,0:T(8,128)(2,1)S(1)} collective-permute-done((bf16[4,192,256]{2,1,0:T(8,128)(2,1)S(1)}, bf16[4,192,256]{2,1,0:T(8,128)(2,1)S(1)}, u32[]{:S(2)}, u32[]{:S(2)}) %collective-permute-start.15) | collective-permute-done | bytes 393248 | tf_op jit(solution)/shard_map/ppermute | solution.py:43
  101.4 5.3 %all-to-all-done.refs_4_.refs_8_ = bf16[8,2,192,256]{3,2,1,0:T(8,128)(2,1)S(1)} async-done(((bf16[8,2,192,256]{3,2,1,0:T(8,128)(2,1)}), bf16[8,2,192,256]{3,2,1,0:T(8,128)(2,1)S(1)}, u32[]{:S(2)}, u32[]{:S(2)}) %all-to-all-start) | async-done | bytes 1572896 | tf_op jit(solution)/shard_map/all_to_all | solution.py:1058
  106.7 3.4 fusion.62
  110.9 16.4 %all_to_all.35.refs_0_ = bf16[8,192,128]{2,1,0:T(8,128)(2,1)} all-to-all(bf16[8,192,128]{2,1,0:T(8,128)(2,1)S(1)} %fusion.59), channel_id=1, replica_groups=mesh['dp'=4,'seq'=2,'tensor'=4] {'dp','seq'}, dimensions={0} | all-to-all | bytes 786432 | tf_op jit(solution)/shard_map/all_to_all | solution.py:1058
  127.6 4.1 %all-to-all-start.2 = ((bf16[8,192,128]{2,1,0:T(8,128)(2,1)}), bf16[8,192,128]{2,1,0:T(8,128)(2,1)}, u32[]{:S(2)}, u32[]{:S(2)}) async-start(bf16[8,192,128]{2,1,0:T(8,128)(2,1)} %fusion.62), calls=%async_computation.2 | async-start | bytes 786432 | tf_op jit(solution)/shard_map/all_to_all | solution.py:1058
  131.8 6.2 %collective-permute-done.18.refs_2_ = bf16[8,192,128]{2,1,0:T(8,128)(2,1)} collective-permute-done((bf16[8,192,128]{2,1,0:T(8,128)(2,1)}, bf16[8,192,128]{2,1,0:T(8,128)(2,1)}, u32[]{:S(2)}, u32[]{:S(2)}) %collective-permute-start.18) | collective-permute-done | bytes 393248 | tf_op jit(solution)/shard_map/ppermute | solution.py:43
  140.4 2.5 all-to-all-done.2.refs_0_
  144.7 13.5 %expert.2 = (bf16[2,8,192,128]{3,2,1,0:T(8,128)(2,1)}, bf16[2,8,192,128]{3,2,1,0:T(8,128)(2,1)}, bf16[4,768,256]{2,1,0:T(8,128)(2,1)}, bf16[4,768,256]{2,1,0:T(8...) custom-call(s32[4]{0:T(128)} %pad_add_fusion.own_ref, ...), custom_call_target="tpu_custom_call" | custom-call | flops 9663676416 | bytes 12582912 | tf_op jit(solution)/shard_map/expert/pallas_call | solution.py:861
  158.8 1.9 collective-permute-done.23
  163.7 13.5 %expert.3 = (bf16[2,8,192,128]{3,2,1,0:T(8,128)(2,1)}, bf16[2,8,192,128]{3,2,1,0:T(8,128)(2,1)}, bf16[4,768,256]{2,1,0:T(8,128)(2,1)}, bf16[4,768,256]{2,1,0:T(8...) custom-call(s32[4]{0:T(128)} %pad_add_fusion.own_ref, ...), custom_call_target="tpu_custom_call" | custom-call | flops 9663676416 | bytes 12582912 | tf_op jit(solution)/shard_map/expert/pallas_call | solution.py:861
  178.2 3.6 %all-to-all-start.3 = ((bf16[8,192,128]{2,1,0:T(8,128)(2,1)}), bf16[8,192,128]{2,1,0:T(8,128)(2,1)S(1)}, u32[]{:S(2)}, u32[]{:S(2)}) async-start(bf16[8,192,128]{2,1,0:T(8,128)(2,1)} %fusion.73), calls=%async_computation.3 | async-start | bytes 786432 | tf_op jit(solution)/shard_map/all_to_all | solution.py:1058
  183.7 6.8 %result.1 = (bf16[2,8,192,256]{3,2,1,0:T(8,128)(2,1)}, bf16[2,8,192,256]{3,2,1,0:T(8,128)(2,1)}) custom-call(s32[4]{0:T(128)} %pad_add_fusion.own_ref, bf16[4,768,256]{2,1,0:T(8,128)(2,1)} %get-tuple-element.162.refs_0_.refs_1_, f32[4,1,256]{2,1,0:T(1,128)} %get-tuple-element.163.refs_1_.refs_3_, bf16[4,768,256]{2,1,0:T(8,128)(2,1)} %get-tuple-element.164.refs_2_.refs_5_, ...), custom_call_target="tpu_custom_call" | custom-call | flops 7247757312 | bytes 9437184 | tf_op jit(solution)/shard_map/result/pallas_call | solution.py:903
  190.5 3.6 %all-to-all-done.3 = bf16[8,192,128]{2,1,0:T(8,128)(2,1)S(1)} async-done(((bf16[8,192,128]{2,1,0:T(8,128)(2,1)}), bf16[8,192,128]{2,1,0:T(8,128)(2,1)S(1)}, u32[]{:S(2)}, u32[]{:S(2)}) %all-to-all-start.3) | async-done | bytes 393248 | tf_op jit(solution)/shard_map/all_to_all | solution.py:1058
  196.3 2.1 fusion.72
  198.4 16.8 %all-to-all-start.4 = ((bf16[8,192,128]{2,1,0:T(8,128)(2,1)}), bf16[8,192,128]{2,1,0:T(8,128)(2,1)S(1)}, u32[]{:S(2)}, u32[]{:S(2)}) async-start(bf16[8,192,128]{2,1,0:T(8,128)(2,1)} %fusion.72), calls=%async_computation.4 | async-start | bytes 786432 | tf_op jit(solution)/shard_map/all_to_all | solution.py:1058
  215.2 3.2 fusion.41
  218.4 2.2 fusion.69
  222.3 11.8 %grads.1 = (f32[768,768]{1,0:T(8,128)}, f32[768,768]{1,0:T(8,128)}, f32[768,1]{1,0:T(8,128)}) custom-call(s32[4]{0:T(128)} %pad_add_fusion.own_ref, bf16[4,768,256]{2,1,0:T(8,128)(2,1)} %get-tuple-element.174.refs_0_, bf16[4,768,256]{2,1,0:T(8,128)(2,1)} %get-tuple-element.162.refs_0_.refs_1_, bf16[4,768,256]{2,1,0:T(8,128)(2,1)} %get-tuple-element.175.refs_2_, ...), custom_call_target="tpu_custom_call" | custom-call | flops 9663676416 | bytes 12582912 | tf_op jit(solution)/shard_map/grads/pallas_call | solution.py:932
  234.2 2.5 fusion.47.refs_0_
  237.0 3.9 %collective-permute-done.29 = bf16[8,192,256]{2,1,0:T(8,128)(2,1)S(1)} collective-permute-done((bf16[8,192,256]{2,1,0:T(8,128)(2,1)}, bf16[8,192,256]{2,1,0:T(8,128)(2,1)S(1)}, u32[]{:S(2)}, u32[]{:S(2)}) %collective-permute-start.29) | collective-permute-done | bytes 786464 | tf_op jit(solution)/shard_map/ppermute | solution.py:43
  240.9 2.3 fusion.19
  243.3 4.9 %collective-permute-done.30.refs_2_ = bf16[4,192,256]{2,1,0:T(8,128)(2,1)S(1)} collective-permute-done((bf16[4,192,256]{2,1,0:T(8,128)(2,1)S(1)}, bf16[4,192,256]{2,1,0:T(8,128)(2,1)S(1)}, u32[]{:S(2)}, u32[]{:S(2)}) %collective-permute-start.30) | collective-permute-done | bytes 393248 | tf_op jit(solution)/shard_map/ppermute | solution.py:43
  248.2 5.8 %all-to-all-start.5 = ((bf16[8,192,256]{2,1,0:T(8,128)(2,1)}), bf16[8,192,256]{2,1,0:T(8,128)(2,1)S(1)}, u32[]{:S(2)}, u32[]{:S(2)}) async-start(bf16[8,192,256]{2,1,0:T(8,128)(2,1)} %fusion.19), calls=%async_computation.5 | async-start | bytes 1572864 | tf_op jit(solution)/shard_map/all_to_all | solution.py:1058
  257.2 22.0 %attend_back.1 = (bf16[4,192,256]{2,1,0:T(8,128)(2,1)}, bf16[8,384,256]{2,1,0:T(8,128)(2,1)}, f32[3,32,128]{2,1,0:T(8,128)}) custom-call(s32[15]{0:T(128)} %get-tuple-element.127.meta_ref, bf16[4,192,256]{2,1,0:T(8,128)(2,1)} %get-tuple-element.134.q_ref, bf16[8,384,256]{2,1,0:T(8,128)(2,1)} %get-tuple-element.135.kv_ref, ...), custom_call_target="tpu_custom_call" | custom-call | flops 4026531840 | bytes 16777216 | tf_op jit(solution)/shard_map/attend_back/pallas_call | solution.py:445
  279.2 10.5 %project_back.1 = (bf16[2,768,256]{2,1,0:T(8,128)(2,1)}, bf16[2,768,256]{2,1,0:T(8,128)(2,1)}, bf16[2,768,256]{2,1,0:T(8,128)(2,1)}, bf16[2,768,256]{2,1,0:T(8,1...) custom-call(s32[4]{0:T(128)} %pad_add_fusion.own_ref, ...), custom_call_target="tpu_custom_call" | custom-call | flops 3623878656 | bytes 12582912 | tf_op jit(solution)/shard_map/project_back/pallas_call | solution.py:651
  292.4 1.9 fusion.79
  296.5 3.4 collective-permute-start.35
  303.3 3.9 %fusion.65 = bf16[192,4,256]{2,0,1:T(8,128)(2,1)} fusion(s32[8,256]{1,0:T(8,128)S(1)} %multiply_add_fusion, s32[4,256]{1,0:T(4,128)S(1)} %bitcast.278, bf16[8,192,256]{2,1,0:T(8,128)(2,1)S(1)} %all-to-all-done.5, bf16[4,192,256]{2,1,0:T(8,128)(2,1)} %copy-done.29, bf16[2,4,192,256]{3,2,1,0:T(8,128)(2,1)} %copy-done.22, ...), kind=kOutput, calls=%fused_computation.39 | convolution fusion | flops 808779776 | bytes 2371584 | tf_op jit(solution)/shard_map/eds,enqs->ndq/dot_general | solution.py:38
  308.9 4.5 %collective-permute-done.35 = bf16[4,96,768]{2,1,0:T(8,128)(2,1)S(1)} collective-permute-done((bf16[4,96,768]{2,1,0:T(8,128)(2,1)}, bf16[4,96,768]{2,1,0:T(8,128)(2,1)S(1)}, u32[]{:S(2)}, u32[]{:S(2)}) %collective-permute-start.35) | collective-permute-done | bytes 589856 | tf_op jit(solution)/shard_map/ppermute | solution.py:43
  313.4 3.5 all-to-all-start.6
  318.7 2.0 fusion.71
  322.9 2.9 collective-permute-start.42
  327.1 1.9 collective-permute-start.45
  333.0 7.4 %collective-permute-done.41 = bf16[96,768]{1,0:T(8,128)(2,1)S(1)} collective-permute-done((bf16[96,768]{1,0:T(8,128)(2,1)S(1)}, bf16[96,768]{1,0:T(8,128)(2,1)S(1)}, u32[]{:S(2)}, u32[]{:S(2)}) %collective-permute-start.41) | collective-permute-done | bytes 147488 | tf_op jit(solution)/shard_map/ppermute | solution.py:43
  343.0 3.9 %finish.1 = (f32[256,768]{1,0:T(8,128)}, f32[256,768]{1,0:T(8,128)}) custom-call(f32[256,768]{1,0:T(8,128)} %input_ref.1, f32[768,1]{1,0:T(8,128)} %copy.133.refs_16_.gain_ref, bf16[768,256]{1,0:T(8,128)(2,1)} %pad_maximum_fusion.5.branch_ref, bf16[768,256]{1,0:T(8,128)(2,1)} %bitcast.262, bf16[2,768,256]{2,1,0:T(8,128)(2,1)} %get-tuple-element.193.refs_0_, ...), custom_call_target="tpu_custom_call" | custom-call | tf_op jit(solution)/shard_map/finish/pallas_call | solution.py:690
  (258 shorter events, 70.1 us)
Async XLA Ops:
  3.2 11.9 %collective-permute-start.4 = (bf16[96,768]{1,0:T(8,128)(2,1)}, bf16[96,768]{1,0:T(8,128)(2,1)S(1)}, u32[]{:S(2)}, u32[]{:S(2)}) collective-permute-start(bf16[96,768]{1,0:T(8,128)(2,1)} %pad_maximum_fusion.7.refs_8_), channel_id=1, source_target_pairs={{0,24},{8,16},{16,8},{24,0},{1,25},{9,17},{17,9},{25,1},{2,26},{10... | collective-permute-start | bytes 442376 | tf_op jit(solution)/shard_map/ppermute | solution.py:43
  8.3 12.8 %collective-permute-start.3 = (bf16[96,768]{1,0:T(8,128)(2,1)}, bf16[96,768]{1,0:T(8,128)(2,1)}, u32[]{:S(2)}, u32[]{:S(2)}) collective-permute-start(bf16[96,768]{1,0:T(8,128)(2,1)} %pad_maximum_fusion.7.refs_8_), channel_id=1, source_target_pairs={{0,16},{8,24},{16,0},{24,8},{1,17},{9,25},{17,1},{25,9},{2,18},{10... | collective-permute-start | bytes 442376 | tf_op jit(solution)/shard_map/ppermute | solution.py:43
  8.3 14.3 %collective-permute-start.2 = (bf16[96,768]{1,0:T(8,128)(2,1)}, bf16[96,768]{1,0:T(8,128)(2,1)}, u32[]{:S(2)}, u32[]{:S(2)}) collective-permute-start(bf16[96,768]{1,0:T(8,128)(2,1)} %pad_maximum_fusion.7.refs_8_), channel_id=1, source_target_pairs={{0,8},{8,0},{16,24},{24,16},{1,9},{9,1},{17,25},{25,17},{2,10},{10... | collective-permute-start | bytes 442376 | tf_op jit(solution)/shard_map/ppermute | solution.py:43
  11.7 10.9 %collective-permute-start.1 = (bf16[784,256]{1,0:T(8,128)(2,1)S(1)}, bf16[784,256]{1,0:T(8,128)(2,1)}, u32[]{:S(2)}, u32[]{:S(2)}) collective-permute-start(bf16[784,256]{1,0:T(8,128)(2,1)S(1)} %get-tuple-element.285), channel_id=1, source_target_pairs={{0,2},{1,3},{2,0},{3,1},{4,6},{5,7},{6,4},{7,5},{8,10},{9,11},{10,... | collective-permute-start | bytes 1204232 | tf_op jit(solution)/shard_map/ppermute | solution.py:43
  13.4 10.3 %collective-permute-start = (bf16[784,256]{1,0:T(8,128)(2,1)S(1)}, bf16[784,256]{1,0:T(8,128)(2,1)}, u32[]{:S(2)}, u32[]{:S(2)}) collective-permute-start(bf16[784,256]{1,0:T(8,128)(2,1)S(1)} %get-tuple-element.285), channel_id=1, source_target_pairs={{0,4},{4,0},{1,5},{5,1},{2,6},{6,2},{3,7},{7,3},{8,12},{12,8},{9,1... | collective-permute-start | bytes 1204232 | tf_op jit(solution)/shard_map/ppermute | solution.py:43
  15.2 7.5 %collective-permute-start.5 = (bf16[2,192,256]{2,1,0:T(8,128)(2,1)S(1)}, bf16[2,192,256]{2,1,0:T(8,128)(2,1)S(1)}, u32[]{:S(2)}, u32[]{:S(2)}) collective-permute-start(bf16[2,192,256]{2,1,0:T(8,128)(2,1)S(1)} %get-tuple-element.287), channel_id=1, source_target_pairs={{0,1},{1,0},{2,3},{3,2},{4,5},{5,4},{6,7},{7,6},{8,9},{9,8},{10,11... | collective-permute-start | bytes 589832 | tf_op jit(solution)/shard_map/ppermute | solution.py:43
  21.1 24.1 %collective-permute-start.12 = (bf16[96,768]{1,0:T(8,128)(2,1)}, bf16[96,768]{1,0:T(8,128)(2,1)}, u32[]{:S(2)}, u32[]{:S(2)}) collective-permute-start(bf16[96,768]{1,0:T(8,128)(2,1)} %pad_maximum_fusion.7.refs_8_), channel_id=1, source_target_pairs={{0,4},{4,0},{1,5},{5,1},{2,6},{6,2},{3,7},{7,3},{8,12},{12,8},{9,1... | collective-permute-start | bytes 442376 | tf_op jit(solution)/shard_map/ppermute | solution.py:43
  22.6 25.9 %collective-permute-start.8 = (bf16[784,256]{1,0:T(8,128)(2,1)S(1)}, bf16[784,256]{1,0:T(8,128)(2,1)}, u32[]{:S(2)}, u32[]{:S(2)}) collective-permute-start(bf16[784,256]{1,0:T(8,128)(2,1)S(1)} %get-tuple-element.285), channel_id=1, source_target_pairs={{0,1},{1,0},{2,3},{3,2},{4,5},{5,4},{6,7},{7,6},{8,9},{9,8},{10,11... | collective-permute-start | bytes 1204232 | tf_op jit(solution)/shard_map/ppermute | solution.py:43
  23.7 24.8 %collective-permute-start.10 = (bf16[784,256]{1,0:T(8,128)(2,1)}, bf16[784,256]{1,0:T(8,128)(2,1)}, u32[]{:S(2)}, u32[]{:S(2)}) collective-permute-start(bf16[784,256]{1,0:T(8,128)(2,1)} %collective-permute-done), channel_id=1, source_target_pairs={{0,1},{1,0},{2,3},{3,2},{4,5},{5,4},{6,7},{7,6},{8,9},{9,8},{10,11... | collective-permute-start | bytes 1204232 | tf_op jit(solution)/shard_map/ppermute | solution.py:43
  23.7 12.0 %collective-permute-start.6 = (bf16[784,256]{1,0:T(8,128)(2,1)}, bf16[784,256]{1,0:T(8,128)(2,1)}, u32[]{:S(2)}, u32[]{:S(2)}) collective-permute-start(bf16[784,256]{1,0:T(8,128)(2,1)} %collective-permute-done), channel_id=1, source_target_pairs={{0,2},{1,3},{2,0},{3,1},{4,6},{5,7},{6,4},{7,5},{8,10},{9,11},{10,... | collective-permute-start | bytes 1204232 | tf_op jit(solution)/shard_map/ppermute | solution.py:43
  29.3 12.2 %collective-permute-start.7 = (bf16[3,96,768]{2,1,0:T(8,128)(2,1)}, bf16[3,96,768]{2,1,0:T(8,128)(2,1)}, u32[]{:S(2)}, u32[]{:S(2)}) collective-permute-start(bf16[3,96,768]{2,1,0:T(8,128)(2,1)} %pad_maximum_fusion.3), channel_id=1, source_target_pairs={{0,4},{4,0},{1,5},{5,1},{2,6},{6,2},{3,7},{7,3},{8,12},{12,8},{9,1... | collective-permute-start | bytes 1327112 | tf_op jit(solution)/shard_map/ppermute | solution.py:43
  35.7 12.8 %collective-permute-start.9 = (bf16[784,256]{1,0:T(8,128)(2,1)}, bf16[784,256]{1,0:T(8,128)(2,1)S(1)}, u32[]{:S(2)}, u32[]{:S(2)}) collective-permute-start(bf16[784,256]{1,0:T(8,128)(2,1)} %collective-permute-done.1), channel_id=1, source_target_pairs={{0,1},{1,0},{2,3},{3,2},{4,5},{5,4},{6,7},{7,6},{8,9},{9,8},{10,11... | collective-permute-start | bytes 1204232 | tf_op jit(solution)/shard_map/ppermute | solution.py:43
  41.5 7.1 %collective-permute-start.11 = (bf16[784,256]{1,0:T(8,128)(2,1)}, bf16[784,256]{1,0:T(8,128)(2,1)}, u32[]{:S(2)}, u32[]{:S(2)}) collective-permute-start(bf16[784,256]{1,0:T(8,128)(2,1)} %collective-permute-done.6), channel_id=1, source_target_pairs={{0,1},{1,0},{2,3},{3,2},{4,5},{5,4},{6,7},{7,6},{8,9},{9,8},{10,11... | collective-permute-start | bytes 1204232 | tf_op jit(solution)/shard_map/ppermute | solution.py:43
  45.2 13.0 %collective-permute-start.13 = (bf16[2,2,192,256]{3,2,1,0:T(8,128)(2,1)S(1)}, bf16[2,2,192,256]{3,2,1,0:T(8,128)(2,1)S(1)}, u32[]{:S(2)}, u32[]{:S(2)}) collective-permute-start(bf16[2,2,192,256]{3,2,1,0:T(8,128)(2,1)S(1)} %pad_maximum_fusion.4), channel_id=1, source_target_pairs={{0,2},{1,3},{2,0},{3,1},{4,6},{5,7},{6,4},{7,5},{8,10},{9,11},{10,... | collective-permute-start | bytes 1179656 | tf_op jit(solution)/shard_map/ppermute | solution.py:43
  62.1 44.6 %all-to-all-start = ((bf16[8,2,192,256]{3,2,1,0:T(8,128)(2,1)}), bf16[8,2,192,256]{3,2,1,0:T(8,128)(2,1)S(1)}, u32[]{:S(2)}, u32[]{:S(2)}) async-start(bf16[8,2,192,256]{3,2,1,0:T(8,128)(2,1)} %fusion.20), calls=%async_computation | async-start | bytes 3145728 | tf_op jit(solution)/shard_map/all_to_all | solution.py:1058
  88.5 11.2 %collective-permute-start.15 = (bf16[4,192,256]{2,1,0:T(8,128)(2,1)S(1)}, bf16[4,192,256]{2,1,0:T(8,128)(2,1)S(1)}, u32[]{:S(2)}, u32[]{:S(2)}) collective-permute-start(bf16[4,192,256]{2,1,0:T(8,128)(2,1)S(1)} %fusion.76), channel_id=1, source_target_pairs={{0,2},{1,3},{2,0},{3,1},{4,6},{5,7},{6,4},{7,5},{8,10},{9,11},{10,... | collective-permute-start | bytes 1179656 | tf_op jit(solution)/shard_map/ppermute | solution.py:43
  106.7 37.9 %collective-permute-start.20 = (bf16[8,2,192,256]{3,2,1,0:T(8,128)(2,1)S(1)}, bf16[8,2,192,256]{3,2,1,0:T(8,128)(2,1)}, u32[]{:S(2)}, u32[]{:S(2)}) collective-permute-start(bf16[8,2,192,256]{3,2,1,0:T(8,128)(2,1)S(1)} %all-to-all-done.refs_4_.refs_8_), channel_id=1, source_target_pairs={{0,1},{1,0},{2,3},{3,2},{4,5},{5,4},{6,7},{7,6},{8,9},{9,8},{10,11... | collective-permute-start | bytes 4718600 | tf_op jit(solution)/shard_map/ppermute | solution.py:43
  127.3 10.7 %collective-permute-start.18 = (bf16[8,192,128]{2,1,0:T(8,128)(2,1)}, bf16[8,192,128]{2,1,0:T(8,128)(2,1)}, u32[]{:S(2)}, u32[]{:S(2)}) collective-permute-start(bf16[8,192,128]{2,1,0:T(8,128)(2,1)} %all_to_all.35.refs_0_), channel_id=1, source_target_pairs={{0,2},{1,3},{2,0},{3,1},{4,6},{5,7},{6,4},{7,5},{8,10},{9,11},{10,... | collective-permute-start | bytes 1179656 | tf_op jit(solution)/shard_map/ppermute | solution.py:43
  127.6 15.3 %all-to-all-start.2 = ((bf16[8,192,128]{2,1,0:T(8,128)(2,1)}), bf16[8,192,128]{2,1,0:T(8,128)(2,1)}, u32[]{:S(2)}, u32[]{:S(2)}) async-start(bf16[8,192,128]{2,1,0:T(8,128)(2,1)} %fusion.62), calls=%async_computation.2 | async-start | bytes 786432 | tf_op jit(solution)/shard_map/all_to_all | solution.py:1058
  131.7 12.9 %collective-permute-start.17 = (bf16[8,192,128]{2,1,0:T(8,128)(2,1)}, bf16[8,192,128]{2,1,0:T(8,128)(2,1)}, u32[]{:S(2)}, u32[]{:S(2)}) collective-permute-start(bf16[8,192,128]{2,1,0:T(8,128)(2,1)} %all_to_all.35.refs_0_), channel_id=1, source_target_pairs={{0,1},{1,0},{2,3},{3,2},{4,5},{5,4},{6,7},{7,6},{8,9},{9,8},{10,11... | collective-permute-start | bytes 1179656 | tf_op jit(solution)/shard_map/ppermute | solution.py:43
  138.0 6.7 %collective-permute-start.19 = (bf16[8,192,128]{2,1,0:T(8,128)(2,1)}, bf16[8,192,128]{2,1,0:T(8,128)(2,1)}, u32[]{:S(2)}, u32[]{:S(2)}) collective-permute-start(bf16[8,192,128]{2,1,0:T(8,128)(2,1)} %collective-permute-done.18.refs_2_), channel_id=1, source_target_pairs={{0,1},{1,0},{2,3},{3,2},{4,5},{5,4},{6,7},{7,6},{8,9},{9,8},{10,11... | collective-permute-start | bytes 1179656 | tf_op jit(solution)/shard_map/ppermute | solution.py:43
  142.9 15.2 %collective-permute-start.21 = (bf16[8,192,128]{2,1,0:T(8,128)(2,1)}, bf16[8,192,128]{2,1,0:T(8,128)(2,1)S(1)}, u32[]{:S(2)}, u32[]{:S(2)}) collective-permute-start(bf16[8,192,128]{2,1,0:T(8,128)(2,1)} %all-to-all-done.2.refs_0_), channel_id=1, source_target_pairs={{0,2},{1,3},{2,0},{3,1},{4,6},{5,7},{6,4},{7,5},{8,10},{9,11},{10,... | collective-permute-start | bytes 1179656 | tf_op jit(solution)/shard_map/ppermute | solution.py:43
  158.1 2.6 collective-permute-start.23
  158.2 4.0 %collective-permute-start.16 = (bf16[8,192,128]{2,1,0:T(8,128)(2,1)}, bf16[8,192,128]{2,1,0:T(8,128)(2,1)S(1)}, u32[]{:S(2)}, u32[]{:S(2)}) collective-permute-start(bf16[8,192,128]{2,1,0:T(8,128)(2,1)} %all-to-all-done.2.refs_0_), channel_id=1, source_target_pairs={{0,1},{1,0},{2,3},{3,2},{4,5},{5,4},{6,7},{7,6},{8,9},{9,8},{10,11... | collective-permute-start | bytes 1179656 | tf_op jit(solution)/shard_map/ppermute | solution.py:43
  158.7 3.5 %collective-permute-start.22 = (bf16[8,192,128]{2,1,0:T(8,128)(2,1)S(1)}, bf16[8,192,128]{2,1,0:T(8,128)(2,1)S(1)}, u32[]{:S(2)}, u32[]{:S(2)}) collective-permute-start(bf16[8,192,128]{2,1,0:T(8,128)(2,1)S(1)} %collective-permute-done.21.refs_2_), channel_id=1, source_target_pairs={{0,1},{1,0},{2,3},{3,2},{4,5},{5,4},{6,7},{7,6},{8,9},{9,8},{10,11... | collective-permute-start | bytes 1179656 | tf_op jit(solution)/shard_map/ppermute | solution.py:43
  161.8 15.4 %collective-permute-start.24 = (bf16[8,192,128]{2,1,0:T(8,128)(2,1)S(1)}, bf16[8,192,128]{2,1,0:T(8,128)(2,1)S(1)}, u32[]{:S(2)}, u32[]{:S(2)}) collective-permute-start(bf16[8,192,128]{2,1,0:T(8,128)(2,1)S(1)} %fusion.77), channel_id=1, source_target_pairs={{0,2},{1,3},{2,0},{3,1},{4,6},{5,7},{6,4},{7,5},{8,10},{9,11},{10,... | collective-permute-start | bytes 1179656 | tf_op jit(solution)/shard_map/ppermute | solution.py:43
  177.2 4.6 %collective-permute-start.25 = (bf16[2,8,192,128]{3,2,1,0:T(8,128)(2,1)}, bf16[2,8,192,128]{3,2,1,0:T(8,128)(2,1)S(1)}, u32[]{:S(2)}, u32[]{:S(2)}) collective-permute-start(bf16[2,8,192,128]{3,2,1,0:T(8,128)(2,1)} %get-tuple-element.160), channel_id=1, source_target_pairs={{0,1},{1,0},{2,3},{3,2},{4,5},{5,4},{6,7},{7,6},{8,9},{9,8},{10,11... | collective-permute-start | bytes 2359304 | tf_op jit(solution)/shard_map/ppermute | solution.py:43
  178.2 16.0 %all-to-all-start.3 = ((bf16[8,192,128]{2,1,0:T(8,128)(2,1)}), bf16[8,192,128]{2,1,0:T(8,128)(2,1)S(1)}, u32[]{:S(2)}, u32[]{:S(2)}) async-start(bf16[8,192,128]{2,1,0:T(8,128)(2,1)} %fusion.73), calls=%async_computation.3 | async-start | bytes 786432 | tf_op jit(solution)/shard_map/all_to_all | solution.py:1058
  181.9 12.2 %collective-permute-start.26 = (bf16[8,192,128]{2,1,0:T(8,128)(2,1)S(1)}, bf16[8,192,128]{2,1,0:T(8,128)(2,1)S(1)}, u32[]{:S(2)}, u32[]{:S(2)}) collective-permute-start(bf16[8,192,128]{2,1,0:T(8,128)(2,1)S(1)} %fusion.78), channel_id=1, source_target_pairs={{0,2},{1,3},{2,0},{3,1},{4,6},{5,7},{6,4},{7,5},{8,10},{9,11},{10,... | collective-permute-start | bytes 1179656 | tf_op jit(solution)/shard_map/ppermute | solution.py:43
  194.2 24.2 %collective-permute-start.27 = (bf16[2,8,192,256]{3,2,1,0:T(8,128)(2,1)}, bf16[2,8,192,256]{3,2,1,0:T(8,128)(2,1)}, u32[]{:S(2)}, u32[]{:S(2)}) collective-permute-start(bf16[2,8,192,256]{3,2,1,0:T(8,128)(2,1)} %get-tuple-element.172), channel_id=1, source_target_pairs={{0,1},{1,0},{2,3},{3,2},{4,5},{5,4},{6,7},{7,6},{8,9},{9,8},{10,11... | collective-permute-start | bytes 4718600 | tf_op jit(solution)/shard_map/ppermute | solution.py:43
  198.4 35.8 %all-to-all-start.4 = ((bf16[8,192,128]{2,1,0:T(8,128)(2,1)}), bf16[8,192,128]{2,1,0:T(8,128)(2,1)S(1)}, u32[]{:S(2)}, u32[]{:S(2)}) async-start(bf16[8,192,128]{2,1,0:T(8,128)(2,1)} %fusion.72), calls=%async_computation.4 | async-start | bytes 786432 | tf_op jit(solution)/shard_map/all_to_all | solution.py:1058
  220.6 20.3 %collective-permute-start.29 = (bf16[8,192,256]{2,1,0:T(8,128)(2,1)}, bf16[8,192,256]{2,1,0:T(8,128)(2,1)S(1)}, u32[]{:S(2)}, u32[]{:S(2)}) collective-permute-start(bf16[8,192,256]{2,1,0:T(8,128)(2,1)} %fusion.69), channel_id=1, source_target_pairs={{0,2},{1,3},{2,0},{3,1},{4,6},{5,7},{6,4},{7,5},{8,10},{9,11},{10,... | collective-permute-start | bytes 2359304 | tf_op jit(solution)/shard_map/ppermute | solution.py:43
  236.7 11.5 %collective-permute-start.30 = (bf16[4,192,256]{2,1,0:T(8,128)(2,1)S(1)}, bf16[4,192,256]{2,1,0:T(8,128)(2,1)S(1)}, u32[]{:S(2)}, u32[]{:S(2)}) collective-permute-start(bf16[4,192,256]{2,1,0:T(8,128)(2,1)S(1)} %fusion.47.refs_0_), channel_id=1, source_target_pairs={{0,2},{1,3},{2,0},{3,1},{4,6},{5,7},{6,4},{7,5},{8,10},{9,11},{10,... | collective-permute-start | bytes 1179656 | tf_op jit(solution)/shard_map/ppermute | solution.py:43
  248.2 30.9 %all-to-all-start.5 = ((bf16[8,192,256]{2,1,0:T(8,128)(2,1)}), bf16[8,192,256]{2,1,0:T(8,128)(2,1)S(1)}, u32[]{:S(2)}, u32[]{:S(2)}) async-start(bf16[8,192,256]{2,1,0:T(8,128)(2,1)} %fusion.19), calls=%async_computation.5 | async-start | bytes 1572864 | tf_op jit(solution)/shard_map/all_to_all | solution.py:1058
  289.7 2.7 collective-permute-start.32
  290.0 4.2 %collective-permute-start.33 = (bf16[2,768,256]{2,1,0:T(8,128)(2,1)}, bf16[2,768,256]{2,1,0:T(8,128)(2,1)S(1)}, u32[]{:S(2)}, u32[]{:S(2)}) collective-permute-start(bf16[2,768,256]{2,1,0:T(8,128)(2,1)} %get-tuple-element.194), channel_id=1, source_target_pairs={{0,1},{1,0},{2,3},{3,2},{4,5},{5,4},{6,7},{7,6},{8,9},{9,8},{10,11... | collective-permute-start | bytes 2359304 | tf_op jit(solution)/shard_map/ppermute | solution.py:43
  296.4 5.2 %collective-permute-start.36 = (f32[8064]{0:T(1024)S(1)}, f32[8064]{0:T(1024)S(1)}, u32[]{:S(2)}, u32[]{:S(2)}) collective-permute-start(f32[8064]{0:T(1024)S(1)} %pad_maximum_fusion.9), channel_id=1, source_target_pairs={{0,8},{8,0},{16,24},{24,16},{1,9},{9,1},{17,25},{25,17},{2,10},{10... | collective-permute-start | bytes 96776 | tf_op jit(solution)/shard_map/ppermute | solution.py:43
  296.5 17.0 %collective-permute-start.35 = (bf16[4,96,768]{2,1,0:T(8,128)(2,1)}, bf16[4,96,768]{2,1,0:T(8,128)(2,1)S(1)}, u32[]{:S(2)}, u32[]{:S(2)}) collective-permute-start(bf16[4,96,768]{2,1,0:T(8,128)(2,1)} %get-tuple-element.198), channel_id=1, source_target_pairs={{0,4},{4,0},{1,5},{5,1},{2,6},{6,2},{3,7},{7,3},{8,12},{12,8},{9,1... | collective-permute-start | bytes 1769480 | tf_op jit(solution)/shard_map/ppermute | solution.py:43
  299.9 13.6 %collective-permute-start.34 = (bf16[768,256]{1,0:T(8,128)(2,1)}, bf16[768,256]{1,0:T(8,128)(2,1)}, u32[]{:S(2)}, u32[]{:S(2)}) collective-permute-start(bf16[768,256]{1,0:T(8,128)(2,1)} %fusion.79), channel_id=1, source_target_pairs={{0,2},{1,3},{2,0},{3,1},{4,6},{5,7},{6,4},{7,5},{8,10},{9,11},{10,... | collective-permute-start | bytes 1179656 | tf_op jit(solution)/shard_map/ppermute | solution.py:43
  301.6 7.3 %collective-permute-start.37 = (f32[8064]{0:T(1024)S(1)}, f32[8064]{0:T(1024)S(1)}, u32[]{:S(2)}, u32[]{:S(2)}) collective-permute-start(f32[8064]{0:T(1024)S(1)} %fusion.98), channel_id=1, source_target_pairs={{0,16},{8,24},{16,0},{24,8},{1,17},{9,25},{17,1},{25,9},{2,18},{10... | collective-permute-start | bytes 96776 | tf_op jit(solution)/shard_map/ppermute | solution.py:43
  307.2 34.8 %collective-permute-start.38 = (bf16[768,256]{1,0:T(8,128)(2,1)}, bf16[768,256]{1,0:T(8,128)(2,1)}, u32[]{:S(2)}, u32[]{:S(2)}) collective-permute-start(bf16[768,256]{1,0:T(8,128)(2,1)} %fusion.80), channel_id=1, source_target_pairs={{0,2},{1,3},{2,0},{3,1},{4,6},{5,7},{6,4},{7,5},{8,10},{9,11},{10,... | collective-permute-start | bytes 1179656 | tf_op jit(solution)/shard_map/ppermute | solution.py:43
  313.4 28.6 %all-to-all-start.6 = ((bf16[4,192,256]{2,1,0:T(8,128)(2,1)}), bf16[4,192,256]{2,1,0:T(8,128)(2,1)S(1)}, u32[]{:S(2)}, u32[]{:S(2)}) async-start(bf16[4,192,256]{2,1,0:T(8,128)(2,1)} %bitcast.270), calls=%async_computation.6 | async-start | bytes 786432 | tf_op jit(solution)/shard_map/all_to_all | solution.py:1288
  316.9 8.9 %collective-permute-start.43 = (f32[8064]{0:T(1024)S(1)}, f32[8064]{0:T(1024)S(1)}, u32[]{:S(2)}, u32[]{:S(2)}) collective-permute-start(f32[8064]{0:T(1024)S(1)} %add.210), channel_id=1, source_target_pairs={{0,4},{4,0},{1,5},{5,1},{2,6},{6,2},{3,7},{7,3},{8,12},{12,8},{9,1... | collective-permute-start | bytes 96776 | tf_op jit(solution)/shard_map/ppermute | solution.py:43
  320.7 21.3 %collective-permute-start.39 = (bf16[768,256]{1,0:T(8,128)(2,1)}, bf16[768,256]{1,0:T(8,128)(2,1)S(1)}, u32[]{:S(2)}, u32[]{:S(2)}) collective-permute-start(bf16[768,256]{1,0:T(8,128)(2,1)} %fusion.71), channel_id=1, source_target_pairs={{0,4},{4,0},{1,5},{5,1},{2,6},{6,2},{3,7},{7,3},{8,12},{12,8},{9,1... | collective-permute-start | bytes 1179656 | tf_op jit(solution)/shard_map/ppermute | solution.py:43
  322.3 10.7 %collective-permute-start.40 = (bf16[96,768]{1,0:T(8,128)(2,1)S(1)}, bf16[96,768]{1,0:T(8,128)(2,1)S(1)}, u32[]{:S(2)}, u32[]{:S(2)}) collective-permute-start(bf16[96,768]{1,0:T(8,128)(2,1)S(1)} %get-tuple-element.278), channel_id=1, source_target_pairs={{0,8},{8,0},{16,24},{24,16},{1,9},{9,1},{17,25},{25,17},{2,10},{10... | collective-permute-start | bytes 442376 | tf_op jit(solution)/shard_map/ppermute | solution.py:43
  322.9 10.1 %collective-permute-start.42 = (bf16[96,768]{1,0:T(8,128)(2,1)S(1)}, bf16[96,768]{1,0:T(8,128)(2,1)S(1)}, u32[]{:S(2)}, u32[]{:S(2)}) collective-permute-start(bf16[96,768]{1,0:T(8,128)(2,1)S(1)} %get-tuple-element.279), channel_id=1, source_target_pairs={{0,24},{8,16},{16,8},{24,0},{1,25},{9,17},{17,9},{25,1},{2,26},{10... | collective-permute-start | bytes 442376 | tf_op jit(solution)/shard_map/ppermute | solution.py:43
  327.1 3.9 %collective-permute-start.45 = (f32[8064]{0:T(1024)S(1)}, f32[8064]{0:T(1024)S(1)}, u32[]{:S(2)}, u32[]{:S(2)}) collective-permute-start(f32[8064]{0:T(1024)S(1)} %add.221), channel_id=1, source_target_pairs={{0,2},{1,3},{2,0},{3,1},{4,6},{5,7},{6,4},{7,5},{8,10},{9,11},{10,... | collective-permute-start | bytes 96776 | tf_op jit(solution)/shard_map/ppermute | solution.py:43
  331.0 9.4 %collective-permute-start.41 = (bf16[96,768]{1,0:T(8,128)(2,1)S(1)}, bf16[96,768]{1,0:T(8,128)(2,1)S(1)}, u32[]{:S(2)}, u32[]{:S(2)}) collective-permute-start(bf16[96,768]{1,0:T(8,128)(2,1)S(1)} %get-tuple-element.280), channel_id=1, source_target_pairs={{0,16},{8,24},{16,0},{24,8},{1,17},{9,25},{17,1},{25,9},{2,18},{10... | collective-permute-start | bytes 442376 | tf_op jit(solution)/shard_map/ppermute | solution.py:43
  (55 other events, 364.6 us)
